TPU v7x, 32 devices: a whole 2x2x4 slice. The times are simulated.
32 devices in a mesh: pipe: 2 (over x), dp: 4 (over z), tensor: 4 (over y, core).
Axes of the slice: x: 2, y: 2, z: 4, core: 2. Of those that a mesh axis runs over, the one named last changes fastest.
Arguments:
- embeds: bfloat16 [2, 8, 1024, 512], P('pipe', 'dp', 'tensor'), may hold values from -6 to 6
- segments: int32 [2, 8, 1024], P(None, 'dp'), may hold values from -1 to 23, as said below
- cotangent: bfloat16 [8, 1024, 512], P('dp', 'tensor'), may hold values from -6 to 6
- norm_gains: float32 [2, 3, 512], P('pipe'), may hold values from 0.5 to 1.5
- attn_in: bfloat16 [2, 512, 3, 512], P('pipe', None, None, 'tensor'), may hold values from -0.25 to 0.25
- attn_out: bfloat16 [2, 512, 512], P('pipe', 'tensor'), may hold values from -1.75 to 1.75
- cross_proj: bfloat16 [2, 512, 2, 512], P('pipe', None, None, 'tensor'), may hold values from -1 to 1
- ffn_in: bfloat16 [2, 512, 2048], P('pipe', None, 'tensor'), may hold values from -0.25 to 0.25
- ffn_out: bfloat16 [2, 2048, 512], P('pipe', 'tensor'), may hold values from -1 to 1
Outputs:
- section_out: bfloat16 [2, 8, 1024, 512], P('pipe', 'dp', 'tensor')
- embeds_grad: bfloat16 [2, 8, 1024, 512], P('pipe', 'dp', 'tensor')
- norm_gains_grad: float32 [2, 3, 512], P('pipe', None, 'dp')
- attn_in_grad: float32 [2, 512, 3, 512], P('pipe', 'dp', None, 'tensor')
- attn_out_grad: float32 [2, 512, 512], P('pipe', 'tensor', 'dp')
- cross_proj_grad: float32 [2, 512, 2, 512], P('pipe', 'dp', None, 'tensor')
- ffn_in_grad: float32 [2, 512, 2048], P('pipe', 'dp', 'tensor')
- ffn_out_grad: float32 [2, 2048, 512], P('pipe', 'tensor', 'dp')
Inputs may be any that keep to these rules, and one draw needn't show every extreme that they name: In every packed row the 24 sentence pairs take the numbers 0 to 23 in order on both sides, segments[0] for the source and segments[1] for the target; each pair is a run of 34 to 42 consecutive slots on each side, and the slots after the last pair, at least one on each side, are padding numbered -1.
All inputs are finite; a program needn't handle non-finite values.
Results may differ from a plain program's by a relative error of at most 0.028.
Values may be sent and summed in bfloat16 or wider, within the bound.
A program may use at most 128 MiB of HBM per device.

v0:
```python
import jax
import jax.numpy as jnp
from jax import lax
from jax.sharding import PartitionSpec as P

DH = 64


norm_eps = 1e-05
masked_score = -1000000000.0


def passed_along(shard, axis, by):
    count = lax.axis_size(axis)
    pairs = [(i, i + by) for i in range(count) if 0 <= i + by < count]
    return lax.ppermute(shard, axis, pairs)


def layer_norm(values, gain_row):
    centered = values - jnp.mean(values, axis=-1, keepdims=True)
    spread = jnp.mean(centered * centered, axis=-1, keepdims=True)
    return centered * lax.rsqrt(spread + norm_eps) * gain_row


def norm_backward(values, gain_row, grad_normed):
    _, pullback = jax.vjp(layer_norm, values, gain_row)
    return pullback(grad_normed)


def split_heads(block_rows, head_size):
    return block_rows.reshape(block_rows.shape[0], block_rows.shape[1] // head_size, head_size)


def attend_forward(query_heads, key_heads, value_heads, allowed, score_scale):
    scores = (
        jnp.einsum("qhd,khd->hqk", query_heads, key_heads, preferred_element_type=jnp.float32)
        * score_scale
    )
    scores = jnp.where(allowed[None], scores, masked_score)
    row_max = jnp.max(scores, axis=-1, keepdims=True)
    exp_scores = jnp.exp(scores - row_max)
    probabilities = exp_scores / jnp.sum(exp_scores, axis=-1, keepdims=True)
    rounded_probs = probabilities.astype(jnp.bfloat16)
    mixed_heads = jnp.einsum(
        "hqk,khd->qhd", rounded_probs, value_heads, preferred_element_type=jnp.float32
    )
    mixed_rows = mixed_heads.reshape(mixed_heads.shape[0], -1).astype(jnp.bfloat16)
    return (mixed_rows, probabilities, rounded_probs)


def attend_backward(
    query_heads, key_heads, value_heads, probabilities, rounded_probs, grad_heads, score_scale
):
    d_values = jnp.einsum(
        "hqk,qhd->khd", rounded_probs, grad_heads, preferred_element_type=jnp.float32
    )
    d_probs = jnp.einsum(
        "qhd,khd->hqk", grad_heads, value_heads, preferred_element_type=jnp.float32
    )
    row_inner = jnp.sum(d_probs * probabilities, axis=-1, keepdims=True)
    d_scores = (probabilities * (d_probs - row_inner)).astype(jnp.bfloat16)
    d_query = (
        jnp.einsum("hqk,khd->qhd", d_scores, key_heads, preferred_element_type=jnp.float32)
        * score_scale
    )
    d_keys = (
        jnp.einsum("hqk,qhd->khd", d_scores, query_heads, preferred_element_type=jnp.float32)
        * score_scale
    )
    return (d_query, d_keys, d_values)


def self_forward(full_rows, in_map, allowed, head_size):
    packed = jnp.einsum(
        "ld,dcj->lcj", full_rows, in_map, preferred_element_type=jnp.float32
    ).astype(jnp.bfloat16)
    query_heads = split_heads(packed[:, 0], head_size)
    key_heads = split_heads(packed[:, 1], head_size)
    value_heads = split_heads(packed[:, 2], head_size)
    mixed_rows, probabilities, rounded_probs = attend_forward(
        query_heads, key_heads, value_heads, allowed, head_size ** (-0.5)
    )
    return ((query_heads, key_heads, value_heads), mixed_rows, probabilities, rounded_probs)


def self_backward(full_rows, in_map, out_map, allowed, grad_rows, head_size):
    heads, mixed_rows, probabilities, rounded_probs = self_forward(
        full_rows, in_map, allowed, head_size
    )
    d_out_map = jnp.einsum("lj,ld->jd", mixed_rows, grad_rows, preferred_element_type=jnp.float32)
    d_mixed = jnp.einsum(
        "ld,jd->lj", grad_rows, out_map, preferred_element_type=jnp.float32
    ).astype(jnp.bfloat16)
    d_query, d_keys, d_values = attend_backward(
        heads[0],
        heads[1],
        heads[2],
        probabilities,
        rounded_probs,
        split_heads(d_mixed, head_size),
        head_size ** (-0.5),
    )
    slot_total = full_rows.shape[0]
    d_packed = jnp.stack(
        [
            d_query.reshape(slot_total, -1),
            d_keys.reshape(slot_total, -1),
            d_values.reshape(slot_total, -1),
        ],
        axis=1,
    ).astype(jnp.bfloat16)
    d_in_map = jnp.einsum("ld,lcj->dcj", full_rows, d_packed, preferred_element_type=jnp.float32)
    d_normed = jnp.einsum("lcj,dcj->ld", d_packed, in_map, preferred_element_type=jnp.float32)
    return (d_normed, d_in_map, d_out_map)


def cross_forward(full_rows, cross_maps, received_kv, allowed, head_size):
    query_heads = split_heads(
        jnp.dot(full_rows, cross_maps[:, 0], preferred_element_type=jnp.float32).astype(
            jnp.bfloat16
        ),
        head_size,
    )
    key_heads = split_heads(received_kv[:, 0], head_size)
    value_heads = split_heads(received_kv[:, 1], head_size)
    mixed_rows, probabilities, rounded_probs = attend_forward(
        query_heads, key_heads, value_heads, allowed, head_size ** (-0.5)
    )
    return ((query_heads, key_heads, value_heads), mixed_rows, probabilities, rounded_probs)


def cross_output(full_rows, cross_maps, received_kv, allowed, head_size):
    _, mixed_rows, _, _ = cross_forward(full_rows, cross_maps, received_kv, allowed, head_size)
    return jnp.einsum("lj,dj->ld", mixed_rows, cross_maps[:, 1], preferred_element_type=jnp.float32)


def cross_backward(full_rows, cross_maps, received_kv, allowed, grad_rows, head_size):
    heads, mixed_rows, probabilities, rounded_probs = cross_forward(
        full_rows, cross_maps, received_kv, allowed, head_size
    )
    d_out_map = jnp.einsum("lj,ld->dj", mixed_rows, grad_rows, preferred_element_type=jnp.float32)
    d_mixed = jnp.dot(grad_rows, cross_maps[:, 1], preferred_element_type=jnp.float32).astype(
        jnp.bfloat16
    )
    d_query, d_keys, d_values = attend_backward(
        heads[0],
        heads[1],
        heads[2],
        probabilities,
        rounded_probs,
        split_heads(d_mixed, head_size),
        head_size ** (-0.5),
    )
    query_total = full_rows.shape[0]
    key_total = d_keys.shape[0]
    d_query_rows = d_query.reshape(query_total, -1).astype(jnp.bfloat16)
    d_query_map = jnp.einsum(
        "ld,lj->dj", full_rows, d_query_rows, preferred_element_type=jnp.float32
    )
    d_normed = jnp.einsum(
        "lj,dj->ld", d_query_rows, cross_maps[:, 0], preferred_element_type=jnp.float32
    )
    d_memory_kv = jnp.stack(
        [d_keys.reshape(key_total, -1), d_values.reshape(key_total, -1)], axis=1
    )
    d_cross = jnp.stack([d_query_map, d_out_map], axis=1)
    return (d_normed, d_cross, d_memory_kv)


def memory_forward(full_rows, cross_maps):
    return jnp.einsum(
        "ld,dcj->lcj", full_rows, cross_maps, preferred_element_type=jnp.float32
    ).astype(jnp.bfloat16)


def memory_backward(full_rows, cross_maps, grad_kv):
    d_cross = jnp.einsum("ld,lcj->dcj", full_rows, grad_kv, preferred_element_type=jnp.float32)
    d_normed = jnp.einsum("lcj,dcj->ld", grad_kv, cross_maps, preferred_element_type=jnp.float32)
    return (d_normed, d_cross)


def ffn_forward(full_rows, up_map, down_map):
    hidden = jnp.dot(full_rows, up_map, preferred_element_type=jnp.float32)
    active = jax.nn.gelu(hidden).astype(jnp.bfloat16)
    return jnp.dot(active, down_map, preferred_element_type=jnp.float32)


def ffn_backward(full_rows, up_map, down_map, grad_rows):
    hidden = jnp.dot(full_rows, up_map, preferred_element_type=jnp.float32)
    active, gelu_pull = jax.vjp(jax.nn.gelu, hidden)
    d_down = jnp.einsum(
        "lf,ld->fd", active.astype(jnp.bfloat16), grad_rows, preferred_element_type=jnp.float32
    )
    d_active = jnp.einsum("ld,fd->lf", grad_rows, down_map, preferred_element_type=jnp.float32)
    d_hidden = gelu_pull(d_active)[0].astype(jnp.bfloat16)
    d_up = jnp.einsum("ld,lf->df", full_rows, d_hidden, preferred_element_type=jnp.float32)
    d_normed = jnp.einsum("lf,df->ld", d_hidden, up_map, preferred_element_type=jnp.float32)
    return (d_normed, d_up, d_down)


def spread_rows(local_part):
    return lax.all_gather(local_part, "tensor", axis=0, tiled=True)


def collect_rows(partial_value):
    return lax.psum_scatter(
        partial_value.astype(jnp.bfloat16), "tensor", scatter_dimension=0, tiled=True
    ).astype(jnp.float32)


def spread_grads(local_part):
    return lax.all_gather(local_part, "tensor", axis=0, tiled=True)


def collect_grads(partial_value):
    return lax.psum_scatter(
        partial_value.astype(jnp.bfloat16), "tensor", scatter_dimension=0, tiled=True
    ).astype(jnp.float32)


def send_memory(made_kv):
    return passed_along(made_kv, "pipe", 1)


def return_memory(grad_kv):
    return passed_along(grad_kv, "pipe", -1)


def reduce_weights(tick_grads):
    gain_total = lax.psum(tick_grads[0], "tensor")
    return (
        lax.psum_scatter(
            gain_total.astype(jnp.bfloat16), "dp", scatter_dimension=1, tiled=True
        ).astype(jnp.float32),
        lax.psum_scatter(
            tick_grads[1].astype(jnp.bfloat16), "dp", scatter_dimension=0, tiled=True
        ).astype(jnp.float32),
        lax.psum_scatter(
            tick_grads[2].astype(jnp.bfloat16), "dp", scatter_dimension=1, tiled=True
        ).astype(jnp.float32),
        lax.psum_scatter(
            tick_grads[3].astype(jnp.bfloat16), "dp", scatter_dimension=0, tiled=True
        ).astype(jnp.float32),
        lax.psum_scatter(
            tick_grads[4].astype(jnp.bfloat16), "dp", scatter_dimension=0, tiled=True
        ).astype(jnp.float32),
        lax.psum_scatter(
            tick_grads[5].astype(jnp.bfloat16), "dp", scatter_dimension=1, tiled=True
        ).astype(jnp.float32),
    )


def body(embeds, segments, cotangent, norm_gains, attn_in, attn_out, cross_proj, ffn_in, ffn_out):
    section_index = lax.axis_index("pipe")
    is_encoder = section_index == 0
    micro_count = embeds.shape[1]
    local_rows = embeds.shape[2]
    model_width = embeds.shape[3]
    slot_count = segments.shape[2]
    head_width = attn_in.shape[3]
    hidden_width = ffn_in.shape[2]
    data_count = lax.axis_size("dp")
    head_size = DH
    norm_rows = norm_gains[0]
    in_map = attn_in[0]
    out_map = attn_out[0]
    cross_maps = cross_proj[0]
    up_map = ffn_in[0]
    down_map = ffn_out[0]
    section_inputs = embeds[0]
    places = jnp.arange(slot_count)
    causal = places[None, :] <= places[:, None]
    share_width = model_width // data_count
    zero_inputs = jnp.zeros((micro_count, local_rows, model_width), jnp.bfloat16)
    reduced_zero = (
        jnp.zeros((3, share_width), jnp.float32),
        jnp.zeros((share_width, 3, head_width), jnp.float32),
        jnp.zeros((head_width, share_width), jnp.float32),
        jnp.zeros((share_width, 2, head_width), jnp.float32),
        jnp.zeros((share_width, hidden_width), jnp.float32),
        jnp.zeros((hidden_width, share_width), jnp.float32),
    )

    def tick_slot(tick_index, offset):
        mb_raw = tick_index + offset
        is_valid = (mb_raw >= 0) & (mb_raw < micro_count)
        mb_index = jnp.clip(mb_raw, 0, micro_count - 1)
        stash_slot = jnp.where(is_valid, mb_raw, micro_count)
        return (is_valid, mb_index, stash_slot)

    zero_rows = jnp.zeros((slot_count, model_width), jnp.float32)
    zero_kv = jnp.zeros((slot_count, 2, head_width), jnp.bfloat16)
    zero_up = jnp.zeros((model_width, hidden_width), jnp.float32)
    zero_down = jnp.zeros((hidden_width, model_width), jnp.float32)
    zero_cross = jnp.zeros((model_width, 2, head_width), jnp.float32)

    def masks_of(mb_index):
        seg_source = lax.dynamic_index_in_dim(segments[0], mb_index, 0, keepdims=False)
        seg_target = lax.dynamic_index_in_dim(segments[1], mb_index, 0, keepdims=False)
        seg_self = jnp.where(is_encoder, seg_source, seg_target)
        self_allowed = (seg_self[:, None] == seg_self[None, :]) & (causal | is_encoder)
        cross_allowed = seg_target[:, None] == seg_source[None, :]
        return (self_allowed, cross_allowed)

    def forward_tick(tick_index, loop_state):
        received_kv, stash_res, stash_norm, stash_kv, section_rows = loop_state
        is_valid, mb_index, stash_slot = tick_slot(tick_index, -section_index)
        self_allowed, cross_allowed = masks_of(mb_index)
        picked = lax.dynamic_index_in_dim(section_inputs, mb_index, 0, keepdims=False).astype(
            jnp.float32
        )
        start_rows = jnp.where(is_valid, picked, 0.0)
        full_first = spread_rows(layer_norm(start_rows, norm_rows[0]).astype(jnp.bfloat16))
        _, mixed_rows, _, _ = self_forward(full_first, in_map, self_allowed, head_size)
        first_rows = start_rows + collect_rows(
            jnp.dot(mixed_rows, out_map, preferred_element_type=jnp.float32)
        )
        full_middle = spread_rows(layer_norm(first_rows, norm_rows[1]).astype(jnp.bfloat16))
        middle = lax.cond(
            is_encoder,
            lambda: ffn_forward(full_middle, up_map, down_map),
            lambda: cross_output(full_middle, cross_maps, received_kv, cross_allowed, head_size),
        )
        second_rows = first_rows + collect_rows(middle)
        normed_last = layer_norm(second_rows, norm_rows[2]).astype(jnp.bfloat16)
        full_last = spread_rows(normed_last)
        last_partial, made_kv = lax.cond(
            is_encoder,
            lambda: (zero_rows, memory_forward(full_last, cross_maps)),
            lambda: (ffn_forward(full_last, up_map, down_map), zero_kv),
        )
        final_rows = second_rows + collect_rows(last_partial)
        out_rows = jnp.where(is_encoder, normed_last, final_rows.astype(jnp.bfloat16))
        previous = lax.dynamic_index_in_dim(section_rows, mb_index, 0, keepdims=False)
        section_rows = lax.dynamic_update_index_in_dim(
            section_rows, jnp.where(is_valid, out_rows, previous), mb_index, 0
        )
        stash_res = lax.dynamic_update_index_in_dim(
            stash_res, jnp.stack([start_rows, first_rows, second_rows]), stash_slot, 0
        )
        stash_norm = lax.dynamic_update_index_in_dim(
            stash_norm, jnp.stack([full_first, full_middle, full_last]), stash_slot, 0
        )
        stash_kv = lax.dynamic_update_index_in_dim(stash_kv, received_kv, stash_slot, 0)
        received_kv = send_memory(made_kv)
        return (received_kv, stash_res, stash_norm, stash_kv, section_rows)

    forward_init = (
        zero_kv,
        jnp.zeros((micro_count + 1, 3, local_rows, model_width), jnp.float32),
        jnp.zeros((micro_count + 1, 3, slot_count, model_width), jnp.bfloat16),
        jnp.zeros((micro_count + 1, slot_count, 2, head_width), jnp.bfloat16),
        jnp.zeros((micro_count, local_rows, model_width), jnp.bfloat16),
    )
    _, stash_res, stash_norm, stash_kv, section_rows = lax.fori_loop(
        0, micro_count + 1, forward_tick, forward_init
    )

    def backward_tick(tick_index, grad_memory, input_grads):
        is_valid, mb_index, stash_slot = tick_slot(tick_index, section_index - 1)
        self_allowed, cross_allowed = masks_of(mb_index)
        residuals = lax.dynamic_index_in_dim(stash_res, stash_slot, 0, keepdims=False)
        normed_full = lax.dynamic_index_in_dim(stash_norm, stash_slot, 0, keepdims=False)
        kv_used = lax.dynamic_index_in_dim(stash_kv, stash_slot, 0, keepdims=False)
        given_grad = lax.dynamic_index_in_dim(cotangent, mb_index, 0, keepdims=False).astype(
            jnp.float32
        )
        out_grad = jnp.where(is_valid & jnp.logical_not(is_encoder), given_grad, 0.0)
        grad_full = spread_grads(out_grad.astype(jnp.bfloat16))

        def memory_branch():
            d_normed, d_cross = memory_backward(normed_full[2], cross_maps, grad_memory)
            return (d_normed, zero_up, zero_down, d_cross)

        def feed_last():
            d_normed, d_up, d_down = ffn_backward(normed_full[2], up_map, down_map, grad_full)
            return (d_normed, d_up, d_down, zero_cross)

        d_normed, d_up_last, d_down_last, d_cross_last = lax.cond(
            is_encoder, memory_branch, feed_last
        )
        d_rows, d_gain_last = norm_backward(residuals[2], norm_rows[2], collect_grads(d_normed))
        grad_second = out_grad + d_rows
        grad_full = spread_grads(grad_second.astype(jnp.bfloat16))

        def feed_middle():
            d_normed_mid, d_up, d_down = ffn_backward(normed_full[1], up_map, down_map, grad_full)
            return (d_normed_mid, d_up, d_down, zero_cross, zero_kv)

        def cross_middle():
            d_normed_mid, d_cross, d_memory_kv = cross_backward(
                normed_full[1], cross_maps, kv_used, cross_allowed, grad_full, head_size
            )
            return (d_normed_mid, zero_up, zero_down, d_cross, d_memory_kv.astype(jnp.bfloat16))

        d_normed, d_up_mid, d_down_mid, d_cross_mid, d_memory_kv = lax.cond(
            is_encoder, feed_middle, cross_middle
        )
        d_rows, d_gain_mid = norm_backward(residuals[1], norm_rows[1], collect_grads(d_normed))
        grad_first = grad_second + d_rows
        grad_full = spread_grads(grad_first.astype(jnp.bfloat16))
        d_normed, d_in_map, d_out_map = self_backward(
            normed_full[0], in_map, out_map, self_allowed, grad_full, head_size
        )
        d_rows, d_gain_first = norm_backward(residuals[0], norm_rows[0], collect_grads(d_normed))
        grad_start = grad_first + d_rows
        previous = lax.dynamic_index_in_dim(input_grads, mb_index, 0, keepdims=False)
        input_grads = lax.dynamic_update_index_in_dim(
            input_grads, jnp.where(is_valid, grad_start.astype(jnp.bfloat16), previous), mb_index, 0
        )
        grad_memory = return_memory(d_memory_kv)
        tick_grads = (
            jnp.stack([d_gain_first, d_gain_mid, d_gain_last]),
            d_in_map,
            d_out_map,
            d_cross_mid + d_cross_last,
            d_up_mid + d_up_last,
            d_down_mid + d_down_last,
        )
        return (grad_memory, tick_grads, input_grads)

    def backward_step(tick_index, loop_state):
        grad_memory, running, input_grads = loop_state
        grad_memory, tick_grads, input_grads = backward_tick(tick_index, grad_memory, input_grads)
        reduced = reduce_weights(tick_grads)
        running = jax.tree.map(jnp.add, running, reduced)
        return (grad_memory, running, input_grads)

    _, totals, input_grads = lax.fori_loop(
        0, micro_count + 1, backward_step, (zero_kv, reduced_zero, zero_inputs)
    )
    totals, input_grads = (totals, input_grads)
    return (
        section_rows[None],
        input_grads[None],
        totals[0][None],
        totals[1][None],
        totals[2][None],
        totals[3][None],
        totals[4][None],
        totals[5][None],
    )


def solution(mesh):
    return jax.shard_map(
        body,
        mesh=mesh,
        in_specs=(
            P("pipe", "dp", "tensor", None),
            P(None, "dp", None),
            P("dp", "tensor", None),
            P("pipe", None, None),
            P("pipe", None, None, "tensor"),
            P("pipe", "tensor", None),
            P("pipe", None, None, "tensor"),
            P("pipe", None, "tensor"),
            P("pipe", "tensor", None),
        ),
        out_specs=(
            P("pipe", "dp", "tensor", None),
            P("pipe", "dp", "tensor", None),
            P("pipe", None, "dp"),
            P("pipe", "dp", None, "tensor"),
            P("pipe", "tensor", "dp"),
            P("pipe", "dp", None, "tensor"),
            P("pipe", "dp", "tensor"),
            P("pipe", "tensor", "dp"),
        ),
        check_vma=False,
    )
```

profile of v0, /device:TPU:0, one launch (start us, length us, event | category | flops | bytes accessed | tf_op | source)
XLA Modules:
  0.0 1551.5 jit_solution(3891155846792082933)
XLA Ops:
  21.9 517.7 %while.54 = (s32[]{:T(128)}, bf16[1024,2,128]{2,1,0:T(2,128)(2,1)}, f32[3,3,256,512]{3,2,1,0:T(8,128)}, bf16[3,3,1024,512]{3,2,1,0:T(8,128)(2,1)}, bf16[3,1024,2...) while((s32[]{:T(128)}, bf16[1024,2,128]{2,1,0:T(2,128)(2,1)}, ...), condition=%wide.region_18.19_spmd.clone, body=%wide.region_0.18_spmd.clone.sunk | while | flops 3266185984 | bytes 130189864 | solution.py:355
  26.9 18.1 %all-gather.7.cloned.1.call-done = bf16[1024,512]{1,0:T(8,128)(2,1)} async-done(((bf16[256,512]{1,0:T(8,128)(2,1)}), bf16[1024,512]{1,0:T(8,128)(2,1)}) %all-gather.7.cloned.1.call-update) | async-done | bytes 1048592 | tf_op jit(solution)/shard_map/while/body/eval_jaxpr/all_gather | solution.py:202
  57.9 25.0 %reduce-scatter.29.cloned.1.call-done = bf16[256,512]{1,0:T(8,128)(2,1)} async-done(((bf16[1024,512]{1,0:T(8,128)(2,1)}), bf16[256,512]{1,0:T(8,128)(2,1)}) %reduce-scatter.29.cloned.1.call-update) | async-done | bytes 262160 | tf_op jit(solution)/shard_map/while/body/eval_jaxpr/reduce_scatter | solution.py:206
  87.9 16.9 %all-gather.9.cloned.1.call-done = bf16[1024,512]{1,0:T(8,128)(2,1)} async-done(((bf16[256,512]{1,0:T(8,128)(2,1)}), bf16[1024,512]{1,0:T(8,128)(2,1)}) %all-gather.9.cloned.1.call-update) | async-done | bytes 1048592 | tf_op jit(solution)/shard_map/while/body/eval_jaxpr/all_gather | solution.py:202
  108.9 36.3 %reduce-scatter.31.cloned.1.call-done = bf16[256,512]{1,0:T(8,128)(2,1)} async-done(((bf16[1024,512]{1,0:T(8,128)(2,1)}), bf16[256,512]{1,0:T(8,128)(2,1)}) %reduce-scatter.31.cloned.1.call-update) | async-done | bytes 262160 | tf_op jit(solution)/shard_map/while/body/eval_jaxpr/reduce_scatter | solution.py:206
  148.2 16.8 %all-gather.11.cloned.1.call-done = bf16[1024,512]{1,0:T(8,128)(2,1)} async-done(((bf16[256,512]{1,0:T(8,128)(2,1)}), bf16[1024,512]{1,0:T(8,128)(2,1)}) %all-gather.11.cloned.1.call-update) | async-done | bytes 1048592 | tf_op jit(solution)/shard_map/while/body/eval_jaxpr/all_gather | solution.py:202
  201.2 15.4 all-gather.7.cloned.1.call-done
  229.6 25.0 %reduce-scatter.29.cloned.1.call-done = bf16[256,512]{1,0:T(8,128)(2,1)} async-done(((bf16[1024,512]{1,0:T(8,128)(2,1)}), bf16[256,512]{1,0:T(8,128)(2,1)}) %reduce-scatter.29.cloned.1.call-update) | async-done | bytes 262160 | tf_op jit(solution)/shard_map/while/body/eval_jaxpr/reduce_scatter | solution.py:206
  259.6 16.8 %all-gather.9.cloned.1.call-done = bf16[1024,512]{1,0:T(8,128)(2,1)} async-done(((bf16[256,512]{1,0:T(8,128)(2,1)}), bf16[1024,512]{1,0:T(8,128)(2,1)}) %all-gather.9.cloned.1.call-update) | async-done | bytes 1048592 | tf_op jit(solution)/shard_map/while/body/eval_jaxpr/all_gather | solution.py:202
  280.5 36.3 %reduce-scatter.31.cloned.1.call-done = bf16[256,512]{1,0:T(8,128)(2,1)} async-done(((bf16[1024,512]{1,0:T(8,128)(2,1)}), bf16[256,512]{1,0:T(8,128)(2,1)}) %reduce-scatter.31.cloned.1.call-update) | async-done | bytes 262160 | tf_op jit(solution)/shard_map/while/body/eval_jaxpr/reduce_scatter | solution.py:206
  319.8 16.8 %all-gather.11.cloned.1.call-done = bf16[1024,512]{1,0:T(8,128)(2,1)} async-done(((bf16[256,512]{1,0:T(8,128)(2,1)}), bf16[1024,512]{1,0:T(8,128)(2,1)}) %all-gather.11.cloned.1.call-update) | async-done | bytes 1048592 | tf_op jit(solution)/shard_map/while/body/eval_jaxpr/all_gather | solution.py:202
  372.9 15.4 all-gather.7.cloned.1.call-done
  401.3 25.0 %reduce-scatter.29.cloned.1.call-done = bf16[256,512]{1,0:T(8,128)(2,1)} async-done(((bf16[1024,512]{1,0:T(8,128)(2,1)}), bf16[256,512]{1,0:T(8,128)(2,1)}) %reduce-scatter.29.cloned.1.call-update) | async-done | bytes 262160 | tf_op jit(solution)/shard_map/while/body/eval_jaxpr/reduce_scatter | solution.py:206
  431.2 16.8 %all-gather.9.cloned.1.call-done = bf16[1024,512]{1,0:T(8,128)(2,1)} async-done(((bf16[256,512]{1,0:T(8,128)(2,1)}), bf16[1024,512]{1,0:T(8,128)(2,1)}) %all-gather.9.cloned.1.call-update) | async-done | bytes 1048592 | tf_op jit(solution)/shard_map/while/body/eval_jaxpr/all_gather | solution.py:202
  452.2 36.3 %reduce-scatter.31.cloned.1.call-done = bf16[256,512]{1,0:T(8,128)(2,1)} async-done(((bf16[1024,512]{1,0:T(8,128)(2,1)}), bf16[256,512]{1,0:T(8,128)(2,1)}) %reduce-scatter.31.cloned.1.call-update) | async-done | bytes 262160 | tf_op jit(solution)/shard_map/while/body/eval_jaxpr/reduce_scatter | solution.py:206
  491.5 16.8 %all-gather.11.cloned.1.call-done = bf16[1024,512]{1,0:T(8,128)(2,1)} async-done(((bf16[256,512]{1,0:T(8,128)(2,1)}), bf16[1024,512]{1,0:T(8,128)(2,1)}) %all-gather.11.cloned.1.call-update) | async-done | bytes 1048592 | tf_op jit(solution)/shard_map/while/body/eval_jaxpr/all_gather | solution.py:202
  541.4 1000.0 %while.55 = (s32[]{:T(128)}, bf16[1024,2,128]{0,2,1:T(8,128)(2,1)}, f32[3,128]{1,0:T(4,128)}, f32[128,3,128]{2,0,1:T(8,128)}, f32[128,128]{1,0:T(8,128)}, /*inde...) while((s32[]{:T(128)}, bf16[1024,2,128]{0,2,1:T(8,128)(2,1)}, ...), condition=%wide.region_55.56_spmd.clone, body=%wide.region_19.55_spmd.clone.sunk | while | flops 8540954624 | bytes 374696032 | solution.py:429
  545.3 15.3 all-gather.13.cloned.1.call-done
  560.7 10.5 conditional.14
  577.7 26.4 %reduce-scatter.35.cloned.1.call-done = bf16[256,512]{1,0:T(8,128)(2,1)} async-done(((bf16[1024,512]{1,0:T(8,128)(2,1)}), bf16[256,512]{1,0:T(8,128)(2,1)}) %reduce-scatter.35.cloned.1.call-update) | async-done | bytes 262160 | tf_op jit(solution)/shard_map/while/body/eval_jaxpr/reduce_scatter | solution.py:216
  611.4 16.2 %all-gather.15.cloned.1.call-done = bf16[1024,512]{1,0:T(8,128)(2,1)} async-done(((bf16[256,512]{1,0:T(8,128)(2,1)}), bf16[1024,512]{1,0:T(8,128)(2,1)}) %all-gather.15.cloned.1.call-update) | async-done | bytes 1048592 | tf_op jit(solution)/shard_map/while/body/eval_jaxpr/all_gather | solution.py:212
  627.6 25.2 %conditional.15 = (bf16[1024,512]{1,0:T(8,128)(2,1)}, f32[512,512]{1,0:T(8,128)}, f32[512,512]{1,0:T(8,128)}, f32[512,2,128]{0,2,1:T(8,128)}, bf16[1024,2,128]{0,2,1:T(8,128)(2,1)}) conditional(s32[]{:T(128)} %convert_element_type.829, (s32[1,1,1024]{2,1,0:T(1,128)}, s32[1,1,1024]{2,1,0:T(1,128)}, bf16[3,1024,512]{2,1,0:T(8,128)(2,1)S(1)}, ...), branch_computations={%region_27.30_spmd, %region_31.31_spmd} | conditional | flops 2699558912 | bytes 122945824 | solution.py:396
  653.6 34.3 %reduce-scatter.37.cloned.1.call-done = bf16[256,512]{1,0:T(8,128)(2,1)} async-done(((bf16[1024,512]{1,0:T(8,128)(2,1)}), bf16[256,512]{1,0:T(8,128)(2,1)}) %reduce-scatter.37.cloned.1.call-update) | async-done | bytes 262160 | tf_op jit(solution)/shard_map/while/body/eval_jaxpr/reduce_scatter | solution.py:216
  755.7 20.9 %reduce-scatter.49.cloned.1.call-done = bf16[128,512]{1,0:T(8,128)(2,1)} async-done(((bf16[512,512]{1,0:T(8,128)(2,1)}), bf16[128,512]{1,0:T(8,128)(2,1)}) %reduce-scatter.49.cloned.1.call-update) | async-done | bytes 131088 | tf_op jit(solution)/shard_map/while/body/eval_jaxpr/reduce_scatter | solution.py:244
  777.6 19.1 %reduce-scatter.45.cloned.1.call-done = bf16[128,128]{1,0:T(8,128)(2,1)} async-done(((bf16[512,128]{1,0:T(8,128)(2,1)}), bf16[128,128]{1,0:T(8,128)(2,1)}) %reduce-scatter.45.cloned.1.call-update) | async-done | bytes 32784 | tf_op jit(solution)/shard_map/while
  798.3 19.7 %reduce-scatter.43.cloned.1.call-done = bf16[128,3,128]{2,0,1:T(8,128)(2,1)} async-done(((bf16[512,3,128]{2,0,1:T(8,128)(2,1)}), bf16[128,3,128]{2,0,1:T(8,128)(2,1)}) %reduce-scatter.43.cloned.1.call-update) | async-done | bytes 98320 | tf_op jit(solution)/shard_map/while/body/eval_jaxpr/reduce_scatter | solution.py:235
  819.5 24.3 %reduce-scatter.39.cloned.1.call-done = bf16[256,512]{1,0:T(8,128)(2,1)} async-done(((bf16[1024,512]{1,0:T(8,128)(2,1)}), bf16[256,512]{1,0:T(8,128)(2,1)}) %reduce-scatter.39.cloned.1.call-update) | async-done | bytes 262160 | tf_op jit(solution)/shard_map/while/body/eval_jaxpr/reduce_scatter | solution.py:216
  854.9 19.0 %reduce-scatter.41.cloned.1.call-done = bf16[128,3]{1,0:T(8,128)(2,1)} async-done(((bf16[512,3]{1,0:T(8,128)(2,1)}), bf16[128,3]{1,0:T(8,128)(2,1)}) %reduce-scatter.41.cloned.1.call-update) | async-done | bytes 784 | tf_op jit(solution)/shard_map/while
  880.0 13.5 all-gather.13.cloned.1.call-done
  910.5 26.4 %reduce-scatter.35.cloned.1.call-done = bf16[256,512]{1,0:T(8,128)(2,1)} async-done(((bf16[1024,512]{1,0:T(8,128)(2,1)}), bf16[256,512]{1,0:T(8,128)(2,1)}) %reduce-scatter.35.cloned.1.call-update) | async-done | bytes 262160 | tf_op jit(solution)/shard_map/while/body/eval_jaxpr/reduce_scatter | solution.py:216
  944.1 16.2 %all-gather.15.cloned.1.call-done = bf16[1024,512]{1,0:T(8,128)(2,1)} async-done(((bf16[256,512]{1,0:T(8,128)(2,1)}), bf16[1024,512]{1,0:T(8,128)(2,1)}) %all-gather.15.cloned.1.call-update) | async-done | bytes 1048592 | tf_op jit(solution)/shard_map/while/body/eval_jaxpr/all_gather | solution.py:212
  960.3 25.0 %conditional.15 = (bf16[1024,512]{1,0:T(8,128)(2,1)}, f32[512,512]{1,0:T(8,128)}, f32[512,512]{1,0:T(8,128)}, f32[512,2,128]{0,2,1:T(8,128)}, bf16[1024,2,128]{0,2,1:T(8,128)(2,1)}) conditional(s32[]{:T(128)} %convert_element_type.829, (s32[1,1,1024]{2,1,0:T(1,128)}, s32[1,1,1024]{2,1,0:T(1,128)}, bf16[3,1024,512]{2,1,0:T(8,128)(2,1)S(1)}, ...), branch_computations={%region_27.30_spmd, %region_31.31_spmd} | conditional | flops 2699558912 | bytes 122945824 | solution.py:396
  986.2 34.3 %reduce-scatter.37.cloned.1.call-done = bf16[256,512]{1,0:T(8,128)(2,1)} async-done(((bf16[1024,512]{1,0:T(8,128)(2,1)}), bf16[256,512]{1,0:T(8,128)(2,1)}) %reduce-scatter.37.cloned.1.call-update) | async-done | bytes 262160 | tf_op jit(solution)/shard_map/while/body/eval_jaxpr/reduce_scatter | solution.py:216
  1088.1 21.1 %reduce-scatter.49.cloned.1.call-done = bf16[128,512]{1,0:T(8,128)(2,1)} async-done(((bf16[512,512]{1,0:T(8,128)(2,1)}), bf16[128,512]{1,0:T(8,128)(2,1)}) %reduce-scatter.49.cloned.1.call-update) | async-done | bytes 131088 | tf_op jit(solution)/shard_map/while/body/eval_jaxpr/reduce_scatter | solution.py:244
  1110.2 19.1 %reduce-scatter.45.cloned.1.call-done = bf16[128,128]{1,0:T(8,128)(2,1)} async-done(((bf16[512,128]{1,0:T(8,128)(2,1)}), bf16[128,128]{1,0:T(8,128)(2,1)}) %reduce-scatter.45.cloned.1.call-update) | async-done | bytes 32784 | tf_op jit(solution)/shard_map/while
  1131.7 18.9 %reduce-scatter.43.cloned.1.call-done = bf16[128,3,128]{2,0,1:T(8,128)(2,1)} async-done(((bf16[512,3,128]{2,0,1:T(8,128)(2,1)}), bf16[128,3,128]{2,0,1:T(8,128)(2,1)}) %reduce-scatter.43.cloned.1.call-update) | async-done | bytes 98320 | tf_op jit(solution)/shard_map/while/body/eval_jaxpr/reduce_scatter | solution.py:235
  1152.2 24.2 %reduce-scatter.39.cloned.1.call-done = bf16[256,512]{1,0:T(8,128)(2,1)} async-done(((bf16[1024,512]{1,0:T(8,128)(2,1)}), bf16[256,512]{1,0:T(8,128)(2,1)}) %reduce-scatter.39.cloned.1.call-update) | async-done | bytes 262160 | tf_op jit(solution)/shard_map/while/body/eval_jaxpr/reduce_scatter | solution.py:216
  1187.5 19.0 %reduce-scatter.41.cloned.1.call-done = bf16[128,3]{1,0:T(8,128)(2,1)} async-done(((bf16[512,3]{1,0:T(8,128)(2,1)}), bf16[128,3]{1,0:T(8,128)(2,1)}) %reduce-scatter.41.cloned.1.call-update) | async-done | bytes 784 | tf_op jit(solution)/shard_map/while
  1212.4 13.1 all-gather.13.cloned.1.call-done
  1242.6 26.4 %reduce-scatter.35.cloned.1.call-done = bf16[256,512]{1,0:T(8,128)(2,1)} async-done(((bf16[1024,512]{1,0:T(8,128)(2,1)}), bf16[256,512]{1,0:T(8,128)(2,1)}) %reduce-scatter.35.cloned.1.call-update) | async-done | bytes 262160 | tf_op jit(solution)/shard_map/while/body/eval_jaxpr/reduce_scatter | solution.py:216
  1276.2 16.2 %all-gather.15.cloned.1.call-done = bf16[1024,512]{1,0:T(8,128)(2,1)} async-done(((bf16[256,512]{1,0:T(8,128)(2,1)}), bf16[1024,512]{1,0:T(8,128)(2,1)}) %all-gather.15.cloned.1.call-update) | async-done | bytes 1048592 | tf_op jit(solution)/shard_map/while/body/eval_jaxpr/all_gather | solution.py:212
  1292.4 25.2 %conditional.15 = (bf16[1024,512]{1,0:T(8,128)(2,1)}, f32[512,512]{1,0:T(8,128)}, f32[512,512]{1,0:T(8,128)}, f32[512,2,128]{0,2,1:T(8,128)}, bf16[1024,2,128]{0,2,1:T(8,128)(2,1)}) conditional(s32[]{:T(128)} %convert_element_type.829, (s32[1,1,1024]{2,1,0:T(1,128)}, s32[1,1,1024]{2,1,0:T(1,128)}, bf16[3,1024,512]{2,1,0:T(8,128)(2,1)S(1)}, ...), branch_computations={%region_27.30_spmd, %region_31.31_spmd} | conditional | flops 2699558912 | bytes 122945824 | solution.py:396
  1318.5 34.3 %reduce-scatter.37.cloned.1.call-done = bf16[256,512]{1,0:T(8,128)(2,1)} async-done(((bf16[1024,512]{1,0:T(8,128)(2,1)}), bf16[256,512]{1,0:T(8,128)(2,1)}) %reduce-scatter.37.cloned.1.call-update) | async-done | bytes 262160 | tf_op jit(solution)/shard_map/while/body/eval_jaxpr/reduce_scatter | solution.py:216
  1420.5 21.1 %reduce-scatter.49.cloned.1.call-done = bf16[128,512]{1,0:T(8,128)(2,1)} async-done(((bf16[512,512]{1,0:T(8,128)(2,1)}), bf16[128,512]{1,0:T(8,128)(2,1)}) %reduce-scatter.49.cloned.1.call-update) | async-done | bytes 131088 | tf_op jit(solution)/shard_map/while/body/eval_jaxpr/reduce_scatter | solution.py:244
  1442.6 19.1 %reduce-scatter.45.cloned.1.call-done = bf16[128,128]{1,0:T(8,128)(2,1)} async-done(((bf16[512,128]{1,0:T(8,128)(2,1)}), bf16[128,128]{1,0:T(8,128)(2,1)}) %reduce-scatter.45.cloned.1.call-update) | async-done | bytes 32784 | tf_op jit(solution)/shard_map/while
  1464.1 18.8 %reduce-scatter.43.cloned.1.call-done = bf16[128,3,128]{2,0,1:T(8,128)(2,1)} async-done(((bf16[512,3,128]{2,0,1:T(8,128)(2,1)}), bf16[128,3,128]{2,0,1:T(8,128)(2,1)}) %reduce-scatter.43.cloned.1.call-update) | async-done | bytes 98320 | tf_op jit(solution)/shard_map/while/body/eval_jaxpr/reduce_scatter | solution.py:235
  1484.5 24.1 %reduce-scatter.39.cloned.1.call-done = bf16[256,512]{1,0:T(8,128)(2,1)} async-done(((bf16[1024,512]{1,0:T(8,128)(2,1)}), bf16[256,512]{1,0:T(8,128)(2,1)}) %reduce-scatter.39.cloned.1.call-update) | async-done | bytes 262160 | tf_op jit(solution)/shard_map/while/body/eval_jaxpr/reduce_scatter | solution.py:216
  1519.7 19.0 %reduce-scatter.41.cloned.1.call-done = bf16[128,3]{1,0:T(8,128)(2,1)} async-done(((bf16[512,3]{1,0:T(8,128)(2,1)}), bf16[128,3]{1,0:T(8,128)(2,1)}) %reduce-scatter.41.cloned.1.call-update) | async-done | bytes 784 | tf_op jit(solution)/shard_map/while
  (767 shorter events, 633.2 us)
Async XLA Ops:
  25.4 57.6 %reduce-scatter.29.cloned.1.call-start = ((), (), s32[]{:S(2)}) async-start(), calls=%async_computation.13 | async-start | bytes 1310720 | tf_op jit(solution)/shard_map/while/body/eval_jaxpr/reduce_scatter | solution.py:206
  57.9 46.8 %all-gather.9.cloned.1.call-start = ((), (), s32[]{:S(2)}) async-start(), calls=%async_computation.14 | async-start | bytes 1310720 | tf_op jit(solution)/shard_map/while/body/eval_jaxpr/all_gather | solution.py:202
  87.8 57.4 %reduce-scatter.31.cloned.1.call-start = ((), (), s32[]{:S(2)}) async-start(), calls=%async_computation.15 | async-start | bytes 1310720 | tf_op jit(solution)/shard_map/while/body/eval_jaxpr/reduce_scatter | solution.py:206
  108.8 56.2 %all-gather.11.cloned.1.call-start = ((), (), s32[]{:S(2)}) async-start(), calls=%async_computation.16 | async-start | bytes 1310720 | tf_op jit(solution)/shard_map/while/body/eval_jaxpr/all_gather | solution.py:202
  199.8 54.9 %reduce-scatter.29.cloned.1.call-start = ((), (), s32[]{:S(2)}) async-start(), calls=%async_computation.13 | async-start | bytes 1310720 | tf_op jit(solution)/shard_map/while/body/eval_jaxpr/reduce_scatter | solution.py:206
  229.6 46.8 %all-gather.9.cloned.1.call-start = ((), (), s32[]{:S(2)}) async-start(), calls=%async_computation.14 | async-start | bytes 1310720 | tf_op jit(solution)/shard_map/while/body/eval_jaxpr/all_gather | solution.py:202
  259.5 57.3 %reduce-scatter.31.cloned.1.call-start = ((), (), s32[]{:S(2)}) async-start(), calls=%async_computation.15 | async-start | bytes 1310720 | tf_op jit(solution)/shard_map/while/body/eval_jaxpr/reduce_scatter | solution.py:206
  280.5 56.2 %all-gather.11.cloned.1.call-start = ((), (), s32[]{:S(2)}) async-start(), calls=%async_computation.16 | async-start | bytes 1310720 | tf_op jit(solution)/shard_map/while/body/eval_jaxpr/all_gather | solution.py:202
  371.4 54.9 %reduce-scatter.29.cloned.1.call-start = ((), (), s32[]{:S(2)}) async-start(), calls=%async_computation.13 | async-start | bytes 1310720 | tf_op jit(solution)/shard_map/while/body/eval_jaxpr/reduce_scatter | solution.py:206
  401.2 46.8 %all-gather.9.cloned.1.call-start = ((), (), s32[]{:S(2)}) async-start(), calls=%async_computation.14 | async-start | bytes 1310720 | tf_op jit(solution)/shard_map/while/body/eval_jaxpr/all_gather | solution.py:202
  431.1 57.3 %reduce-scatter.31.cloned.1.call-start = ((), (), s32[]{:S(2)}) async-start(), calls=%async_computation.15 | async-start | bytes 1310720 | tf_op jit(solution)/shard_map/while/body/eval_jaxpr/reduce_scatter | solution.py:206
  452.1 56.2 %all-gather.11.cloned.1.call-start = ((), (), s32[]{:S(2)}) async-start(), calls=%async_computation.16 | async-start | bytes 1310720 | tf_op jit(solution)/shard_map/while/body/eval_jaxpr/all_gather | solution.py:202
  543.2 60.9 %reduce-scatter.35.cloned.1.call-start = ((), (), s32[]{:S(2)}) async-start(), calls=%async_computation.19 | async-start | bytes 1310720 | tf_op jit(solution)/shard_map/while/body/eval_jaxpr/reduce_scatter | solution.py:216
  571.2 56.4 %all-gather.15.cloned.1.call-start = ((), (), s32[]{:S(2)}) async-start(), calls=%async_computation.20 | async-start | bytes 1310720 | tf_op jit(solution)/shard_map/while/body/eval_jaxpr/all_gather | solution.py:212
  610.7 77.2 %reduce-scatter.37.cloned.1.call-start = ((), (), s32[]{:S(2)}) async-start(), calls=%async_computation.21 | async-start | bytes 1310720 | tf_op jit(solution)/shard_map/while/body/eval_jaxpr/reduce_scatter | solution.py:216
  652.8 61.1 %all-gather.17.cloned.1.call-start = ((), (), s32[]{:S(2)}) async-start(), calls=%async_computation.22 | async-start | bytes 1310720 | tf_op jit(solution)/shard_map/while/body/eval_jaxpr/all_gather | solution.py:212
  693.6 50.4 %reduce-scatter.47.cloned.1.call-start = ((), (), s32[]{:S(2)}) async-start(), calls=%async_computation.27 | async-start | bytes 327680 | tf_op jit(solution)/shard_map/while
  698.9 55.7 %reduce-scatter.51.cloned.1.call-start = ((), (), s32[]{:S(2)}) async-start(), calls=%async_computation.29 | async-start | bytes 655360 | tf_op jit(solution)/shard_map/while
  706.8 69.8 %reduce-scatter.49.cloned.1.call-start = ((), (), s32[]{:S(2)}) async-start(), calls=%async_computation.28 | async-start | bytes 655360 | tf_op jit(solution)/shard_map/while/body/eval_jaxpr/reduce_scatter | solution.py:244
  713.7 83.1 %reduce-scatter.45.cloned.1.call-start = ((), (), s32[]{:S(2)}) async-start(), calls=%async_computation.26 | async-start | bytes 163840 | tf_op jit(solution)/shard_map/while
  733.2 84.7 %reduce-scatter.43.cloned.1.call-start = ((), (), s32[]{:S(2)}) async-start(), calls=%async_computation.25 | async-start | bytes 491520 | tf_op jit(solution)/shard_map/while/body/eval_jaxpr/reduce_scatter | solution.py:235
  740.1 103.7 %reduce-scatter.39.cloned.1.call-start = ((), (), s32[]{:S(2)}) async-start(), calls=%async_computation.23 | async-start | bytes 1310720 | tf_op jit(solution)/shard_map/while/body/eval_jaxpr/reduce_scatter | solution.py:216
  741.9 131.9 %reduce-scatter.41.cloned.1.call-start = ((), (), s32[]{:S(2)}) async-start(), calls=%async_computation.24 | async-start | bytes 163840 | tf_op jit(solution)/shard_map/while
  742.8 132.0 %collective-permute-start.1 = (bf16[1024,2,128]{0,2,1:T(8,128)(2,1)}, bf16[1024,2,128]{0,2,1:T(8,128)(2,1)S(1)}, u32[]{:S(2)}, u32[]{:S(2)}) collective-permute-start(bf16[1024,2,128]{0,2,1:T(8,128)(2,1)} %get-tuple-element.1838), channel_id=1, source_target_pairs={{16,0},{17,1},{18,2},{19,3},{20,4},{21,5},{22,6},{23,7},{24,8},{25... | collective-permute-start | bytes 1572872 | tf_op jit(solution)/shard_map/while/body/eval_jaxpr/ppermute | solution.py:16
  877.8 59.1 %reduce-scatter.35.cloned.1.call-start = ((), (), s32[]{:S(2)}) async-start(), calls=%async_computation.19 | async-start | bytes 1310720 | tf_op jit(solution)/shard_map/while/body/eval_jaxpr/reduce_scatter | solution.py:216
  904.0 56.4 %all-gather.15.cloned.1.call-start = ((), (), s32[]{:S(2)}) async-start(), calls=%async_computation.20 | async-start | bytes 1310720 | tf_op jit(solution)/shard_map/while/body/eval_jaxpr/all_gather | solution.py:212
  943.4 77.0 %reduce-scatter.37.cloned.1.call-start = ((), (), s32[]{:S(2)}) async-start(), calls=%async_computation.21 | async-start | bytes 1310720 | tf_op jit(solution)/shard_map/while/body/eval_jaxpr/reduce_scatter | solution.py:216
  985.4 61.3 %all-gather.17.cloned.1.call-start = ((), (), s32[]{:S(2)}) async-start(), calls=%async_computation.22 | async-start | bytes 1310720 | tf_op jit(solution)/shard_map/while/body/eval_jaxpr/all_gather | solution.py:212
  1026.2 50.6 %reduce-scatter.47.cloned.1.call-start = ((), (), s32[]{:S(2)}) async-start(), calls=%async_computation.27 | async-start | bytes 327680 | tf_op jit(solution)/shard_map/while
  1031.5 55.5 %reduce-scatter.51.cloned.1.call-start = ((), (), s32[]{:S(2)}) async-start(), calls=%async_computation.29 | async-start | bytes 655360 | tf_op jit(solution)/shard_map/while
  1039.4 69.8 %reduce-scatter.49.cloned.1.call-start = ((), (), s32[]{:S(2)}) async-start(), calls=%async_computation.28 | async-start | bytes 655360 | tf_op jit(solution)/shard_map/while/body/eval_jaxpr/reduce_scatter | solution.py:244
  1046.2 83.1 %reduce-scatter.45.cloned.1.call-start = ((), (), s32[]{:S(2)}) async-start(), calls=%async_computation.26 | async-start | bytes 163840 | tf_op jit(solution)/shard_map/while
  1066.0 84.6 %reduce-scatter.43.cloned.1.call-start = ((), (), s32[]{:S(2)}) async-start(), calls=%async_computation.25 | async-start | bytes 491520 | tf_op jit(solution)/shard_map/while/body/eval_jaxpr/reduce_scatter | solution.py:235
  1072.9 103.6 %reduce-scatter.39.cloned.1.call-start = ((), (), s32[]{:S(2)}) async-start(), calls=%async_computation.23 | async-start | bytes 1310720 | tf_op jit(solution)/shard_map/while/body/eval_jaxpr/reduce_scatter | solution.py:216
  1074.7 131.8 %reduce-scatter.41.cloned.1.call-start = ((), (), s32[]{:S(2)}) async-start(), calls=%async_computation.24 | async-start | bytes 163840 | tf_op jit(solution)/shard_map/while
  1075.5 131.8 %collective-permute-start.1 = (bf16[1024,2,128]{0,2,1:T(8,128)(2,1)}, bf16[1024,2,128]{0,2,1:T(8,128)(2,1)S(1)}, u32[]{:S(2)}, u32[]{:S(2)}) collective-permute-start(bf16[1024,2,128]{0,2,1:T(8,128)(2,1)} %get-tuple-element.1838), channel_id=1, source_target_pairs={{16,0},{17,1},{18,2},{19,3},{20,4},{21,5},{22,6},{23,7},{24,8},{25... | collective-permute-start | bytes 1572872 | tf_op jit(solution)/shard_map/while/body/eval_jaxpr/ppermute | solution.py:16
  1210.2 58.7 %reduce-scatter.35.cloned.1.call-start = ((), (), s32[]{:S(2)}) async-start(), calls=%async_computation.19 | async-start | bytes 1310720 | tf_op jit(solution)/shard_map/while/body/eval_jaxpr/reduce_scatter | solution.py:216
  1236.0 56.4 %all-gather.15.cloned.1.call-start = ((), (), s32[]{:S(2)}) async-start(), calls=%async_computation.20 | async-start | bytes 1310720 | tf_op jit(solution)/shard_map/while/body/eval_jaxpr/all_gather | solution.py:212
  1275.5 77.2 %reduce-scatter.37.cloned.1.call-start = ((), (), s32[]{:S(2)}) async-start(), calls=%async_computation.21 | async-start | bytes 1310720 | tf_op jit(solution)/shard_map/while/body/eval_jaxpr/reduce_scatter | solution.py:216
  1317.7 61.1 %all-gather.17.cloned.1.call-start = ((), (), s32[]{:S(2)}) async-start(), calls=%async_computation.22 | async-start | bytes 1310720 | tf_op jit(solution)/shard_map/while/body/eval_jaxpr/all_gather | solution.py:212
  1358.5 50.4 %reduce-scatter.47.cloned.1.call-start = ((), (), s32[]{:S(2)}) async-start(), calls=%async_computation.27 | async-start | bytes 327680 | tf_op jit(solution)/shard_map/while
  1363.8 55.6 %reduce-scatter.51.cloned.1.call-start = ((), (), s32[]{:S(2)}) async-start(), calls=%async_computation.29 | async-start | bytes 655360 | tf_op jit(solution)/shard_map/while
  1371.7 69.9 %reduce-scatter.49.cloned.1.call-start = ((), (), s32[]{:S(2)}) async-start(), calls=%async_computation.28 | async-start | bytes 655360 | tf_op jit(solution)/shard_map/while/body/eval_jaxpr/reduce_scatter | solution.py:244
  1378.5 83.2 %reduce-scatter.45.cloned.1.call-start = ((), (), s32[]{:S(2)}) async-start(), calls=%async_computation.26 | async-start | bytes 163840 | tf_op jit(solution)/shard_map/while
  1398.0 84.8 %reduce-scatter.43.cloned.1.call-start = ((), (), s32[]{:S(2)}) async-start(), calls=%async_computation.25 | async-start | bytes 491520 | tf_op jit(solution)/shard_map/while/body/eval_jaxpr/reduce_scatter | solution.py:235
  1404.9 103.6 %reduce-scatter.39.cloned.1.call-start = ((), (), s32[]{:S(2)}) async-start(), calls=%async_computation.23 | async-start | bytes 1310720 | tf_op jit(solution)/shard_map/while/body/eval_jaxpr/reduce_scatter | solution.py:216
  1406.8 131.9 %reduce-scatter.41.cloned.1.call-start = ((), (), s32[]{:S(2)}) async-start(), calls=%async_computation.24 | async-start | bytes 163840 | tf_op jit(solution)/shard_map/while
  1407.6 131.9 %collective-permute-start.1 = (bf16[1024,2,128]{0,2,1:T(8,128)(2,1)}, bf16[1024,2,128]{0,2,1:T(8,128)(2,1)S(1)}, u32[]{:S(2)}, u32[]{:S(2)}) collective-permute-start(bf16[1024,2,128]{0,2,1:T(8,128)(2,1)} %get-tuple-element.1838), channel_id=1, source_target_pairs={{16,0},{17,1},{18,2},{19,3},{20,4},{21,5},{22,6},{23,7},{24,8},{25... | collective-permute-start | bytes 1572872 | tf_op jit(solution)/shard_map/while/body/eval_jaxpr/ppermute | solution.py:16
  (144 other events, 4148.8 us)
Sparse Core Ops, SparseCore 0:
  25.5 19.4 all-gather.6
  58.0 24.8 reduce-scatter.28
  87.9 16.7 all-gather.8
  108.9 36.2 reduce-scatter.30
  148.3 16.7 all-gather.10
  168.7 25.6 reduce-scatter.32
  199.9 16.7 all-gather.6
  229.7 24.9 reduce-scatter.28
  280.6 36.1 reduce-scatter.30
  319.9 16.7 all-gather.10
  340.3 25.6 reduce-scatter.32
  371.5 16.7 all-gather.6
  401.3 24.8 reduce-scatter.28
  431.2 16.7 all-gather.8
  452.2 36.1 reduce-scatter.30
  491.5 16.7 all-gather.10
  512.0 25.6 reduce-scatter.32
  571.3 32.7 reduce-scatter.34
  610.8 16.7 all-gather.14
  652.9 34.8 reduce-scatter.36
  712.7 19.6 reduce-scatter.46
  734.7 19.8 reduce-scatter.50
  756.7 19.8 reduce-scatter.48
  779.3 17.4 reduce-scatter.44
  799.1 18.7 reduce-scatter.42
  820.6 23.1 reduce-scatter.38
  853.5 20.2 reduce-scatter.40
  904.1 32.7 reduce-scatter.34
  943.6 16.7 all-gather.14
  985.5 34.8 reduce-scatter.36
  1045.3 19.6 reduce-scatter.46
  1067.1 19.8 reduce-scatter.50
  1089.3 19.8 reduce-scatter.48
  1111.9 17.4 reduce-scatter.44
  1131.7 18.7 reduce-scatter.42
  1153.2 23.1 reduce-scatter.38
  1186.2 20.2 reduce-scatter.40
  1236.2 32.7 reduce-scatter.34
  1275.7 16.7 all-gather.14
  1317.8 34.8 reduce-scatter.36
  1358.6 16.7 all-gather.16
  1377.6 19.6 reduce-scatter.46
  1399.4 19.8 reduce-scatter.50
  1421.6 19.9 reduce-scatter.48
  1444.2 17.4 reduce-scatter.44
  1464.1 18.6 reduce-scatter.42
  1485.4 23.1 reduce-scatter.38
  1518.3 20.3 reduce-scatter.40
  (6 shorter events, 96.3 us)
where the time goes:
time: 1570 us; the launch traced here: 1550 us
  waiting for transfers between devices  968 us (62%)
  matrix products  199 us (13%)
  other arithmetic  162 us (10%)
  local copies, waits for them, and re-layouts  141 us (9%)
  loops' own time  27.3 us (2%)
  starting transfers between devices  22.2 us (1%)
  blocking collectives  17.6 us (1%)
    reduce_scatter x9, waiting for transfers between devices, collect_grads(): lax.psum_scatter(partial_value.astype(jnp.bfloat16), 'tensor', scatter_di...  254 us
    reduce_scatter x9, waiting for transfers between devices, collect_rows(): lax.psum_scatter(partial_value.astype(jnp.bfloat16), 'tensor', scatter_di...  206 us
    all_gather x9, waiting for transfers between devices, spread_rows(): return lax.all_gather(local_part, 'tensor', axis=0, tiled=True)  150 us
    while x66, waiting for transfers between devices  143 us
    all_gather x9, waiting for transfers between devices, spread_grads(): return lax.all_gather(local_part, 'tensor', axis=0, tiled=True)  90.6 us
    reduce_scatter x3, waiting for transfers between devices, reduce_weights(): lax.psum_scatter(tick_grads[4].astype(jnp.bfloat16), 'dp', scatter_dimens...  63.1 us
    reduce_scatter x3, waiting for transfers between devices, reduce_weights(): lax.psum_scatter(tick_grads[1].astype(jnp.bfloat16), 'dp', scatter_dimens...  57.3 us
    while x264, local copies, waits for them, and re-layouts  53.9 us
  transfers between devices with their start and end apart: 60, of which 51 were waited for; matrix products, arithmetic and copies ran while one was open for 15% of the time, Pallas kernels for 0%

commit v1 on v0

v1 whole, which is shorter than its diff:
```python
import functools

import jax
import jax.numpy as jnp
from jax import lax
from jax.experimental import pallas as pl
from jax.experimental.pallas import tpu as pltpu
from jax.sharding import PartitionSpec as P

EPS = 1e-05
MASKED = -1000000000.0
DH = 64
HALO = 64
F32 = jnp.float32
BF16 = jnp.bfloat16
GELU_C = 0.7978845608028654
GELU_A = 0.044715
VMEM = pl.BlockSpec(memory_space=pltpu.VMEM)
SMEM = pl.BlockSpec(memory_space=pltpu.SMEM)


def mm(a, b):
    return lax.dot_general(a, b, (((1,), (0,)), ((), ())), preferred_element_type=F32)


def mm_nt(a, b):
    return lax.dot_general(a, b, (((1,), (1,)), ((), ())), preferred_element_type=F32)


def mm_tn(a, b):
    return lax.dot_general(a, b, (((0,), (0,)), ((), ())), preferred_element_type=F32)


def norm_parts(v):
    c = v - jnp.mean(v, axis=-1, keepdims=True)
    r = lax.rsqrt(jnp.mean(c * c, axis=-1, keepdims=True) + EPS)
    return c * r, r


def norm(v, gain):
    xhat, _ = norm_parts(v)
    return xhat * gain


def norm_back(v, gain, dn):
    xhat, r = norm_parts(v)
    dxh = dn * gain
    m1 = jnp.mean(dxh, axis=-1, keepdims=True)
    m2 = jnp.mean(dxh * xhat, axis=-1, keepdims=True)
    return r * (dxh - m1 - xhat * m2), jnp.sum(dn * xhat, axis=0, keepdims=True)


def lane_low(shape):
    return lax.broadcasted_iota(jnp.int32, shape, 1) < DH


def head_pick(rows, h):
    low = lane_low(rows.shape)
    return jnp.where(low if h == 0 else jnp.logical_not(low), rows, jnp.zeros_like(rows))


def pair_join(a, b):
    return jnp.where(lane_low(a.shape), a, b)


def attend(q2, k2, v2, bias, keep):
    outs = []
    for h in range(2):
        s = mm_nt(head_pick(q2, h), k2) + bias
        e = jnp.exp(s - jnp.max(s, axis=-1, keepdims=True))
        p = e * (1.0 / jnp.sum(e, axis=-1, keepdims=True))
        pb = p.astype(BF16)
        keep(h, pb)
        outs.append(mm(pb, v2))
    return pair_join(*outs)


def attend_back(q2, k2, v2, do2, pbs):
    dq, dk, dv = [], [], []
    for h in range(2):
        pb = pbs(h)
        dp = mm_nt(head_pick(do2, h), v2)
        dv.append(mm_tn(pb, do2))
        p = pb.astype(F32)
        ds = (p * (dp - jnp.sum(dp * p, axis=-1, keepdims=True))).astype(BF16)
        dq.append(mm(ds, k2))
        dk.append(mm_tn(ds, q2))
    return pair_join(*dq) * (DH**-0.5), pair_join(*dk), pair_join(*dv)


def gelu_parts(h):
    th = jnp.tanh(GELU_C * (h + GELU_A * (h * h * h)))
    half = 0.5 * (1.0 + th)
    u = h * half
    slope = half + (0.5 * GELU_C) * h * (1.0 - th * th) * (1.0 + (3.0 * GELU_A) * (h * h))
    return u, slope


def self_forward(is_enc_ref, xw_ref, sq_ref, sk_ref, gain_ref, wa_ref, wo_ref, nw_ref, q_ref, k_ref, v_ref, p_ref, o_ref, e1_ref, bias_ref):
    rows, win, width = xw_ref.shape
    own = sq_ref.shape[1]
    is_enc = is_enc_ref[0] > 0
    for r in range(rows):
        xr = xw_ref[r].astype(F32)
        nw_ref[pl.ds(r * win, win), :] = norm(xr, gain_ref[pl.ds(0, 1), :]).astype(BF16)
        same = sq_ref[r] == sk_ref[r]
        qpos = lax.broadcasted_iota(jnp.int32, (own, win), 0)
        kpos = lax.broadcasted_iota(jnp.int32, (own, win), 1) - HALO
        before = kpos - qpos <= jnp.where(is_enc, 4 * win, 0)
        bias_ref[r] = jnp.where(same & before, 0.0, MASKED)

    def project(t, _):
        packed = mm(nw_ref[...], wa_ref[t])
        hw = q_ref.shape[-1]
        for r in range(rows):
            q = packed[r * win + HALO : r * win + HALO + own, :hw].astype(BF16)
            q_ref[t, r] = q * jnp.asarray(DH**-0.5, BF16)
            k_ref[t, r] = packed[r * win : (r + 1) * win, hw : 2 * hw].astype(BF16)
            v_ref[t, r] = packed[r * win : (r + 1) * win, 2 * hw :].astype(BF16)
        return 0

    lax.fori_loop(0, wa_ref.shape[0], project, 0)

    def one(i, _):
        t, r = i // rows, i % rows

        def keep(h, pb):
            p_ref[t, r, h] = pb

        o2 = attend(q_ref[t, r], k_ref[t, r], v_ref[t, r], bias_ref[r], keep)
        hw = o2.shape[1]
        o_ref[pl.ds(pl.multiple_of(r * own, own), own), pl.ds(pl.multiple_of(t * hw, hw), hw)] = o2.astype(BF16)
        return 0

    lax.fori_loop(0, wa_ref.shape[0] * rows, one, 0)
    e1 = mm(o_ref[...], wo_ref[...])
    for r in range(rows):
        e1_ref[pl.ds(r * own, own), :] = xw_ref[r, pl.ds(HALO, own), :].astype(F32) + e1[r * own : (r + 1) * own]


def enc_feed(is_enc_ref, e1_ref, gain_ref, w1_ref, w2_ref, n2_ref, u_ref, gp_ref, e2_ref, mem_ref):
    @pl.when(is_enc_ref[0] > 0)
    def _():
        n2_ref[...] = norm(e1_ref[...], gain_ref[pl.ds(1, 1), :]).astype(BF16)
        e2_ref[...] = e1_ref[...]

        def one(t, _):
            u, gp = gelu_parts(mm(n2_ref[...], w1_ref[t]))
            u = u.astype(BF16)
            u_ref[t] = u
            gp_ref[t] = gp.astype(BF16)
            e2_ref[...] += mm(u, w2_ref[t])
            return 0

        lax.fori_loop(0, w1_ref.shape[0], one, 0)
        mem_ref[...] = norm(e2_ref[...], gain_ref[pl.ds(2, 1), :]).astype(BF16)


def dec_middle(
    is_enc_ref, memw_ref, sq_ref, sk_ref, d1_ref, gain_ref, cot_ref, c0_ref, c1_ref, w1_ref, w2_ref,
    out_ref, dw1_ref, dw2_ref, dc0_ref, dc1_ref, dmem_ref, g1_ref, dgain_ref,
    c_ref, q_ref, k_ref, v_ref, p_ref, oc_ref, d2_ref, n3_ref, dn_ref, do_ref, dkv_ref, bias_ref,
):
    @pl.when(is_enc_ref[0] == 0)
    def _():
        rows, win, width = memw_ref.shape
        own = sq_ref.shape[1]
        pairs = c0_ref.shape[0]
        hw = q_ref.shape[-1]
        for r in range(rows):
            bias_ref[r] = jnp.where(sq_ref[r] == sk_ref[r], 0.0, MASKED)
        c_ref[...] = norm(d1_ref[...], gain_ref[pl.ds(1, 1), :]).astype(BF16)

        def project(t, _):
            q = mm(c_ref[...], c1_ref[t, :, :hw]).astype(BF16) * jnp.asarray(DH**-0.5, BF16)
            for r in range(rows):
                q_ref[t, r] = q[r * own : (r + 1) * own]
                kv = mm(memw_ref[r], c0_ref[t])
                k_ref[t, r] = kv[:, :hw].astype(BF16)
                v_ref[t, r] = kv[:, hw:].astype(BF16)
            return 0

        lax.fori_loop(0, pairs, project, 0)
        d2_ref[...] = d1_ref[...]

        def at(t, r):
            return pl.ds(pl.multiple_of(r * own, own), own), pl.ds(pl.multiple_of(t * hw, hw), hw)

        def one(i, _):
            t, r = i // rows, i % rows

            def keep(h, pb):
                p_ref[t, r, h] = pb

            o2 = attend(q_ref[t, r], k_ref[t, r], v_ref[t, r], bias_ref[r], keep).astype(BF16)
            oc_ref[at(t, r)] = o2
            rs = pl.ds(pl.multiple_of(r * own, own), own)
            d2_ref[rs, :] += mm_nt(o2, c1_ref[t, :, hw:])
            return 0

        lax.fori_loop(0, pairs * rows, one, 0)
        n3_ref[...] = norm(d2_ref[...], gain_ref[pl.ds(2, 1), :]).astype(BF16)
        out_ref[...] = d2_ref[...]
        dn_ref[...] = jnp.zeros_like(dn_ref)

        def feed(t, _):
            u, gp = gelu_parts(mm(n3_ref[...], w1_ref[t]))
            u = u.astype(BF16)
            out_ref[...] += mm(u, w2_ref[t])
            dh = (mm_nt(cot_ref[...], w2_ref[t]) * gp).astype(BF16)
            dw2_ref[t] = mm_tn(u, cot_ref[...]).astype(BF16)
            dw1_ref[t] = mm_tn(n3_ref[...], dh).astype(BF16)
            dn_ref[...] += mm_nt(dh, w1_ref[t])
            return 0

        lax.fori_loop(0, w1_ref.shape[0], feed, 0)
        dx, dg = norm_back(d2_ref[...], gain_ref[pl.ds(2, 1), :], dn_ref[...])
        dgain_ref[pl.ds(2, 1), :] = dg
        g2 = cot_ref[...].astype(F32) + dx
        g1_ref[...] = g2
        gb = g2.astype(BF16)
        do_ref[...] = jnp.zeros_like(do_ref)
        dn_ref[...] = jnp.zeros_like(dn_ref)

        def out_back(t, _):
            lanes = pl.ds(pl.multiple_of(t * hw, hw), hw)
            dc1_ref[t, :, hw:] = mm_tn(gb, oc_ref[:, lanes]).astype(BF16)
            do_ref[:, lanes] = mm(gb, c1_ref[t, :, hw:]).astype(BF16)
            return 0

        lax.fori_loop(0, pairs, out_back, 0)

        def back(i, _):
            t, r = i // rows, i % rows
            dq, dk, dv = attend_back(q_ref[t, r], k_ref[t, r], v_ref[t, r], do_ref[at(t, r)], lambda h: p_ref[t, r, h])
            q_ref[t, r] = dq.astype(BF16)
            rs = pl.ds(pl.multiple_of(r * win, win), win)
            dkv_ref[t, rs, :hw] = dk.astype(BF16)
            dkv_ref[t, rs, hw:] = dv.astype(BF16)
            return 0

        lax.fori_loop(0, pairs * rows, back, 0)
        dmem_ref[...] = jnp.zeros_like(dmem_ref)
        memw = memw_ref[...].reshape(rows * win, width)

        def maps_back(t, _):
            dq = q_ref[t].reshape(rows * own, hw)
            dc1_ref[t, :, :hw] = mm_tn(c_ref[...], dq).astype(BF16)
            dn_ref[...] += mm_nt(dq, c1_ref[t, :, :hw])
            dc0_ref[t] = mm_tn(memw, dkv_ref[t]).astype(BF16)
            dmem_ref[...] += mm_nt(dkv_ref[t], c0_ref[t])
            return 0

        lax.fori_loop(0, pairs, maps_back, 0)
        dx, dg = norm_back(d1_ref[...], gain_ref[pl.ds(1, 1), :], dn_ref[...])
        dgain_ref[pl.ds(1, 1), :] = dg
        dgain_ref[pl.ds(0, 1), :] = jnp.zeros_like(dg)
        g1_ref[...] += dx


def enc_feed_back(is_enc_ref, dmem_ref, e2_ref, e1_ref, n2_ref, u_ref, gp_ref, gain_ref, w1_ref, w2_ref, dw1_ref, dw2_ref, g_ref, dgain_ref, dn_ref):
    @pl.when(is_enc_ref[0] > 0)
    def _():
        dx, dg = norm_back(e2_ref[...], gain_ref[pl.ds(2, 1), :], dmem_ref[...].astype(F32))
        dgain_ref[pl.ds(2, 1), :] = dg
        g_ref[...] = dx
        gb = dx.astype(BF16)
        dn_ref[...] = jnp.zeros_like(dn_ref)

        def feed(t, _):
            dh = (mm_nt(gb, w2_ref[t]) * gp_ref[t].astype(F32)).astype(BF16)
            dw2_ref[t] = mm_tn(u_ref[t], gb).astype(BF16)
            dw1_ref[t] = mm_tn(n2_ref[...], dh).astype(BF16)
            dn_ref[...] += mm_nt(dh, w1_ref[t])
            return 0

        lax.fori_loop(0, w1_ref.shape[0], feed, 0)
        dx, dg = norm_back(e1_ref[...], gain_ref[pl.ds(1, 1), :], dn_ref[...])
        dgain_ref[pl.ds(1, 1), :] = dg
        dgain_ref[pl.ds(0, 1), :] = jnp.zeros_like(dg)
        g_ref[...] += dx


def self_backward(g_ref, nw_ref, q_ref, k_ref, v_ref, p_ref, o_ref, wa_ref, wo_ref, da_ref, do_out_ref, dnw_ref, do_ref, dqkv_ref):
    pairs, rows, own, hw = q_ref.shape
    win = k_ref.shape[2]
    gb = g_ref[...].astype(BF16)
    do_out_ref[...] = mm_tn(o_ref[...], gb).astype(BF16)
    do_ref[...] = mm_nt(gb, wo_ref[...]).astype(BF16)
    dnw_ref[...] = jnp.zeros_like(dnw_ref)

    def back(i, _):
        t, r = i // rows, i % rows
        do2 = do_ref[pl.ds(pl.multiple_of(r * own, own), own), pl.ds(pl.multiple_of(t * hw, hw), hw)]
        dq, dk, dv = attend_back(q_ref[t, r], k_ref[t, r], v_ref[t, r], do2, lambda h: p_ref[t, r, h])
        base = pl.multiple_of(r * win, HALO)
        dqkv_ref[t, pl.ds(base, HALO), :hw] = jnp.zeros((HALO, hw), BF16)
        dqkv_ref[t, pl.ds(base + HALO + own, HALO), :hw] = jnp.zeros((HALO, hw), BF16)
        dqkv_ref[t, pl.ds(base + HALO, own), :hw] = dq.astype(BF16)
        dqkv_ref[t, pl.ds(base, win), hw : 2 * hw] = dk.astype(BF16)
        dqkv_ref[t, pl.ds(base, win), 2 * hw :] = dv.astype(BF16)
        return 0

    lax.fori_loop(0, pairs * rows, back, 0)

    def maps_back(t, _):
        da_ref[t] = mm_tn(nw_ref[...], dqkv_ref[t]).astype(BF16)
        dnw_ref[...] += mm_nt(dqkv_ref[t], wa_ref[t])
        return 0

    lax.fori_loop(0, pairs, maps_back, 0)


def call(kernel, name, outs, scratch, args, scalars=1):
    return pl.pallas_call(
        kernel,
        name=name,
        out_shape=[jax.ShapeDtypeStruct(*o) for o in outs],
        in_specs=[SMEM] * scalars + [VMEM] * (len(args) - scalars),
        out_specs=[VMEM] * len(outs),
        scratch_shapes=[pltpu.VMEM(*s) for s in scratch],
        compiler_params=pltpu.CompilerParams(vmem_limit_bytes=60 << 20),
    )(*args)


def shifted(rows, by):
    n = lax.axis_size("tensor")
    return lax.ppermute(rows, "tensor", [(i, i + by) for i in range(n) if 0 <= i + by < n])


def body(embeds, segments, cotangent, norm_gains, attn_in, attn_out, cross_proj, ffn_in, ffn_out):
    pipe = lax.axis_index("pipe")
    me = lax.axis_index("tensor")
    shards = lax.axis_size("tensor")
    is_enc = pipe == 0
    enc_flag = jnp.where(is_enc, 1, 0).astype(jnp.int32).reshape(1)
    rows, own, width = embeds.shape[1:]
    slots = segments.shape[2]
    hw = attn_in.shape[3]
    fw = ffn_in.shape[2]
    win = own + 2 * HALO
    cwin = 2 * own + 2 * HALO
    tokens = rows * own

    gather = functools.partial(lax.all_gather, axis_name="tensor", axis=0)
    wa = gather(attn_in[0].reshape(width, 3 * hw))
    wo = gather(attn_out[0], tiled=True)
    w1 = gather(ffn_in[0])
    w2 = gather(ffn_out[0])
    cx = cross_proj[0].reshape(width, 2 * hw)
    c1 = gather(cx)
    c0 = gather(lax.ppermute(cx, "pipe", [(0, 1), (1, 0)]))
    gains = norm_gains[0]

    x = embeds[0]
    xw = jnp.concatenate([shifted(x[:, own - HALO :], 1), x, shifted(x[:, :HALO], -1)], axis=1)
    seg_self = jnp.where(is_enc, segments[0], segments[1])
    padded = jnp.pad(seg_self, ((0, 0), (HALO, HALO)), constant_values=-2)
    start = me * own
    sq = lax.dynamic_slice(seg_self, (0, start), (rows, own))[:, :, None]
    sk = lax.dynamic_slice(padded, (0, start), (rows, win))[:, None, :]

    nw, q, k, v, p, o, e1 = call(
        self_forward,
        "self_forward",
        [
            ((rows * win, width), BF16),
            ((shards, rows, own, hw), BF16),
            ((shards, rows, win, hw), BF16),
            ((shards, rows, win, hw), BF16),
            ((shards, rows, 2, own, win), BF16),
            ((tokens, width), BF16),
            ((tokens, width), F32),
        ],
        [((rows, own, win), F32)],
        (enc_flag, xw, sq, sk, gains, wa, wo),
    )
    n2, u, gp, e2, mem = call(
        enc_feed,
        "enc_feed",
        [
            ((tokens, width), BF16),
            ((shards, tokens, fw), BF16),
            ((shards, tokens, fw), BF16),
            ((tokens, width), F32),
            ((tokens, width), BF16),
        ],
        [],
        (enc_flag, e1, gains, w1, w2),
    )
    mem = mem.reshape(rows, own, width)
    moved = lax.ppermute(mem, "pipe", [(0, 1), (1, 0)])
    all_mem = lax.all_gather(moved, "tensor", axis=1, tiled=True)
    cstart = jnp.minimum(me * (own - HALO), slots - cwin)
    memw = lax.dynamic_slice(all_mem, (0, cstart, 0), (rows, cwin, width))
    csk = lax.dynamic_slice(segments[0], (0, cstart), (rows, cwin))[:, None, :]
    csq = lax.dynamic_slice(segments[1], (0, start), (rows, own))[:, :, None]
    dec_out, dw1d, dw2d, dc0, dc1, dmemw, g1, dgain_d = call(
        dec_middle,
        "dec_middle",
        [
            ((tokens, width), F32),
            ((shards, width, fw), BF16),
            ((shards, fw, width), BF16),
            ((shards, width, 2 * hw), BF16),
            ((shards, width, 2 * hw), BF16),
            ((rows * cwin, width), F32),
            ((tokens, width), F32),
            ((3, width), F32),
        ],
        [
            ((tokens, width), BF16),
            ((shards, rows, own, hw), BF16),
            ((shards, rows, cwin, hw), BF16),
            ((shards, rows, cwin, hw), BF16),
            ((shards, rows, 2, own, cwin), BF16),
            ((tokens, width), BF16),
            ((tokens, width), F32),
            ((tokens, width), BF16),
            ((tokens, width), F32),
            ((tokens, width), BF16),
            ((shards, rows * cwin, 2 * hw), BF16),
            ((rows, own, cwin), F32),
        ],
        (enc_flag, memw, csq, csk, e1, gains, cotangent.reshape(tokens, width), c0, c1, w1, w2),
    )
    dmem = jnp.zeros((rows, slots, width), BF16)
    dmem = lax.dynamic_update_slice(dmem, dmemw.reshape(rows, cwin, width).astype(BF16), (0, cstart, 0))
    dmem = lax.psum_scatter(dmem, "tensor", scatter_dimension=1, tiled=True)
    dmem = lax.ppermute(dmem, "pipe", [(0, 1), (1, 0)]).reshape(tokens, width)
    dw1e, dw2e, ge, dgain_e = call(
        enc_feed_back,
        "enc_feed_back",
        [
            ((shards, width, fw), BF16),
            ((shards, fw, width), BF16),
            ((tokens, width), F32),
            ((3, width), F32),
        ],
        [((tokens, width), F32)],
        (enc_flag, dmem, e2, e1, n2, u, gp, gains, w1, w2),
    )
    g = jnp.where(is_enc, ge, g1)
    dw1 = jnp.where(is_enc, dw1e, dw1d)
    dw2 = jnp.where(is_enc, dw2e, dw2d)
    dgain = jnp.where(is_enc, dgain_e, dgain_d)
    da, dwo, dnw = call(
        self_backward,
        "self_backward",
        [
            ((shards, width, 3 * hw), BF16),
            ((width, width), BF16),
            ((rows * win, width), F32),
        ],
        [
            ((tokens, width), BF16),
            ((shards, rows * win, 3 * hw), BF16),
        ],
        (g, nw, q, k, v, p, o, wa, wo),
        scalars=0,
    )
    dnw = dnw.reshape(rows, win, width)
    from_right = shifted(dnw[:, :HALO].astype(BF16), -1).astype(F32)
    from_left = shifted(dnw[:, own + HALO :].astype(BF16), 1).astype(F32)
    dn = dnw[:, HALO : HALO + own]
    dn = dn.at[:, own - HALO :].add(from_right).at[:, :HALO].add(from_left).reshape(tokens, width)
    dx, dg0 = norm_back(x.reshape(tokens, width).astype(F32), gains[0:1], dn)
    grad_x = (g + dx).astype(BF16).reshape(rows, own, width)
    dgain = dgain.at[0:1].add(dg0)
    dgain = lax.psum(dgain, ("tensor", "dp"))
    share = width // lax.axis_size("dp")
    dgain = lax.dynamic_slice(dgain, (0, lax.axis_index("dp") * share), (3, share))

    section = jnp.where(is_enc, mem, dec_out.reshape(rows, own, width).astype(BF16))

    def scattered(v, dim):
        v = lax.psum_scatter(v, "tensor", scatter_dimension=0, tiled=False)
        return lax.psum_scatter(v, "dp", scatter_dimension=dim, tiled=True).astype(F32)

    da = scattered(da, 0).reshape(-1, 3, hw)
    dwo = scattered(dwo.reshape(shards, hw, width), 1)
    dw1 = scattered(dw1, 0)
    dw2 = scattered(dw2, 1)
    dc0 = scattered(dc0, 0)
    dc1 = scattered(dc1, 0)
    dc0 = lax.ppermute(dc0, "pipe", [(0, 1), (1, 0)])
    dc = jnp.where(is_enc, dc0, dc1).reshape(-1, 2, hw)
    return (section[None], grad_x[None], dgain[None], da[None], dwo[None], dc[None], dw1[None], dw2[None])


def solution(mesh):
    return jax.shard_map(
        body,
        mesh=mesh,
        in_specs=(
            P("pipe", "dp", "tensor", None),
            P(None, "dp", None),
            P("dp", "tensor", None),
            P("pipe", None, None),
            P("pipe", None, None, "tensor"),
            P("pipe", "tensor", None),
            P("pipe", None, None, "tensor"),
            P("pipe", None, "tensor"),
            P("pipe", "tensor", None),
        ),
        out_specs=(
            P("pipe", "dp", "tensor", None),
            P("pipe", "dp", "tensor", None),
            P("pipe", None, "dp"),
            P("pipe", "dp", None, "tensor"),
            P("pipe", "tensor", "dp"),
            P("pipe", "dp", None, "tensor"),
            P("pipe", "dp", "tensor"),
            P("pipe", "tensor", "dp"),
        ),
        check_vma=False,
    )
```

time: 1570 us -> 578 us (0.37); the launches traced: 1550 us -> 577 us
  waiting for transfers between devices: 968 us -> 382 us
  matrix products: 199 us -> 0 us
  other arithmetic: 162 us -> 22.7 us
  local copies, waits for them, and re-layouts: 141 us -> 32.8 us
  Pallas kernels: 0 us -> 65.3 us
  blocking collectives: 17.6 us -> 47.2 us
  loops' own time: 27.3 us -> 0 us
    reduce_scatter x24 -> x11, waiting for transfers between devices: 581 us -> 225 us  [the longest x4 77.6 us: scattered(): lax.psum_scatter(v, 'dp', scatter_dimension=dim, tiled=True).astype(F32)]
    all_gather x18 -> x6, waiting for transfers between devices: 241 us -> 82.3 us  [the longest x1 24.2 us: body(): w2 = gather(ffn_out[0])]
    dot_general x57 -> x0, matrix products: 149 us -> none  [the longest x6 25.5 us: attend_forward(): jnp.einsum('hqk,khd->qhd', rounded_probs, value_heads, preferred_element_...]
    while x66 -> x0, waiting for transfers between devices: 143 us -> none
    pallas_call x0 -> x5, Pallas kernels: none -> 65.3 us  [call(): pl.pallas_call(kernel, name=name, out_shape=[jax.ShapeDtypeStruct(*o) for...]
    while x265 -> x0, local copies, waits for them, and re-layouts: 55.6 us -> none
    convert_element_type x36 -> x3, other arithmetic: 54.4 us -> 5.01 us  [the longest x1 2.96 us: body(): dmemw.reshape(rows, cwin, width).astype(BF16)]
    reduce_sum x36 -> x3, other arithmetic: 46.6 us -> 1 us  [the longest x1 0.54 us: norm_back(): jnp.sum(dn * xhat, axis=0, keepdims=True)]
  transfers between devices with their start and end apart: 60 -> 27, of which waited for: 51 -> 20; matrix products, arithmetic and copies ran while one was open for 15% -> 6% of each run, Pallas kernels for 0% -> 8%
where the time goes in v1:
time: 578 us; the launch traced here: 577 us
  waiting for transfers between devices  382 us (66%)
  Pallas kernels  65.3 us (11%)
  blocking collectives  47.2 us (8%)
  local copies, waits for them, and re-layouts  32.8 us (6%)
  other arithmetic  22.7 us (4%)
  between operations  14.4 us (2%)
  starting transfers between devices  12.1 us (2%)
    reduce_scatter x4, waiting for transfers between devices, scattered(): lax.psum_scatter(v, 'dp', scatter_dimension=dim, tiled=True).astype(F32)  77.6 us
    reduce_scatter x6, waiting for transfers between devices, scattered(): v = lax.psum_scatter(v, 'tensor', scatter_dimension=0, tiled=False)  75.5 us
    reduce_scatter x1, waiting for transfers between devices, body(): dmem = lax.psum_scatter(dmem, 'tensor', scatter_dimension=1, tiled=True)  71.8 us
    pallas_call x5, Pallas kernels, call(): pl.pallas_call(kernel, name=name, out_shape=[jax.ShapeDtypeStruct(*o) for...  65.3 us
    unnamed x21, waiting for transfers between devices  41.2 us
    psum x1, blocking collectives, body(): dgain = lax.psum(dgain, ('tensor', 'dp'))  33.6 us
    all_gather x1, waiting for transfers between devices, body(): w2 = gather(ffn_out[0])  24.2 us
    all_gather x1, waiting for transfers between devices, body(): c0 = gather(lax.ppermute(cx, 'pipe', [(0, 1), (1, 0)]))  18.7 us
  transfers between devices with their start and end apart: 27, of which 20 were waited for; matrix products, arithmetic and copies ran while one was open for 6% of the time, Pallas kernels for 8%

profile of v1, /device:TPU:0, one launch (start us, length us, event | category | flops | bytes accessed | tf_op | source)
XLA Modules:
  0.0 576.9 jit_solution(12828093594441786552)
XLA Ops:
  7.3 1.2 copy.25
  11.0 2.4 collective-permute-start
  13.4 1.3 collective-permute-start.1
  16.9 13.6 %all-gather = bf16[1,512,512]{2,1,0:T(8,128)(2,1)} all-gather(bf16[1,128,512]{2,1,0:T(8,128)(2,1)S(1)} %copy-done.12), channel_id=2, replica_groups=mesh['pipe'=2,'dp'=4,'tensor'=4] {'tensor'}, dimensions={1}, use_global_device_ids=true | all-gather | bytes 655360 | tf_op jit(solution)/shard_map/all_gather | solution.py:347
  31.4 4.0 all-gather.9.cloned.1.call-done.wa_ref
  35.4 15.2 %self_forward.1 = (bf16[768,512]{1,0:T(8,128)(2,1)}, bf16[4,2,256,128]{3,2,1,0:T(8,128)(2,1)}, bf16[4,2,384,128]{3,2,1,0:T(8,128)(2,1)}, bf16[4,2,384,128]{3,2,1...) custom-call(s32[1]{0:T(128)} %bitcast.4.is_enc_ref, ...), custom_call_target="tpu_custom_call" | custom-call | tf_op jit(solution)/shard_map/self_forward/pallas_call | solution.py:315
  50.6 9.1 %all-gather.11.cloned.1.call-done.w1_ref = bf16[4,512,512]{2,1,0:T(8,128)(2,1)} async-done(((bf16[1,512,512]{2,1,0:T(8,128)(2,1)}), bf16[4,512,512]{2,1,0:T(8,128)(2,1)}) %all-gather.11.cloned.1.call-update) | async-done | bytes 2097168 | tf_op jit(solution)/shard_map/all_gather | solution.py:348
  59.7 24.2 %all-gather.13.cloned.1.call-done.w2_ref = bf16[4,512,512]{2,1,0:T(8,128)(2,1)} async-done(((bf16[1,512,512]{2,1,0:T(8,128)(2,1)}), bf16[4,512,512]{2,1,0:T(8,128)(2,1)}) %all-gather.13.cloned.1.call-update) | async-done | bytes 2097168 | tf_op jit(solution)/shard_map/all_gather | solution.py:349
  83.9 10.5 %enc_feed.1 = (bf16[512,512]{1,0:T(8,128)(2,1)}, bf16[4,512,512]{2,1,0:T(8,128)(2,1)}, bf16[4,512,512]{2,1,0:T(8,128)(2,1)}, f32[512,512]{1,0:T(8,128)}, bf16[512,512]{1,0:T(8,128)(2,1)}) custom-call(s32[1]{0:T(128)} %bitcast.4.is_enc_ref, f32[512,512]{1,0:T(8,128)} %get-tuple-element.71.e1_ref.d1_ref, f32[3,512]{1,0:T(4,128)} %bitcast.109, ...), custom_call_target="tpu_custom_call" | custom-call | tf_op jit(solution)/shard_map/enc_feed/pallas_call | solution.py:315
  94.4 14.3 %collective-permute-done.2 = bf16[2,256,512]{2,1,0:T(8,128)(2,1)S(1)} collective-permute-done((bf16[2,256,512]{2,1,0:T(8,128)(2,1)}, bf16[2,256,512]{2,1,0:T(8,128)(2,1)S(1)}, u32[]{:S(2)}, u32[]{:S(2)}) %collective-permute-start.2) | collective-permute-done | bytes 524320 | tf_op jit(solution)/shard_map/ppermute | solution.py:392
  110.8 7.3 %collective-permute-done.3 = bf16[512,256]{1,0:T(8,128)(2,1)S(1)} collective-permute-done((bf16[512,256]{1,0:T(8,128)(2,1)S(1)}, bf16[512,256]{1,0:T(8,128)(2,1)S(1)}, u32[]{:S(2)}, u32[]{:S(2)}) %collective-permute-start.3) | collective-permute-done | bytes 262176 | tf_op jit(solution)/shard_map/ppermute | solution.py:352
  120.5 10.8 %all-gather.15.cloned.1.call-done = bf16[2,1024,512]{2,1,0:T(8,128)(2,1)} async-done(((bf16[2,256,512]{2,1,0:T(8,128)(2,1)}), bf16[2,1024,512]{2,1,0:T(8,128)(2,1)}) %all-gather.15.cloned.1.call-update) | async-done | bytes 2097168 | tf_op jit(solution)/shard_map/all_gather | solution.py:393
  131.3 2.7 constant_dynamic-slice_fusion.2.memw_ref
  134.0 15.5 %all-gather.17.cloned.1.call-done.c1_ref = bf16[4,512,256]{2,1,0:T(8,128)(2,1)} async-done(((bf16[1,512,256]{2,1,0:T(8,128)(2,1)}), bf16[4,512,256]{2,1,0:T(8,128)(2,1)}) %all-gather.17.cloned.1.call-update) | async-done | bytes 1048592 | tf_op jit(solution)/shard_map/all_gather | solution.py:351
  149.5 18.7 %all-gather.19.cloned.1.call-done = bf16[2048,256]{1,0:T(8,128)(2,1)} async-done(((bf16[512,256]{1,0:T(8,128)(2,1)}), bf16[2048,256]{1,0:T(8,128)(2,1)}) %all-gather.19.cloned.1.call-update) | async-done | bytes 1048592 | tf_op jit(solution)/shard_map/all_gather | solution.py:352
  168.2 7.9 %dec_middle.1 = (f32[512,512]{1,0:T(8,128)}, bf16[4,512,512]{2,1,0:T(8,128)(2,1)}, bf16[4,512,512]{2,1,0:T(8,128)(2,1)}, bf16[4,512,256]{2,1,0:T(8,128)(2,1)}, b...) custom-call(s32[1]{0:T(128)} %bitcast.4.is_enc_ref, ...), custom_call_target="tpu_custom_call" | custom-call | tf_op jit(solution)/shard_map/dec_middle/pallas_call | solution.py:315
  176.1 3.0 convert_element_type.53
  179.2 9.1 %dynamic_update_slice.3 = bf16[2,1024,512]{2,1,0:T(8,128)(2,1)S(1)} dynamic-update-slice(bf16[2,1024,512]{2,1,0:T(8,128)(2,1)S(1)} %broadcast_in_dim.46, bf16[2,640,512]{2,1,0:T(8,128)(2,1)} %bitcast.87, s32[]{:T(128)} %constant.111.clone.1, s32[]{:T(128)S(6)} %select_n.89, s32[]{:T(128)} %constant.111.clone.1) | dynamic-update-slice | bytes 2621444 | tf_op jit(solution)/shard_map/dynamic_update_slice | solution.py:428
  188.3 1.3 copy-done.2
  191.2 71.8 %reduce-scatter.18.cloned.1.call-done = bf16[2,256,512]{2,1,0:T(8,128)(2,1)} async-done(((bf16[2,1024,512]{2,1,0:T(8,128)(2,1)}), bf16[2,256,512]{2,1,0:T(8,128)(2,1)}) %reduce-scatter.18.cloned.1.call-update) | async-done | bytes 524304 | tf_op jit(solution)/shard_map/reduce_scatter | solution.py:429
  263.1 1.5 collective-permute-start.4
  264.5 12.4 %collective-permute-done.4 = bf16[2,256,512]{2,1,0:T(8,128)(2,1)S(1)} collective-permute-done((bf16[2,256,512]{2,1,0:T(8,128)(2,1)}, bf16[2,256,512]{2,1,0:T(8,128)(2,1)S(1)}, u32[]{:S(2)}, u32[]{:S(2)}) %collective-permute-start.4) | collective-permute-done | bytes 524320 | tf_op jit(solution)/shard_map/ppermute | solution.py:430
  277.7 13.7 %enc_feed_back.1 = (bf16[4,512,512]{2,1,0:T(8,128)(2,1)}, bf16[4,512,512]{2,1,0:T(8,128)(2,1)}, f32[512,512]{1,0:T(8,128)}, f32[3,512]{1,0:T(4,128)}) custom-call(s32[1]{0:T(128)} %bitcast.4.is_enc_ref, bf16[512,512]{1,0:T(8,128)(2,1)} %bitcast.97, f32[512,512]{1,0:T(8,128)} %get-tuple-element.75.e2_ref, f32[512,512]{1,0:T(8,128)} %get-tuple-element.71.e1_ref.d1_ref, ...), custom_call_target="tpu_custom_call" | custom-call | tf_op jit(solution)/shard_map/enc_feed_back/pallas_call | solution.py:315
  291.5 2.4 broadcast_select_fusion.2.g_ref
  293.8 18.0 %self_backward.1 = (bf16[4,512,384]{2,1,0:T(8,128)(2,1)}, bf16[512,512]{1,0:T(8,128)(2,1)}, f32[768,512]{1,0:T(8,128)}) custom-call(f32[512,512]{1,0:T(8,128)} %broadcast_select_fusion.2.g_ref, bf16[768,512]{1,0:T(8,128)(2,1)} %get-tuple-element.81.nw_ref, bf16[4,2,256,128]{3,2,1,0:T(8,128)(2,1)} %get-tuple-element.82.q_ref, ...), custom_call_target="tpu_custom_call" | custom-call | tf_op jit(solution)/shard_map/self_backward/pallas_call | solution.py:315
  313.2 4.9 reduce-scatter.30.cloned.1.call-done
  318.2 3.2 broadcast_select_fusion
  321.4 1.5 copy-done.4
  323.0 3.2 broadcast_select_fusion.1
  326.4 15.9 %reduce-scatter.24.cloned.1.call-done = bf16[1,128,512]{2,1,0:T(8,128)(2,1)} async-done(((bf16[4,128,512]{2,1,0:T(8,128)(2,1)}), bf16[1,128,512]{2,1,0:T(8,128)(2,1)}) %reduce-scatter.24.cloned.1.call-update) | async-done | bytes 131088 | tf_op jit(solution)/shard_map/reduce_scatter | solution.py:477
  342.3 1.8 copy.31
  344.5 28.6 %reduce-scatter.20.cloned.1.call-done = bf16[1,512,384]{2,1,0:T(8,128)(2,1)} async-done(((bf16[4,512,384]{2,1,0:T(8,128)(2,1)}), bf16[1,512,384]{2,1,0:T(8,128)(2,1)}) %reduce-scatter.20.cloned.1.call-update) | async-done | bytes 393232 | tf_op jit(solution)/shard_map/reduce_scatter | solution.py:477
  373.2 21.7 %reduce-scatter.28.cloned.1.call-done = bf16[128,256]{1,0:T(8,128)(2,1)} async-done(((bf16[512,256]{1,0:T(8,128)(2,1)}), bf16[128,256]{1,0:T(8,128)(2,1)}) %reduce-scatter.28.cloned.1.call-update) | async-done | bytes 65552 | tf_op jit(solution)/shard_map/reduce_scatter | solution.py:478
  395.8 1.5 collective-permute-start.7
  397.3 1.9 convert_select_fusion
  399.2 15.9 %reduce-scatter.32.cloned.1.call-done = bf16[128,256]{1,0:T(8,128)(2,1)} async-done(((bf16[512,256]{1,0:T(8,128)(2,1)}), bf16[128,256]{1,0:T(8,128)(2,1)}) %reduce-scatter.32.cloned.1.call-update) | async-done | bytes 65552 | tf_op jit(solution)/shard_map/reduce_scatter | solution.py:478
  416.9 1.3 collective-permute-start.5
  418.2 3.0 collective-permute-start.6
  421.3 26.1 %reduce-scatter.38.cloned.1.call-done = bf16[1,512,512]{2,1,0:T(8,128)(2,1)} async-done(((bf16[4,512,512]{2,1,0:T(8,128)(2,1)}), bf16[1,512,512]{2,1,0:T(8,128)(2,1)}) %reduce-scatter.38.cloned.1.call-update) | async-done | bytes 524304 | tf_op jit(solution)/shard_map/reduce_scatter | solution.py:477
  447.4 2.0 copy.33
  449.5 1.0 fusion.8
  451.3 33.6 %psum.7 = f32[3,512]{1,0:T(4,128)S(1)} all-reduce(f32[3,512]{1,0:T(4,128)S(1)} %scatter-add.14), channel_id=1, replica_groups=mesh['pipe'=2,'dp'=4,'tensor'=4] {'tensor','dp'}, use_global_device_ids=true, to_apply=%region_6.7 | all-reduce | flops 1536 | bytes 12288 | tf_op jit(solution)/shard_map/psum | solution.py:470
  485.5 1.2 fusion.5
  486.7 16.6 %reduce-scatter.40.cloned.1.call-done = bf16[128,128]{1,0:T(8,128)(2,1)} async-done(((bf16[512,128]{1,0:T(8,128)(2,1)}), bf16[128,128]{1,0:T(8,128)(2,1)}) %reduce-scatter.40.cloned.1.call-update) | async-done | bytes 32784
  504.9 19.4 %reduce-scatter.22.cloned.1.call-done = bf16[128,384]{1,0:T(8,128)(2,1)} async-done(((bf16[512,384]{1,0:T(8,128)(2,1)}), bf16[128,384]{1,0:T(8,128)(2,1)}) %reduce-scatter.22.cloned.1.call-update) | async-done | bytes 98320 | tf_op jit(solution)/shard_map/reduce_scatter | solution.py:478
  526.1 20.4 %reduce-scatter.42.cloned.1.call-done = bf16[128,512]{1,0:T(8,128)(2,1)} async-done(((bf16[512,512]{1,0:T(8,128)(2,1)}), bf16[128,512]{1,0:T(8,128)(2,1)}) %reduce-scatter.42.cloned.1.call-update) | async-done | bytes 131088
  548.2 20.6 %reduce-scatter.36.cloned.1.call-done = bf16[128,512]{1,0:T(8,128)(2,1)} async-done(((bf16[512,512]{1,0:T(8,128)(2,1)}), bf16[128,512]{1,0:T(8,128)(2,1)}) %reduce-scatter.36.cloned.1.call-update) | async-done | bytes 131088 | tf_op jit(solution)/shard_map/reduce_scatter | solution.py:478
  568.8 1.6 bitcast_convert_fusion.1
  (124 shorter events, 23.6 us)
Async XLA Ops:
  7.2 3.8 copy-start
  7.2 7.5 %copy-start.13 = (s32[2,2,1024]{2,1,0:T(2,128)S(1)}, s32[2,2,1024]{2,1,0:T(2,128)}, u32[]{:S(2)}) copy-start(s32[2,2,1024]{2,1,0:T(2,128)} %param.16) | copy-start | bytes 49156
  7.2 9.1 %copy-start.14 = (f32[1,3,512]{2,0,1:T(1,128)S(1)}, f32[1,3,512]{2,0,1:T(1,128)}, u32[]{:S(2)}) copy-start(f32[1,3,512]{2,0,1:T(1,128)} %param.18) | copy-start | bytes 18436
  7.2 9.7 %copy-start.12 = (bf16[1,128,512]{2,1,0:T(8,128)(2,1)S(1)}, bf16[1,128,512]{2,1,0:T(8,128)(2,1)}, u32[]{:S(2)}) copy-start(bf16[1,128,512]{2,1,0:T(8,128)(2,1)} %param.20) | copy-start | bytes 393220
  7.2 28.2 %all-gather.9.cloned.1.call-start = ((), (), s32[]{:S(2)}) async-start(), calls=%async_computation.13 | async-start | bytes 1966080 | tf_op jit(solution)/shard_map/all_gather | solution.py:346
  9.4 50.3 %all-gather.11.cloned.1.call-start = ((), (), s32[]{:S(2)}) async-start(), calls=%async_computation.14 | async-start | bytes 2621440 | tf_op jit(solution)/shard_map/all_gather | solution.py:348
  10.2 73.7 %all-gather.13.cloned.1.call-start = ((), (), s32[]{:S(2)}) async-start(), calls=%async_computation.15 | async-start | bytes 2621440 | tf_op jit(solution)/shard_map/all_gather | solution.py:349
  10.9 120.4 %all-gather.15.cloned.1.call-start = ((), (), s32[]{:S(2)}) async-start(), calls=%async_computation.16 | async-start | bytes 2621440 | tf_op jit(solution)/shard_map/all_gather | solution.py:393
  11.0 19.5 %collective-permute-start = (bf16[2,64,512]{2,1,0:T(8,128)(2,1)S(1)}, bf16[2,64,512]{2,1,0:T(8,128)(2,1)S(1)}, u32[]{:S(2)}, u32[]{:S(2)}) collective-permute-start(bf16[2,64,512]{2,1,0:T(8,128)(2,1)S(1)} %get-tuple-element.127), channel_id=1, source_target_pairs={{0,1},{1,2},{2,3},{4,5},{5,6},{6,7},{8,9},{9,10},{10,11},{12,13},{... | collective-permute-start | bytes 393224 | tf_op jit(solution)/shard_map/ppermute | solution.py:328
  13.4 17.1 %collective-permute-start.1 = (bf16[2,64,512]{2,1,0:T(8,128)(2,1)S(1)}, bf16[2,64,512]{2,1,0:T(8,128)(2,1)S(1)}, u32[]{:S(2)}, u32[]{:S(2)}) collective-permute-start(bf16[2,64,512]{2,1,0:T(8,128)(2,1)S(1)} %get-tuple-element.128), channel_id=1, source_target_pairs={{1,0},{2,1},{3,2},{5,4},{6,5},{7,6},{9,8},{10,9},{11,10},{13,12},{... | collective-permute-start | bytes 393224 | tf_op jit(solution)/shard_map/ppermute | solution.py:328
  83.9 25.6 %copy-start.8 = (bf16[1,512,2,128]{3,2,1,0:T(2,128)(2,1)S(1)}, bf16[1,512,2,128]{3,2,1,0:T(2,128)(2,1)}, u32[]{:S(2)}) copy-start(bf16[1,512,2,128]{3,2,1,0:T(2,128)(2,1)} %param.21) | copy-start | bytes 786436
  94.4 14.3 %collective-permute-start.2 = (bf16[2,256,512]{2,1,0:T(8,128)(2,1)}, bf16[2,256,512]{2,1,0:T(8,128)(2,1)S(1)}, u32[]{:S(2)}, u32[]{:S(2)}) collective-permute-start(bf16[2,256,512]{2,1,0:T(8,128)(2,1)} %bitcast.95), channel_id=1, source_target_pairs={{0,16},{16,0},{1,17},{17,1},{2,18},{18,2},{3,19},{19,3},{4,20},{20... | collective-permute-start | bytes 1572872 | tf_op jit(solution)/shard_map/ppermute | solution.py:392
  108.6 0.8 copy-start.10
  109.5 40.0 %all-gather.17.cloned.1.call-start = ((), (), s32[]{:S(2)}) async-start(), calls=%async_computation.17 | async-start | bytes 1310720 | tf_op jit(solution)/shard_map/all_gather | solution.py:351
  110.4 57.8 %all-gather.19.cloned.1.call-start = ((), (), s32[]{:S(2)}) async-start(), calls=%async_computation.29 | async-start | bytes 1310720 | tf_op jit(solution)/shard_map/all_gather | solution.py:352
  110.5 7.7 %collective-permute-start.3 = (bf16[512,256]{1,0:T(8,128)(2,1)S(1)}, bf16[512,256]{1,0:T(8,128)(2,1)S(1)}, u32[]{:S(2)}, u32[]{:S(2)}) collective-permute-start(bf16[512,256]{1,0:T(8,128)(2,1)S(1)} %bitcast.107), channel_id=1, source_target_pairs={{0,16},{16,0},{1,17},{17,1},{2,18},{18,2},{3,19},{19,3},{4,20},{20... | collective-permute-start | bytes 786440 | tf_op jit(solution)/shard_map/ppermute | solution.py:352
  118.2 0.7 copy-start.11
  118.9 144.1 %reduce-scatter.18.cloned.1.call-start = ((), (), s32[]{:S(2)}) async-start(), calls=%async_computation.18 | async-start | bytes 2621440 | tf_op jit(solution)/shard_map/reduce_scatter | solution.py:429
  188.3 1.3 copy-start.2
  189.7 123.0 %reduce-scatter.26.cloned.1.call-start = ((), (), s32[]{:S(2)}) async-start(), calls=%async_computation.22 | async-start | bytes 1310720 | tf_op jit(solution)/shard_map/reduce_scatter | solution.py:477
  190.4 127.7 %reduce-scatter.30.cloned.1.call-start = ((), (), s32[]{:S(2)}) async-start(), calls=%async_computation.24 | async-start | bytes 1310720 | tf_op jit(solution)/shard_map/reduce_scatter | solution.py:477
  191.2 151.1 %reduce-scatter.24.cloned.1.call-start = ((), (), s32[]{:S(2)}) async-start(), calls=%async_computation.21 | async-start | bytes 655360 | tf_op jit(solution)/shard_map/reduce_scatter | solution.py:477
  263.1 13.9 %collective-permute-start.4 = (bf16[2,256,512]{2,1,0:T(8,128)(2,1)}, bf16[2,256,512]{2,1,0:T(8,128)(2,1)S(1)}, u32[]{:S(2)}, u32[]{:S(2)}) collective-permute-start(bf16[2,256,512]{2,1,0:T(8,128)(2,1)} %reduce-scatter.18.cloned.1.call-done), channel_id=1, source_target_pairs={{0,16},{16,0},{1,17},{17,1},{2,18},{18,2},{3,19},{19,3},{4,20},{20... | collective-permute-start | bytes 1572872 | tf_op jit(solution)/shard_map/ppermute | solution.py:430
  276.9 0.8 copy-start.9
  277.7 13.7 %copy-start.7 = (f32[512,512]{1,0:T(8,128)S(1)}, f32[512,512]{1,0:T(8,128)}, u32[]{:S(2)}) copy-start(f32[512,512]{1,0:T(8,128)} %get-tuple-element.80) | copy-start | bytes 3145732
  311.8 6.4 %copy-start.5 = (bf16[4,512,512]{2,1,0:T(8,128)(2,1)S(1)}, bf16[4,512,512]{2,1,0:T(8,128)(2,1)}, u32[]{:S(2)}) copy-start(bf16[4,512,512]{2,1,0:T(8,128)(2,1)} %get-tuple-element.97) | copy-start | bytes 6291460
  311.8 61.2 %reduce-scatter.20.cloned.1.call-start = ((), (), s32[]{:S(2)}) async-start(), calls=%async_computation.19 | async-start | bytes 1966080 | tf_op jit(solution)/shard_map/reduce_scatter | solution.py:477
  312.6 82.3 %reduce-scatter.28.cloned.1.call-start = ((), (), s32[]{:S(2)}) async-start(), calls=%async_computation.23 | async-start | bytes 327680 | tf_op jit(solution)/shard_map/reduce_scatter | solution.py:478
  313.1 102.0 %reduce-scatter.32.cloned.1.call-start = ((), (), s32[]{:S(2)}) async-start(), calls=%async_computation.25 | async-start | bytes 327680 | tf_op jit(solution)/shard_map/reduce_scatter | solution.py:478
  318.1 129.2 %reduce-scatter.38.cloned.1.call-start = ((), (), s32[]{:S(2)}) async-start(), calls=%async_computation.28 | async-start | bytes 2621440 | tf_op jit(solution)/shard_map/reduce_scatter | solution.py:477
  321.4 1.6 copy-start.4
  321.4 163.5 %reduce-scatter.34.cloned.1.call-start = ((), (), s32[]{:S(2)}) async-start(), calls=%async_computation.26 | async-start | bytes 2621440 | tf_op jit(solution)/shard_map/reduce_scatter | solution.py:477
  326.1 71.2 %copy-start.6 = (f32[512,512]{1,0:T(8,128)S(1)}, f32[512,512]{1,0:T(8,128)}, u32[]{:S(2)}) copy-start(f32[512,512]{1,0:T(8,128)} %get-tuple-element.73) | copy-start | bytes 3145732
  326.2 177.2 %reduce-scatter.40.cloned.1.call-start = ((), (), s32[]{:S(2)}) async-start(), calls=%async_computation.30 | async-start | bytes 163840
  342.3 74.4 %copy-start.3 = (f32[768,512]{1,0:T(8,128)S(1)}, f32[768,512]{1,0:T(8,128)}, u32[]{:S(2)}) copy-start(f32[768,512]{1,0:T(8,128)} %get-tuple-element.87) | copy-start | bytes 4718596
  344.1 180.2 %reduce-scatter.22.cloned.1.call-start = ((), (), s32[]{:S(2)}) async-start(), calls=%async_computation.20 | async-start | bytes 491520 | tf_op jit(solution)/shard_map/reduce_scatter | solution.py:478
  373.1 173.4 %reduce-scatter.42.cloned.1.call-start = ((), (), s32[]{:S(2)}) async-start(), calls=%async_computation.31 | async-start | bytes 655360
  395.8 19.4 %collective-permute-start.7 = (f32[128,256]{1,0:T(8,128)S(1)}, f32[128,256]{1,0:T(8,128)S(1)}, u32[]{:S(2)}, u32[]{:S(2)}) collective-permute-start(f32[128,256]{1,0:T(8,128)S(1)} %convert_element_type.62), channel_id=1, source_target_pairs={{0,16},{16,0},{1,17},{17,1},{2,18},{18,2},{3,19},{19,3},{4,20},{20... | collective-permute-start | bytes 393224 | tf_op jit(solution)/shard_map/ppermute | solution.py:486
  416.8 32.7 %copy-start.15 = (f32[3,512]{1,0:T(4,128)S(1)}, f32[3,512]{1,0:T(4,128)}, u32[]{:S(2)}) copy-start(f32[3,512]{1,0:T(4,128)} %get-tuple-element.89) | copy-start | bytes 18436
  416.8 32.7 %copy-start.16 = (f32[3,512]{1,0:T(4,128)S(1)}, f32[3,512]{1,0:T(4,128)}, u32[]{:S(2)}) copy-start(f32[3,512]{1,0:T(4,128)} %get-tuple-element.88) | copy-start | bytes 18436
  416.9 32.6 %collective-permute-start.5 = (bf16[2,64,512]{2,1,0:T(8,128)(2,1)S(1)}, bf16[2,64,512]{2,1,0:T(8,128)(2,1)S(1)}, u32[]{:S(2)}, u32[]{:S(2)}) collective-permute-start(bf16[2,64,512]{2,1,0:T(8,128)(2,1)S(1)} %get-tuple-element.126), channel_id=1, source_target_pairs={{1,0},{2,1},{3,2},{5,4},{6,5},{7,6},{9,8},{10,9},{11,10},{13,12},{... | collective-permute-start | bytes 393224 | tf_op jit(solution)/shard_map/ppermute | solution.py:328
  418.2 32.4 %collective-permute-start.6 = (bf16[2,64,512]{2,1,0:T(8,128)(2,1)S(1)}, bf16[2,64,512]{2,1,0:T(8,128)(2,1)S(1)}, u32[]{:S(2)}, u32[]{:S(2)}) collective-permute-start(bf16[2,64,512]{2,1,0:T(8,128)(2,1)S(1)} %get-tuple-element.125), channel_id=1, source_target_pairs={{0,1},{1,2},{2,3},{4,5},{5,6},{6,7},{8,9},{9,10},{10,11},{12,13},{... | collective-permute-start | bytes 393224 | tf_op jit(solution)/shard_map/ppermute | solution.py:328
  449.4 36.1 %copy-start.1 = (f32[512,512]{1,0:T(8,128)S(1)}, f32[512,512]{1,0:T(8,128)}, u32[]{:S(2)}) copy-start(f32[512,512]{1,0:T(8,128)} %broadcast_select_fusion.2.g_ref) | copy-start | bytes 3145732
  449.4 119.3 %reduce-scatter.36.cloned.1.call-start = ((), (), s32[]{:S(2)}) async-start(), calls=%async_computation.27 | async-start | bytes 655360 | tf_op jit(solution)/shard_map/reduce_scatter | solution.py:478
Sparse Core Ops, SparseCore 0:
  10.2 25.1 all-gather.8
  36.9 22.7 all-gather.10
  61.3 22.5 all-gather.12
  109.6 21.6 all-gather.14
  132.7 16.7 all-gather.16
  151.5 16.7 all-gather.18
  189.8 73.2 reduce-scatter.17
  265.7 24.8 reduce-scatter.25
  293.2 24.8 reduce-scatter.29
  320.6 21.6 reduce-scatter.23
  344.8 28.1 reduce-scatter.19
  375.2 19.6 reduce-scatter.27
  397.2 17.8 reduce-scatter.31
  417.6 29.6 reduce-scatter.37
  449.7 31.7 reduce-scatter.33
  484.3 18.9 reduce-scatter.39
  505.5 18.7 reduce-scatter.21
  526.5 19.9 reduce-scatter.41
  548.8 19.8 reduce-scatter.35

commit v2 on v1

v2 whole, which is shorter than its diff:
```python
import functools

import jax
import jax.numpy as jnp
from jax import lax
from jax.experimental import pallas as pl
from jax.experimental.pallas import tpu as pltpu
from jax.sharding import PartitionSpec as P

EPS = 1e-05
MASKED = -1000000000.0
DH = 64
HALO = 64
F32 = jnp.float32
BF16 = jnp.bfloat16
GELU_C = 0.7978845608028654
GELU_A = 0.044715
MESH = pl.DeviceIdType.MESH
VMEM_LIMIT = 63 << 20


def mm(a, b):
    return lax.dot_general(a, b, (((1,), (0,)), ((), ())), preferred_element_type=F32)


def mm_nt(a, b):
    return lax.dot_general(a, b, (((1,), (1,)), ((), ())), preferred_element_type=F32)


def mm_tn(a, b):
    return lax.dot_general(a, b, (((0,), (0,)), ((), ())), preferred_element_type=F32)


def norm_parts(v):
    c = v - jnp.mean(v, axis=-1, keepdims=True)
    r = lax.rsqrt(jnp.mean(c * c, axis=-1, keepdims=True) + EPS)
    return c * r, r


def norm(v, gain):
    xhat, _ = norm_parts(v)
    return xhat * gain


def norm_back(v, gain, dn):
    xhat, r = norm_parts(v)
    dxh = dn * gain
    m1 = jnp.mean(dxh, axis=-1, keepdims=True)
    m2 = jnp.mean(dxh * xhat, axis=-1, keepdims=True)
    return r * (dxh - m1 - xhat * m2), jnp.sum(dn * xhat, axis=0, keepdims=True)


def lane_low(shape):
    return lax.broadcasted_iota(jnp.int32, shape, 1) < DH


def head_pick(rows, h):
    low = lane_low(rows.shape)
    return jnp.where(low if h == 0 else jnp.logical_not(low), rows, jnp.zeros_like(rows))


def pair_join(a, b):
    return jnp.where(lane_low(a.shape), a, b)


def attend(q2, k2, v2, bias, keep):
    outs = []
    for h in range(2):
        s = mm_nt(head_pick(q2, h), k2) + bias
        e = jnp.exp(s - jnp.max(s, axis=-1, keepdims=True))
        p = e * (1.0 / jnp.sum(e, axis=-1, keepdims=True))
        pb = p.astype(BF16)
        keep(h, pb)
        outs.append(mm(pb, v2))
    return pair_join(*outs)


def attend_back(q2, k2, v2, do2, pbs):
    dq, dk, dv = [], [], []
    for h in range(2):
        pb = pbs(h)
        dp = mm_nt(head_pick(do2, h), v2)
        dv.append(mm_tn(pb, do2))
        p = pb.astype(F32)
        ds = (p * (dp - jnp.sum(dp * p, axis=-1, keepdims=True))).astype(BF16)
        dq.append(mm(ds, k2))
        dk.append(mm_tn(ds, q2))
    return pair_join(*dq) * (DH**-0.5), pair_join(*dk), pair_join(*dv)


def gelu_parts(h):
    th = jnp.tanh(GELU_C * (h + GELU_A * (h * h * h)))
    half = 0.5 * (1.0 + th)
    u = h * half
    slope = half + (0.5 * GELU_C) * h * (1.0 - th * th) * (1.0 + (3.0 * GELU_A) * (h * h))
    return u, slope


def flip(i, bit):
    return i + bit - 2 * bit * lax.rem(lax.div(i, bit), 2)


def bit_of(i, bit):
    return lax.rem(lax.div(i, bit), 2)


def reversed_bits(i, count):
    out, bit = 0, 1
    while bit < count:
        out = 2 * out + (i // bit) % 2
        bit *= 2
    return out


class Links:
    def __init__(self, send, recv, local):
        self.send, self.recv, self.local = send, recv, local
        self.n = self.m = 0
        self.sent = []

    def take(self, count=1):
        self.n += count
        return self.n - count

    def remote(self, src, dst, device, at=None):
        at = self.take() if at is None else at
        return pltpu.make_async_remote_copy(
            src_ref=src, dst_ref=dst, send_sem=self.send.at[at], recv_sem=self.recv.at[at],
            device_id=device, device_id_type=MESH,
        )

    def here(self, src, dst):
        self.m += 1
        return pltpu.make_async_copy(src, dst, self.local.at[self.m - 1])


class Gather:
    def __init__(self, links, src, full, at, inner):
        t, t2 = at["t"], at["t2"]
        half = full.shape[1] // 2
        mine = pl.ds(pl.multiple_of(at["b"] * half, half), half)
        other = pl.ds(pl.multiple_of((1 - at["b"]) * half, half), half)
        self.own = None if inner else links.here(src, full.at[t])
        self.core = links.remote(src, full.at[t], at["C"])
        self.over_y = links.remote(src.at[mine], full.at[t, mine], at["Y"])
        self.over_z = links.remote(full.at[t2, mine], full.at[t2, mine], at["Z"][0])
        self.core_a = links.remote(full.at[t2, mine], full.at[t2, mine], at["C"])
        self.core_b = links.remote(full.at[t2, other], full.at[t2, other], at["C"])

    def start_near(self):
        if self.own is not None:
            self.own.start()
        self.core.start()

    def start_y(self):
        self.over_y.start()

    def step1(self):
        self.over_y.wait_recv()
        self.over_z.start()
        self.core_a.start()

    def step2(self):
        self.over_z.wait_recv()
        self.core_b.start()

    def ready(self, i):
        if i == 0 and self.own is not None:
            self.own.wait()
        if i == 1:
            self.core.wait_recv()
        if i == 3:
            self.core_a.wait_recv()
            self.core_b.wait_recv()

    def finish(self):
        for c in (self.core, self.over_y, self.over_z, self.core_a, self.core_b):
            c.wait_send()


class Reduce:
    def __init__(self, links, part, rc, ry, zb, zr, at):
        self.part, self.at = part, at
        self.rc, self.ry, self.zb, self.zr = rc, ry, zb, zr
        self.dp = zb.shape[0]
        self.core = [links.remote(part(at[f]), rc.at[j], at["C"]) for j, f in enumerate(("t1", "t3"))]
        self.over_y = links.remote(part(at["t2"]), ry, at["Y"])
        self.over_z = []
        off, m, bit, k = 0, self.dp, 1, 0
        self.kept = []
        while m > 1:
            m //= 2
            b = bit_of(at["d"], bit)
            keep, give = off + b * m, off + (1 - b) * m
            self.over_z.append(links.remote(zb.at[pl.ds(give, m)], zr[k], at["Z"][k]))
            self.kept.append((keep, m))
            off, bit, k = keep, 2 * bit, k + 1

    def core_send(self, j):
        self.core[j].start()

    def core_done(self):
        self.core[0].wait_recv()
        self.core[1].wait_recv()
        far, near = self.part(self.at["t2"]), self.part(self.at["t"])
        far[...] = (far[...].astype(F32) + self.rc[1].astype(F32)).astype(BF16)
        self.over_y.start()
        near[...] = (near[...].astype(F32) + self.rc[0].astype(F32)).astype(BF16)

    def y_done(self):
        self.over_y.wait_recv()
        near = self.part(self.at["t"])
        rows = self.zb.shape[1]
        for i in range(self.dp):
            where = pl.ds(i * rows, rows)
            total = near[where].astype(F32) + self.ry[where].astype(F32)
            self.zb[reversed_bits(i, self.dp)] = total.astype(BF16)
        self.over_z[0].start()

    def z_done(self, k, out=None):
        self.over_z[k].wait_recv()
        keep, m = self.kept[k]
        if k == len(self.over_z) - 1:
            out[...] = self.zb[keep].astype(F32) + self.zr[k][0].astype(F32)
        else:
            live = self.zb.at[pl.ds(keep, m)]
            live[...] = (live[...].astype(F32) + self.zr[k][...].astype(F32)).astype(BF16)
            self.over_z[k + 1].start()

    def rest_z(self, k, out):
        for j in range(k, len(self.over_z)):
            self.z_done(j, out)

    def finish(self):
        for c in self.core + [self.over_y] + self.over_z:
            c.wait_send()


def layers(names, *refs):
    ref = dict(zip(names, refs))
    R = lambda name: ref[name]
    p, d, t = lax.axis_index("pipe"), lax.axis_index("dp"), lax.axis_index("tensor")
    is_enc, is_dec = p == 0, p == 1
    dp = lax.axis_size("dp")
    t1, t2, t3 = flip(t, 1), flip(t, 2), 3 - t
    zbits = []
    while 2 ** len(zbits) < dp:
        zbits.append((p, flip(d, 2 ** len(zbits)), t))
    at = dict(t=t, t1=t1, t2=t2, t3=t3, d=d, b=bit_of(d, 1), C=(p, d, t1), Y=(p, d, t2), T=(p, d, t3), X=(1 - p, d, t), Z=zbits)
    rows, own, width = R("x").shape
    win, cwin = own + 2 * HALO, 2 * own + 2 * HALO
    slots = 4 * own
    tokens = rows * own
    hw = R("wa").shape[2] // 3
    inner = t % 3 != 0
    scale = jnp.asarray(DH**-0.5, BF16)
    gain_ref, x_ref = R("gains"), R("x")
    side = 3 * own // 4

    def rowsl(r, n=own):
        return pl.ds(pl.multiple_of(r * n, n), n)

    def lanes(s, n=hw):
        return pl.ds(pl.multiple_of(s * n, n), n)

    def near_first(i):
        return 2 * lax.rem(lax.div(t, 2) + lax.div(i, 2), 2) + lax.rem(lax.rem(t, 2) + lax.rem(i, 2), 2)

    def far_first(i):
        return 2 * lax.rem(lax.div(t, 2) + lax.rem(lax.div(i + 1, 2), 2), 2) + lax.rem(lax.rem(t, 2) + 1 - lax.div(i, 2), 2)

    links = Links(R("send"), R("recv"), R("local"))
    g_wa = Gather(links, R("wa_h"), R("wa"), at, False)
    g_wo = Gather(links, R("wo_h"), R("wo"), at, False)
    g_w1 = Gather(links, R("w1_h"), R("w1"), at, False)
    g_w2 = Gather(links, R("w2_h"), R("w2"), at, False)
    g_c1 = Gather(links, R("cx_h"), R("c1"), at, False)
    c0_x = links.remote(R("cx_h"), R("c0").at[t], at["X"])
    g_c0 = Gather(links, R("c0").at[t], R("c0"), at, True)
    x_right = links.remote(x_ref.at[:, pl.ds(own - HALO, HALO)], R("xh").at[0], (p, d, lax.rem(t + 1, 4)))
    x_left = links.remote(x_ref.at[:, pl.ds(0, HALO)], R("xh").at[1], (p, d, lax.rem(t + 3, 4)))
    base_mem, base_memc, base_memt = links.take(rows), links.take(rows), links.take(rows)
    base_dmc, base_dmt, base_dmx = links.take(rows), links.take(rows), links.take(rows)
    block = pl.ds(pl.multiple_of(t * own, own), own)
    block1 = pl.ds(pl.multiple_of(t1 * own, own), own)
    edge_out = pl.ds(pl.multiple_of(lax.rem(own // 2 + side * t, slots), HALO), side)
    edge_in = pl.ds(pl.multiple_of(lax.rem(own // 2 + side * t3, slots), HALO), side)

    def mem_x(r):
        return links.remote(R("sec").at[rowsl(r)], R("memf").at[r, block], at["X"], base_mem + r)

    def mem_c(r):
        return links.remote(R("memf").at[r, block], R("memf").at[r, block], at["C"], base_memc + r)

    def mem_t(r):
        return links.remote(R("memf").at[r, edge_out], R("memf").at[r, edge_out], at["T"], base_memt + r)

    def in_row(r, span):
        return pl.ds(pl.multiple_of(r * slots + span.start, HALO), span.size)

    def dm_rows(r, span):
        return R("dmf").at[in_row(r, span)]

    def dm_c(r):
        return links.remote(dm_rows(r, block1), R("rcc").at[r], at["C"], base_dmc + r)

    def dm_t(r):
        return links.remote(dm_rows(r, edge_in), R("rct").at[r], at["T"], base_dmt + r)

    def dm_x(r):
        return links.remote(R("dmt").at[r], R("dmr").at[r], at["X"], base_dmx + r)

    def parts_of(buf, n_rows, n_cols, skip=0):
        def part(s):
            return buf.at[pl.ds(pl.multiple_of(skip + s * n_rows, n_rows), n_rows), pl.ds(0, n_cols)]

        return part

    def reduce_of(name, buf, skip=0):
        rc, ry, zb = R("rc_" + name), R("ry_" + name), R("zb_" + name)
        zr = [R(f"zr{k}_{name}") for k in range(len(zbits))]
        return Reduce(links, parts_of(buf, ry.shape[0], ry.shape[1], skip), rc, ry, zb, zr, at)

    r_w2 = reduce_of("w2", R("dw2"))
    r_w1 = reduce_of("w1", R("dmf"))
    r_wo = reduce_of("wo", R("dwo"))
    r_wa = reduce_of("wa", R("cp"))
    r_c0 = reduce_of("c0", R("kv"))
    r_c1 = reduce_of("c1", R("kv"), 4 * width)
    c0_back = links.remote(R("dc0"), R("dc0r"), at["X"])
    dn_right = links.remote(R("dhs").at[1], R("dhr").at[0], (p, d, lax.rem(t + 1, 4)))
    dn_left = links.remote(R("dhs").at[0], R("dhr").at[1], (p, d, lax.rem(t + 3, 4)))
    gain_links = [links.remote(R("dgs").at[k], R("dgr").at[k], dev) for k, dev in enumerate([at["C"], at["Y"]] + zbits)]

    @pl.when(is_dec)
    def _():
        for at_t, start in ((0, 2 * own), (1, 2 * own + side), (3, 2 * own - 2 * HALO)):
            @pl.when(t == at_t)
            def _():
                for r in range(rows):
                    R("memf")[r, pl.ds(start, 2 * HALO), :] = jnp.zeros((2 * HALO, width), BF16)

    barrier = pltpu.get_barrier_semaphore()
    partners = [at["C"], at["Y"], at["T"], at["X"]] + zbits
    for dev in partners:
        pl.semaphore_signal(barrier, inc=1, device_id=dev, device_id_type=MESH)
    pl.semaphore_wait(barrier, len(partners))

    pl.when(t < 3)(x_right.start)
    pl.when(t > 0)(x_left.start)
    g_wa.start_near()
    g_wa.start_y()
    g_wo.start_near()
    g_wo.start_y()

    @pl.when(is_enc)
    def _():
        c0_x.start()
        g_w1.start_near()
        g_w2.start_near()

    @pl.when(is_dec)
    def _():
        g_c1.start_near()
        g_w2.start_near()
        g_w1.start_near()

    nw_ref, bias_ref = R("nw"), R("bias")
    gain0 = gain_ref[pl.ds(0, 1), :]
    for r in range(rows):
        nw_ref[pl.ds(r * win + HALO, own), :] = norm(x_ref[r].astype(F32), gain0).astype(BF16)
        same = R("sq")[r] == R("sk")[r]
        qpos = lax.broadcasted_iota(jnp.int32, (own, win), 0)
        kpos = lax.broadcasted_iota(jnp.int32, (own, win), 1) - HALO
        before = kpos - qpos <= jnp.where(is_enc, 4 * win, 0)
        bias_ref[r] = jnp.where(same & before, 0.0, MASKED)

    @pl.when(t == 0)
    def _():
        R("xh")[0] = jnp.zeros((rows, HALO, width), BF16)

    @pl.when(t == 3)
    def _():
        R("xh")[1] = jnp.zeros((rows, HALO, width), BF16)

    pl.when(t > 0)(x_right.wait_recv)
    pl.when(t < 3)(x_left.wait_recv)
    for r in range(rows):
        nw_ref[pl.ds(r * win, HALO), :] = norm(R("xh")[0, r].astype(F32), gain0).astype(BF16)
        nw_ref[pl.ds(r * win + HALO + own, HALO), :] = norm(R("xh")[1, r].astype(F32), gain0).astype(BF16)

    def after_pair(i):
        @pl.when(i == 0)
        def _():
            g_wa.step1()
            pl.when(is_enc)(g_w1.start_y)
            pl.when(is_dec)(g_c1.start_y)

        @pl.when(i == 1)
        def _():
            g_wa.step2()
            g_wo.step1()
            pl.when(is_enc)(g_w2.start_y)

            @pl.when(is_dec)
            def _():
                c0_x.wait_recv()
                g_c0.start_near()
                g_c0.start_y()
                g_w2.start_y()

        @pl.when(i == 2)
        def _():
            g_wo.step2()
            pl.when(is_enc)(g_w1.step1)

            @pl.when(is_dec)
            def _():
                g_c1.step1()
                g_w1.start_y()

        @pl.when(i == 3)
        def _():
            pl.when(is_enc)(g_w1.step2)

            @pl.when(is_dec)
            def _():
                g_c1.step2()
                g_c0.step1()

    def wait_ready(i, *weights):
        for k in range(4):
            @pl.when(i == k)
            def _():
                for w in weights:
                    w.ready(k)

    q_ref, k_ref, v_ref, p_ref, o_ref = R("q"), R("k"), R("v"), R("p"), R("o")

    def self_pair(i, _):
        s = near_first(i)
        wait_ready(i, g_wa)
        packed = mm(nw_ref[...], R("wa")[s])
        for r in range(rows):
            q_ref[s, r] = packed[r * win + HALO : r * win + HALO + own, :hw].astype(BF16) * scale
            k_ref[s, r] = packed[r * win : (r + 1) * win, hw : 2 * hw].astype(BF16)
            v_ref[s, r] = packed[r * win : (r + 1) * win, 2 * hw :].astype(BF16)

        def one(r, _):
            def keep(h, pb):
                p_ref[s, r, h] = pb

            o2 = attend(q_ref[s, r], k_ref[s, r], v_ref[s, r], bias_ref[r], keep)
            o_ref[rowsl(r), lanes(s)] = o2.astype(BF16)
            return 0

        lax.fori_loop(0, rows, one, 0)
        after_pair(i)
        return 0

    lax.fori_loop(0, 4, self_pair, 0)
    for k in range(4):
        g_wo.ready(k)
    r1_ref, r2_ref, n2_ref, n3_ref = R("r1"), R("r2"), R("n2"), R("n3")
    u_ref, gp_ref, sec_ref = R("u"), R("gp"), R("sec")
    acc_ref, g_ref, gb_ref = R("acc"), R("g"), R("gb")
    first = mm(o_ref[...], R("wo")[...].reshape(4 * hw, width))
    for r in range(rows):
        r1_ref[pl.ds(r * own, own), :] = x_ref[r].astype(F32) + first[r * own : (r + 1) * own]
    n2_ref[...] = norm(r1_ref[...], gain_ref[pl.ds(1, 1), :]).astype(BF16)

    @pl.when(is_enc)
    def _():
        def row(r, _):
            rs = rowsl(r)
            r2_ref[rs, :] = r1_ref[rs, :]

            def one(i, _):
                s = near_first(i)

                @pl.when(r == 0)
                def _():
                    wait_ready(i, g_w1, g_w2)

                u, gp = gelu_parts(mm(n2_ref[rs, :], R("w1")[s]))
                u = u.astype(BF16)
                u_ref[s, rs, :] = u
                gp_ref[s, rs, :] = gp.astype(BF16)
                r2_ref[rs, :] += mm(u, R("w2")[s])
                pl.when((r == 0) & (i == 0))(g_w2.step1)
                pl.when((r == 0) & (i == 1))(g_w2.step2)
                return 0

            lax.fori_loop(0, 4, one, 0)
            sec_ref[rs, :] = norm(r2_ref[rs, :], gain_ref[pl.ds(2, 1), :]).astype(BF16)
            mem_x(r).start()
            return 0

        lax.fori_loop(0, rows, row, 0)

    cstart = pl.multiple_of(jnp.minimum(t * (own - HALO), slots - cwin), HALO)
    cwindow = pl.ds(cstart, cwin)
    kv_ref, cq_ref, cp_ref, dkv_ref, cbias_ref = R("kv"), R("cq"), R("cp"), R("dkv"), R("cbias")
    c0_ref, c1_ref, oc_ref, cot_ref = R("c0"), R("c1"), R("oc"), R("cot")

    @pl.when(is_dec)
    def _():
        g_c0.step2()
        g_w2.step1()
        kv_ref[...] = jnp.zeros_like(kv_ref)
        R("dmf")[...] = jnp.zeros_like(R("dmf"))
        for k in range(4):
            g_c1.ready(k)

        def queries(s, _):
            q = mm(n2_ref[...], c1_ref[s, :, :hw]).astype(BF16) * scale
            for r in range(rows):
                cq_ref[s, r] = q[r * own : (r + 1) * own]
            return 0

        lax.fori_loop(0, 4, queries, 0)
        g_w2.step2()
        g_w1.step1()
        for k in range(4):
            g_w2.ready(k)

        def early(s, _):
            gp_ref[s] = mm_nt(cot_ref[...], R("w2")[s]).astype(BF16)
            return 0

        lax.fori_loop(0, 4, early, 0)
        g_w1.step2()
        for k in range(4):
            g_w1.ready(k)
            g_c0.ready(k)

        def row(r, _):
            rs = rowsl(r)
            cbias_ref[...] = jnp.where(R("csq")[r] == R("csk")[r], 0.0, MASKED)

            def keys(span, n):
                def one(s, _):
                    kv = mm(R("memf")[r, span, :], c0_ref[s])
                    kv_ref[pl.ds(pl.multiple_of(s * slots + span.start, HALO), n), :] = kv.astype(BF16)
                    return 0

                lax.fori_loop(0, 4, one, 0)

            mem_x(r).wait_recv()
            mem_c(r).start()
            pl.when(inner)(mem_t(r).start)
            keys(block, own)
            mem_c(r).wait_recv()
            keys(block1, own)

            @pl.when(inner)
            def _():
                mem_t(r).wait_recv()
                keys(edge_in, side)

            r2_ref[rs, :] = r1_ref[rs, :]

            def window(s):
                return pl.ds(pl.multiple_of(s * slots + cstart, HALO), cwin)

            def cross(s, _):
                def keep(h, pb):
                    cp_ref[rowsl(2 * s + h), :] = pb

                o2 = attend(cq_ref[s, r], kv_ref[window(s), :hw], kv_ref[window(s), hw:], cbias_ref[...], keep).astype(BF16)
                oc_ref[rs, lanes(s)] = o2
                r2_ref[rs, :] += mm_nt(o2, c1_ref[s, :, hw:])
                return 0

            lax.fori_loop(0, 4, cross, 0)
            n3_ref[rs, :] = norm(r2_ref[rs, :], gain_ref[pl.ds(2, 1), :]).astype(BF16)
            dn = pl.ds(0, own)
            acc_ref[dn, :] = jnp.zeros((own, width), F32)
            g_ref[rs, :] = r2_ref[rs, :]

            def feed(s, _):
                u, gp = gelu_parts(mm(n3_ref[rs, :], R("w1")[s]))
                u = u.astype(BF16)
                u_ref[s, rs, :] = u
                g_ref[rs, :] += mm(u, R("w2")[s])
                dh = (gp_ref[s, rs, :].astype(F32) * gp).astype(BF16)
                gp_ref[s, rs, :] = dh
                acc_ref[dn, :] += mm_nt(dh, R("w1")[s])
                return 0

            lax.fori_loop(0, 4, feed, 0)
            sec_ref[rs, :] = g_ref[rs, :].astype(BF16)
            dx, dg = norm_back(r2_ref[rs, :], gain_ref[pl.ds(2, 1), :], acc_ref[dn, :])
            R("dg")[r, pl.ds(2, 1), :] = dg
            g2 = cot_ref[rs, :].astype(F32) + dx
            g_ref[rs, :] = g2
            gb_ref[rs, :] = g2.astype(BF16)
            acc_ref[pl.ds(0, cwin), :] = jnp.zeros((cwin, width), F32)
            ws = pl.ds(pl.multiple_of(r * cwin, HALO), cwin)

            def back(s, _):
                do2 = mm(gb_ref[rs, :], c1_ref[s, :, hw:]).astype(BF16)
                dq, dk, dv = attend_back(
                    cq_ref[s, r], kv_ref[window(s), :hw], kv_ref[window(s), hw:], do2, lambda h: cp_ref[rowsl(2 * s + h), :]
                )
                cq_ref[s, r] = dq.astype(BF16)
                dkv_ref[s, ws, :hw] = dk.astype(BF16)
                dkv_ref[s, ws, hw:] = dv.astype(BF16)
                acc_ref[pl.ds(0, cwin), :] += mm_nt(dkv_ref[s, ws, :], c0_ref[s])
                return 0

            lax.fori_loop(0, 4, back, 0)
            R("dmf")[in_row(r, cwindow), :] = acc_ref[pl.ds(0, cwin), :].astype(BF16)
            dm_c(r).start()
            pl.when(inner)(dm_t(r).start)
            acc_ref[dn, :] = jnp.zeros((own, width), F32)

            def to_normed(s, _):
                acc_ref[dn, :] += mm_nt(cq_ref[s, r], c1_ref[s, :, :hw])
                return 0

            lax.fori_loop(0, 4, to_normed, 0)
            dx, dg = norm_back(r1_ref[rs, :], gain_ref[pl.ds(1, 1), :], acc_ref[dn, :])
            R("dg")[r, pl.ds(1, 1), :] = dg
            dm_c(r).wait_recv()
            acc_ref[dn, :] = R("dmf")[in_row(r, block), :].astype(F32) + R("rcc")[r].astype(F32)

            @pl.when(inner)
            def _():
                dm_t(r).wait_recv()
                place = pl.ds(pl.multiple_of((2 - t) * (own - side), HALO), side)
                acc_ref[place, :] += R("rct")[r].astype(F32)

            R("dmt")[r] = acc_ref[dn, :].astype(BF16)
            dm_x(r).start()
            g_ref[rs, :] += dx
            return 0

        lax.fori_loop(0, rows, row, 0)
        for r in range(rows):
            dm_c(r).wait_send()
            pl.when(inner)(dm_t(r).wait_send)

        def c0_grad(i, _):
            s = far_first(i)
            dst = r_c0.part(s)
            total = mm_tn(R("memf")[0, cwindow, :], dkv_ref[s, pl.ds(0, cwin), :])
            for r in range(1, rows):
                total += mm_tn(R("memf")[r, cwindow, :], dkv_ref[s, pl.ds(r * cwin, cwin), :])
            dst[...] = total.astype(BF16)
            pl.when(i == 0)(lambda: r_c0.core_send(0))
            pl.when(i == 1)(lambda: r_c0.core_send(1))
            return 0

        lax.fori_loop(0, 4, c0_grad, 0)

        def c1_grad(i, _):
            s = far_first(i)
            dst = r_c1.part(s)
            dst[:, :hw] = mm_tn(n2_ref[...], cq_ref[s].reshape(tokens, hw)).astype(BF16)
            dst[:, hw:] = mm_tn(gb_ref[...], oc_ref[:, lanes(s)]).astype(BF16)
            pl.when(i == 0)(lambda: r_c1.core_send(0))
            pl.when(i == 1)(lambda: r_c1.core_send(1))
            return 0

        lax.fori_loop(0, 4, c1_grad, 0)
        r_c0.core_done()

        def w2_grad(i, _):
            s = far_first(i)
            r_w2.part(s)[...] = mm_tn(cot_ref[...], u_ref[s]).astype(BF16)
            pl.when(i == 0)(lambda: r_w2.core_send(0))
            pl.when(i == 1)(lambda: r_w2.core_send(1))
            return 0

        lax.fori_loop(0, 4, w2_grad, 0)
        r_c1.core_done()

        def w1_grad(i, _):
            s = far_first(i)
            r_w1.part(s)[...] = mm_tn(n3_ref[...], gp_ref[s]).astype(BF16)
            pl.when(i == 0)(lambda: r_w1.core_send(0))
            pl.when(i == 1)(lambda: r_w1.core_send(1))
            return 0

        lax.fori_loop(0, 4, w1_grad, 0)

    @pl.when(is_enc)
    def _():
        def row(r, _):
            rs = rowsl(r)
            dm_x(r).wait_recv()
            dx, dg = norm_back(r2_ref[rs, :], gain_ref[pl.ds(2, 1), :], R("dmr")[r].astype(F32))
            R("dg")[r, pl.ds(2, 1), :] = dg
            g_ref[rs, :] = dx
            gb_ref[rs, :] = dx.astype(BF16)
            return 0

        lax.fori_loop(0, rows, row, 0)

        def w2_grad(i, _):
            s = far_first(i)
            r_w2.part(s)[...] = mm_tn(gb_ref[...], u_ref[s]).astype(BF16)
            pl.when(i == 0)(lambda: r_w2.core_send(0))
            pl.when(i == 1)(lambda: r_w2.core_send(1))
            return 0

        lax.fori_loop(0, 4, w2_grad, 0)
        dn = pl.ds(0, tokens)
        acc_ref[dn, :] = jnp.zeros((tokens, width), F32)

        def w1_grad(i, _):
            s = far_first(i)
            dh = (mm_nt(gb_ref[...], R("w2")[s]) * gp_ref[s].astype(F32)).astype(BF16)
            r_w1.part(s)[...] = mm_tn(n2_ref[...], dh).astype(BF16)
            pl.when(i == 0)(lambda: r_w1.core_send(0))
            pl.when(i == 1)(lambda: r_w1.core_send(1))
            acc_ref[dn, :] += mm_nt(dh, R("w1")[s])
            return 0

        lax.fori_loop(0, 4, w1_grad, 0)
        dx, dg = norm_back(r1_ref[...], gain_ref[pl.ds(1, 1), :], acc_ref[dn, :])
        R("dg")[0, pl.ds(1, 1), :] = dg
        for r in range(1, rows):
            R("dg")[r, pl.ds(1, 1), :] = jnp.zeros_like(dg)
        g_ref[...] += dx

    r_w2.core_done()
    gb_ref[...] = g_ref[...].astype(BF16)

    def wo_grad(i, _):
        s = far_first(i)
        r_wo.part(s)[...] = mm_tn(gb_ref[...], o_ref[:, lanes(s)]).astype(BF16)
        pl.when(i == 0)(lambda: r_wo.core_send(0))
        pl.when(i == 1)(lambda: r_wo.core_send(1))
        return 0

    lax.fori_loop(0, 4, wo_grad, 0)
    acc_ref[...] = jnp.zeros_like(acc_ref)
    dqkv_ref = R("dqkv")
    for r in range(rows):
        dqkv_ref[pl.ds(r * win, HALO), :hw] = jnp.zeros((HALO, hw), BF16)
        dqkv_ref[pl.ds(r * win + HALO + own, HALO), :hw] = jnp.zeros((HALO, hw), BF16)

    def self_back(i, _):
        s = far_first(i)
        do = mm_nt(gb_ref[...], R("wo")[s]).astype(BF16)
        R("do")[...] = do

        def one(r, _):
            dq, dk, dv = attend_back(q_ref[s, r], k_ref[s, r], v_ref[s, r], R("do")[rowsl(r), :], lambda h: p_ref[s, r, h])
            base = pl.multiple_of(r * win, HALO)
            dqkv_ref[pl.ds(base + HALO, own), :hw] = dq.astype(BF16)
            dqkv_ref[pl.ds(base, win), hw : 2 * hw] = dk.astype(BF16)
            dqkv_ref[pl.ds(base, win), 2 * hw :] = dv.astype(BF16)
            return 0

        lax.fori_loop(0, rows, one, 0)
        r_wa.part(s)[...] = mm_tn(nw_ref[...], dqkv_ref[...]).astype(BF16)
        acc_ref[...] += mm_nt(dqkv_ref[...], R("wa")[s])

        @pl.when(i == 0)
        def _():
            r_wa.core_send(0)
            r_w1.core_done()

        @pl.when(i == 1)
        def _():
            r_wa.core_send(1)
            r_wo.core_done()
            pl.when(is_dec)(r_c0.y_done)

        @pl.when(i == 2)
        def _():
            pl.when(is_dec)(r_c1.y_done)
            pl.when(is_dec)(lambda: r_c0.z_done(0))

        return 0

    lax.fori_loop(0, 4, self_back, 0)
    for r in range(rows):
        R("dhs")[0, r] = acc_ref[pl.ds(r * win, HALO), :].astype(BF16)
        R("dhs")[1, r] = acc_ref[pl.ds(r * win + HALO + own, HALO), :].astype(BF16)
    pl.when(t < 3)(dn_right.start)
    pl.when(t > 0)(dn_left.start)
    r_wa.core_done()

    @pl.when(t == 0)
    def _():
        R("dhr")[0] = jnp.zeros((rows, HALO, width), BF16)

    @pl.when(t == 3)
    def _():
        R("dhr")[1] = jnp.zeros((rows, HALO, width), BF16)

    pl.when(t > 0)(dn_right.wait_recv)
    pl.when(t < 3)(dn_left.wait_recv)
    for r in range(rows):
        lo, hi = pl.ds(r * win + HALO, HALO), pl.ds(r * win + own, HALO)
        acc_ref[lo, :] += R("dhr")[0, r].astype(F32)
        acc_ref[hi, :] += R("dhr")[1, r].astype(F32)
    total = jnp.zeros((1, width), F32)
    for r in range(rows):
        rs = pl.ds(r * own, own)
        dx, dg = norm_back(x_ref[r].astype(F32), gain0, acc_ref[pl.ds(r * win + HALO, own), :])
        R("gx")[rs, :] = (g_ref[rs, :] + dx).astype(BF16)
        total += dg
    R("dgs")[0] = jnp.zeros((8, width), F32)
    R("dgs")[0, pl.ds(0, 1), :] = total
    R("dgs")[0, pl.ds(1, 2), :] = sum(R("dg")[r, pl.ds(1, 2), :] for r in range(rows))
    gain_links[0].start()

    r_w2.y_done()

    def gain_step(k):
        gain_links[k].wait_recv()
        if k + 1 < len(gain_links):
            R("dgs")[k + 1] = R("dgs")[k] + R("dgr")[k]
            gain_links[k + 1].start()
        else:
            R("dgain")[...] = R("dgs")[k] + R("dgr")[k]

    gain_step(0)

    @pl.when(is_dec)
    def _():
        r_c0.rest_z(1, R("dc0"))
        c0_back.start()
        r_c1.rest_z(0, R("dc"))

    r_w1.y_done()
    gain_step(1)
    r_w2.z_done(0, R("dw2_o"))
    r_wo.y_done()
    gain_step(2)
    r_wa.y_done()
    r_w1.z_done(0, R("dw1_o"))
    for k in range(3, len(gain_links)):
        gain_step(k)
    r_w2.rest_z(1, R("dw2_o"))
    r_wo.z_done(0, R("dwo_o"))
    r_wa.z_done(0, R("da_o"))
    r_w1.rest_z(1, R("dw1_o"))
    r_wo.rest_z(1, R("dwo_o"))
    r_wa.rest_z(1, R("da_o"))

    for g in (g_wa, g_wo, g_w1, g_w2):
        g.finish()
    for g in (r_w2, r_w1, r_wo, r_wa):
        g.finish()
    for c in gain_links:
        c.wait_send()
    pl.when(t < 3)(x_right.wait_send)
    pl.when(t > 0)(x_left.wait_send)
    pl.when(t < 3)(dn_right.wait_send)
    pl.when(t > 0)(dn_left.wait_send)

    @pl.when(is_enc)
    def _():
        c0_x.wait_send()
        for r in range(rows):
            mem_x(r).wait_send()
        c0_back.wait_recv()
        R("dc")[...] = R("dc0r")[...]

    @pl.when(is_dec)
    def _():
        for g in (g_c1, g_c0, r_c0, r_c1):
            g.finish()
        for r in range(rows):
            mem_c(r).wait_send()
            pl.when(inner)(mem_t(r).wait_send)
            dm_x(r).wait_send()
        c0_back.wait_send()


def body(embeds, segments, cotangent, norm_gains, attn_in, attn_out, cross_proj, ffn_in, ffn_out):
    me = lax.axis_index("tensor")
    is_enc = lax.axis_index("pipe") == 0
    dp = lax.axis_size("dp")
    rows, own, width = embeds.shape[1:]
    slots = segments.shape[2]
    hw = attn_in.shape[3]
    fw = ffn_in.shape[2]
    win = own + 2 * HALO
    cwin = 2 * own + 2 * HALO
    tokens = rows * own
    side = 3 * own // 4
    zsteps = (dp - 1).bit_length()

    start = me * own
    seg_self = jnp.where(is_enc, segments[0], segments[1])
    padded = jnp.pad(seg_self, ((0, 0), (HALO, HALO)), constant_values=-2)
    cstart = jnp.minimum(me * (own - HALO), slots - cwin)
    sq = lax.dynamic_slice(seg_self, (0, start), (rows, own))[:, :, None]
    sk = lax.dynamic_slice(padded, (0, start), (rows, win))[:, None, :]
    csq = lax.dynamic_slice(segments[1], (0, start), (rows, own))[:, :, None]
    csk = lax.dynamic_slice(segments[0], (0, cstart), (rows, cwin))[:, None, :]

    ins = dict(
        x=embeds[0], sq=sq, sk=sk, csq=csq, csk=csk, gains=norm_gains[0], cot=cotangent.reshape(tokens, width),
        wa_h=attn_in[0].reshape(width, 3 * hw), wo_h=attn_out[0], w1_h=ffn_in[0], w2_h=ffn_out[0],
        cx_h=cross_proj[0].reshape(width, 2 * hw),
    )
    outs = dict(
        sec=((tokens, width), BF16), gx=((tokens, width), BF16), dgain=((8, width), F32),
        da_o=((width // dp, 3 * hw), F32), dwo_o=((width // dp, hw), F32), dc=((width // dp, 2 * hw), F32),
        dw1_o=((width // dp, fw), F32), dw2_o=((width // dp, fw), F32),
    )
    vm = dict(
        wa=((4, width, 3 * hw), BF16), wo=((4, hw, width), BF16), w1=((4, width, fw), BF16), w2=((4, fw, width), BF16),
        c0=((4, width, 2 * hw), BF16), c1=((4, width, 2 * hw), BF16),
        xh=((2, rows, HALO, width), BF16), nw=((rows * win, width), BF16),
        q=((4, rows, own, hw), BF16), k=((4, rows, win, hw), BF16), v=((4, rows, win, hw), BF16),
        p=((4, rows, 2, own, win), BF16), o=((tokens, width), BF16), bias=((rows, own, win), F32),
        r1=((tokens, width), F32), r2=((tokens, width), F32), n2=((tokens, width), BF16), n3=((tokens, width), BF16),
        u=((4, tokens, fw), BF16), gp=((4, tokens, fw), BF16),
        acc=((rows * win, width), F32), g=((tokens, width), F32), gb=((tokens, width), BF16),
        memf=((rows, slots, width), BF16), kv=((4 * slots, 2 * hw), BF16), cq=((4, rows, own, hw), BF16),
        cp=((8 * own, cwin), BF16), cbias=((own, cwin), F32), oc=((tokens, width), BF16),
        dkv=((4, rows * cwin, 2 * hw), BF16), dmf=((max(rows * slots, 4 * width), max(width, fw)), BF16),
        rcc=((rows, own, width), BF16), rct=((rows, side, width), BF16), dmt=((rows, own, width), BF16),
        dmr=((rows, own, width), BF16), dg=((rows, 8, width), F32), do=((tokens, hw), BF16),
        dqkv=((rows * win, 3 * hw), BF16), dhs=((2, rows, HALO, width), BF16), dhr=((2, rows, HALO, width), BF16),
        dgs=((2 + zsteps, 8, width), F32), dgr=((2 + zsteps, 8, width), F32),
        dw2=((4 * width, fw), BF16), dwo=((4 * width, hw), BF16),
        dc0=((width // dp, 2 * hw), F32), dc0r=((width // dp, 2 * hw), F32),
    )
    grads = dict(
        w2=fw, w1=fw, wo=hw, wa=3 * hw, c0=2 * hw, c1=2 * hw
    )
    for name, m in grads.items():
        vm["rc_" + name] = ((2, width, m), BF16)
        vm["ry_" + name] = ((width, m), BF16)
        vm["zb_" + name] = ((dp, width // dp, m), BF16)
        for k in range(zsteps):
            vm[f"zr{k}_{name}"] = ((dp >> (k + 1), width // dp, m), BF16)
    copies = 140 + 8 * zsteps
    sems = dict(send=pltpu.SemaphoreType.DMA((copies,)), recv=pltpu.SemaphoreType.DMA((copies,)), local=pltpu.SemaphoreType.DMA((8,)))
    in_hbm = {"wa_h", "wo_h", "w1_h", "w2_h", "cx_h"}
    results = pl.pallas_call(
        functools.partial(layers, list(ins) + list(outs) + list(vm) + list(sems)),
        name="layers",
        out_shape=[jax.ShapeDtypeStruct(*o) for o in outs.values()],
        in_specs=[pl.BlockSpec(memory_space=pl.ANY if n in in_hbm else pltpu.VMEM) for n in ins],
        out_specs=[pl.BlockSpec(memory_space=pltpu.VMEM)] * len(outs),
        scratch_shapes=[pltpu.VMEM(*s) for s in vm.values()] + list(sems.values()),
        compiler_params=pltpu.CompilerParams(vmem_limit_bytes=VMEM_LIMIT, collective_id=0, has_side_effects=True),
    )(*ins.values())
    sec, gx, dgain, da, dwo, dc, dw1, dw2 = results
    share = width // dp
    dgain = lax.dynamic_slice(dgain, (0, lax.axis_index("dp") * share), (3, share))
    return (
        sec.reshape(1, rows, own, width), gx.reshape(1, rows, own, width), dgain[None], da.reshape(1, -1, 3, hw),
        dwo.T[None], dc.reshape(1, -1, 2, hw), dw1[None], dw2.T[None],
    )


def solution(mesh):
    return jax.shard_map(
        body,
        mesh=mesh,
        in_specs=(
            P("pipe", "dp", "tensor", None),
            P(None, "dp", None),
            P("dp", "tensor", None),
            P("pipe", None, None),
            P("pipe", None, None, "tensor"),
            P("pipe", "tensor", None),
            P("pipe", None, None, "tensor"),
            P("pipe", None, "tensor"),
            P("pipe", "tensor", None),
        ),
        out_specs=(
            P("pipe", "dp", "tensor", None),
            P("pipe", "dp", "tensor", None),
            P("pipe", None, "dp"),
            P("pipe", "dp", None, "tensor"),
            P("pipe", "tensor", "dp"),
            P("pipe", "dp", None, "tensor"),
            P("pipe", "dp", "tensor"),
            P("pipe", "tensor", "dp"),
        ),
        check_vma=False,
    )
```

time: 578 us -> 196 us (0.34)
  the two profiles are of different devices: /device:TPU:0 before, /device:TPU:19 now
where the time goes in v2:
time: 196 us; the launch traced here: 195 us
  Pallas kernels  180 us (92%)
  local copies, waits for them, and re-layouts  14.6 us (7%)
    pallas_call x1, Pallas kernels, body(): pl.pallas_call(functools.partial(layers, list(ins) + list(outs) + list(vm...  180 us
    unnamed x29, local copies, waits for them, and re-layouts  8.49 us

profile of v2, /device:TPU:19, one launch (start us, length us, event | category | flops | bytes accessed | tf_op | source)
XLA Modules:
  0.0 195.2 jit_solution(612878723348809716)
XLA Ops:
  0.6 0.0 copy-start.9
  0.7 0.0 copy-start.8
  0.7 0.7 copy-done.9
  1.3 0.6 copy.34
  1.9 0.0 copy-done.8
  2.0 0.1 constant_dynamic-slice_fusion.1
  2.0 0.6 broadcast_in_dim.27.refs_4_
  2.6 0.1 pad_dynamic-slice_fusion
  2.7 0.6 broadcast_in_dim.25.refs_2_
  3.3 0.0 copy-start.3
  3.3 0.9 copy.23.refs_3_
  4.2 0.0 copy-start.2
  4.2 0.9 copy.22.refs_1_
  5.0 0.0 copy-done.3
  5.0 0.7 copy.33
  5.8 0.0 copy-done.2
  5.8 0.2 copy.21
  6.0 0.9 copy.24.refs_7_
  6.9 179.9 %layers.1 = (bf16[512,512]{1,0:T(8,128)(2,1)}, bf16[512,512]{1,0:T(8,128)(2,1)}, f32[8,512]{1,0:T(8,128)}, f32[128,384]{1,0:T(8,128)}, f32[128,128]{1,0:T(8,128)...) custom-call(bf16[2,256,512]{2,1,0:T(8,128)(2,1)} %bitcast.34, s32[2,256,1]{2,1,0:T(8,128)} %copy.22.refs_1_, ...), custom_call_target="tpu_custom_call" | custom-call | tf_op jit(solution)/shard_map/layers/pallas_call | solution.py:941
  186.8 0.0 copy-start.7
  186.8 0.7 constant_dynamic-slice_fusion
  187.5 0.6 broadcast_in_dim.28
  188.1 0.0 copy-start.6
  188.1 1.6 copy.27
  189.7 0.0 copy-done.7
  189.7 0.7 reshape.43
  190.4 0.0 copy-done.6
  190.4 0.0 copy-start.5
  190.4 0.1 copy.25
  190.5 0.0 copy-start.1
  190.5 0.8 copy.26
  191.4 0.0 copy-done.5
  191.4 0.8 copy.28
  192.2 0.0 copy-done.1
  192.2 0.0 copy-start
  192.2 0.8 copy.38
  193.0 0.4 copy-done
  193.4 0.0 copy-start.4
  193.4 0.8 copy.39
  194.2 0.3 copy-done.4
  194.5 0.7 copy.40
  (2 shorter events, 0.0 us)
Async XLA Ops:
  0.6 0.7 copy-start.9
  0.7 1.3 copy-start.8
  3.3 1.7 copy-start.3
  4.2 1.6 copy-start.2
  186.8 2.9 %copy-start.7 = (f32[128,256]{1,0:T(8,128)S(1)}, f32[128,256]{1,0:T(8,128)}, u32[]{:S(2)}) copy-start(f32[128,256]{1,0:T(8,128)} %get-tuple-element.21) | copy-start | bytes 393220
  188.1 2.3 %copy-start.6 = (f32[128,384]{1,0:T(8,128)S(1)}, f32[128,384]{1,0:T(8,128)}, u32[]{:S(2)}) copy-start(f32[128,384]{1,0:T(8,128)} %get-tuple-element.19) | copy-start | bytes 589828
  190.4 1.0 copy-start.5
  190.5 1.7 copy-start.1
  192.2 1.2 copy-start
  193.4 1.1 copy-start.4

commit v3 on v2

v3 whole, which is shorter than its diff:
```python
import functools

import jax
import jax.numpy as jnp
from jax import lax
from jax.experimental import pallas as pl
from jax.experimental.pallas import tpu as pltpu
from jax.sharding import PartitionSpec as P

EPS = 1e-05
MASKED = -1000000000.0
DH = 64
HALO = 64
F32 = jnp.float32
BF16 = jnp.bfloat16
GELU_C = 0.7978845608028654
GELU_A = 0.044715
MESH = pl.DeviceIdType.MESH
VMEM_LIMIT = 63 << 20


def mm(a, b):
    return lax.dot_general(a, b, (((1,), (0,)), ((), ())), preferred_element_type=F32)


def mm_nt(a, b):
    return lax.dot_general(a, b, (((1,), (1,)), ((), ())), preferred_element_type=F32)


def mm_tn(a, b):
    return lax.dot_general(a, b, (((0,), (0,)), ((), ())), preferred_element_type=F32)


def norm_parts(v):
    c = v - jnp.mean(v, axis=-1, keepdims=True)
    r = lax.rsqrt(jnp.mean(c * c, axis=-1, keepdims=True) + EPS)
    return c * r, r


def norm(v, gain):
    xhat, _ = norm_parts(v)
    return xhat * gain


def norm_back(v, gain, dn):
    xhat, r = norm_parts(v)
    dxh = dn * gain
    m1 = jnp.mean(dxh, axis=-1, keepdims=True)
    m2 = jnp.mean(dxh * xhat, axis=-1, keepdims=True)
    return r * (dxh - m1 - xhat * m2), jnp.sum(dn * xhat, axis=0, keepdims=True)


def lane_low(shape):
    return lax.broadcasted_iota(jnp.int32, shape, 1) < DH


def pair_join(a, b):
    return jnp.where(lane_low(a.shape), a, b)


def swap_halves(v):
    return pltpu.roll(v, DH, 1)


def attend(q2, k2, v2, mask, keep):
    low, lowq = lane_low(v2.shape), lane_low(q2.shape)
    one, zero = jnp.ones_like(v2), jnp.zeros_like(q2)
    outs = []
    for h in range(2):
        qh = jnp.where(lowq, q2, zero) if h == 0 else jnp.where(lowq, zero, q2)
        s = mask(mm_nt(qh, k2))
        e = jnp.exp(s - jnp.max(s, axis=-1, keepdims=True)).astype(BF16)
        keep(h, e)
        outs.append(mm(e, jnp.where(low, v2, one) if h == 0 else jnp.where(low, one, v2)))
    inv = 1.0 / swap_halves(pair_join(outs[1], outs[0]))
    return pair_join(*outs) * inv, inv


def attend_back(q2, k2, v2, do2, o2, inv, kept):
    low, lowq = lane_low(v2.shape), lane_low(q2.shape)
    one = jnp.ones_like(v2)
    scaled = do2.astype(F32) * inv.astype(F32)
    dob = scaled.astype(BF16)
    minus = (-swap_halves(dob.astype(F32) * o2.astype(F32))).astype(BF16)
    q_t, do_t = q2.T, dob.T
    dq, dk, dv = [], [], []
    for h in range(2):
        e = kept(h)
        rows = slice(h * DH, (h + 1) * DH)
        lhs = jnp.where(lowq, dob, minus) if h == 0 else jnp.where(lowq, minus, dob)
        dp = mm_nt(lhs, jnp.where(low, v2, one) if h == 0 else jnp.where(low, one, v2))
        ds = (dp * e.astype(F32)).astype(BF16)
        dq.append(mm(ds, k2))
        dv.append(mm(do_t[rows], e).astype(BF16))
        dk.append(mm(q_t[rows], ds).astype(BF16))
    return (pair_join(*dq) * (DH**-0.5)).astype(BF16), jnp.concatenate(dk, 0).T, jnp.concatenate(dv, 0).T


def gelu_parts(h):
    h2 = h * h
    half = 0.5 + 0.5 * jnp.tanh(h * (GELU_C + (GELU_C * GELU_A) * h2))
    u = h * half
    slope = half + u * ((1.0 - half) * (2.0 * GELU_C + (6.0 * GELU_C * GELU_A) * h2))
    return u, slope


def flip(i, bit):
    return i + bit - 2 * bit * lax.rem(lax.div(i, bit), 2)


def bit_of(i, bit):
    return lax.rem(lax.div(i, bit), 2)


def reversed_bits(i, count):
    out, bit = 0, 1
    while bit < count:
        out = 2 * out + (i // bit) % 2
        bit *= 2
    return out


class Links:
    def __init__(self, send, recv, local):
        self.send, self.recv, self.local = send, recv, local
        self.n = self.m = 0
        self.sent = []

    def take(self, count=1):
        self.n += count
        return self.n - count

    def remote(self, src, dst, device, at=None):
        at = self.take() if at is None else at
        return pltpu.make_async_remote_copy(
            src_ref=src, dst_ref=dst, send_sem=self.send.at[at], recv_sem=self.recv.at[at],
            device_id=device, device_id_type=MESH,
        )

    def here(self, src, dst):
        self.m += 1
        return pltpu.make_async_copy(src, dst, self.local.at[self.m - 1])


class Gather:
    def __init__(self, links, src, slot, at, planes=None):
        t, t2 = at["t"], at["t2"]
        depth = slot(t, None).shape[0]
        half = depth // 2
        whole = pl.ds(0, depth)
        mine = pl.ds(pl.multiple_of(at["b"] * half, half), half)
        other = pl.ds(pl.multiple_of((1 - at["b"]) * half, half), half)
        if src is None:
            self.own = []
        elif planes is None:
            self.own = [links.here(src, slot(t, whole))]
        else:
            self.own = [links.here(src.at[i], slot(t, whole, i)) for i in range(planes)]
        self.inner = src is None or planes is not None
        src = slot(t, whole) if self.inner else src
        self.core = links.remote(src, slot(t, whole), at["C"])
        self.over_y = links.remote(src.at[mine], slot(t, mine), at["Y"])
        self.over_z = links.remote(slot(t2, mine), slot(t2, mine), at["Z"][0])
        self.core_a = links.remote(slot(t2, mine), slot(t2, mine), at["C"])
        self.core_b = links.remote(slot(t2, other), slot(t2, other), at["C"])

    def start(self):
        for c in self.own:
            c.start()
        if self.inner:
            for c in self.own:
                c.wait()
        self.over_y.start()
        self.core.start()

    def step1(self):
        self.over_y.wait_recv()
        self.over_z.start()
        self.core_a.start()

    def step2(self):
        self.over_z.wait_recv()
        self.core_b.start()

    def ready(self, i):
        if i == 0 and not self.inner:
            for c in self.own:
                c.wait()
        if i == 1:
            self.core.wait_recv()
        if i == 3:
            self.core_a.wait_recv()
            self.core_b.wait_recv()

    def finish(self):
        for c in (self.core, self.over_y, self.over_z, self.core_a, self.core_b):
            c.wait_send()


class Reduce:
    def __init__(self, links, part, rc, ry, zb, zr, at):
        self.part, self.at = part, at
        self.rc, self.ry, self.zb, self.zr = rc, ry, zb, zr
        self.dp = zb.shape[0]
        self.core = [links.remote(part(at[f]), rc.at[j], at["C"]) for j, f in enumerate(("t1", "t3"))]
        self.over_y = links.remote(part(at["t2"]), ry, at["Y"])
        self.over_z = []
        off, m, bit, k = 0, self.dp, 1, 0
        self.kept = []
        while m > 1:
            m //= 2
            b = bit_of(at["d"], bit)
            keep, give = off + b * m, off + (1 - b) * m
            self.over_z.append(links.remote(zb.at[pl.ds(give, m)], zr[k], at["Z"][k]))
            self.kept.append((keep, m))
            off, bit, k = keep, 2 * bit, k + 1

    def core_send(self, j):
        self.core[j].start()

    def core_done(self):
        self.core[0].wait_recv()
        self.core[1].wait_recv()
        far, near = self.part(self.at["t2"]), self.part(self.at["t"])
        far[...] = (far[...].astype(F32) + self.rc[1].astype(F32)).astype(BF16)
        self.over_y.start()
        near[...] = (near[...].astype(F32) + self.rc[0].astype(F32)).astype(BF16)

    def y_done(self):
        self.over_y.wait_recv()
        near = self.part(self.at["t"])
        rows = self.zb.shape[1]
        for i in range(self.dp):
            where = pl.ds(i * rows, rows)
            total = near[where].astype(F32) + self.ry[where].astype(F32)
            self.zb[reversed_bits(i, self.dp)] = total.astype(BF16)
        self.over_z[0].start()

    def z_done(self, k, out=None):
        self.over_z[k].wait_recv()
        keep, m = self.kept[k]
        if k == len(self.over_z) - 1:
            out[...] = self.zb[keep].astype(F32) + self.zr[k][0].astype(F32)
        else:
            live = self.zb.at[pl.ds(keep, m)]
            live[...] = (live[...].astype(F32) + self.zr[k][...].astype(F32)).astype(BF16)
            self.over_z[k + 1].start()

    def rest_z(self, k, out):
        for j in range(k, len(self.over_z)):
            self.z_done(j, out)

    def finish(self):
        for c in self.core + [self.over_y] + self.over_z:
            c.wait_send()


class ReduceZ:
    def __init__(self, links, part, rc, ry, zb, zr, at):
        self.part, self.at = part, at
        self.rc, self.ry, self.zb, self.zr = rc, ry, zb, zr
        self.dp = zb.shape[1]
        self.core = [links.remote(part(at[f]), rc.at[j], at["C"]) for j, f in enumerate(("t1", "t3"))]
        self.over_z, self.kept = [], []
        off, m, bit, k = 0, self.dp, 1, 0
        while m > 1:
            m //= 2
            b = bit_of(at["d"], bit)
            keep, give = off + b * m, off + (1 - b) * m
            self.over_z.append(links.remote(zb.at[:, pl.ds(give, m)], zr[k], at["Z"][k]))
            self.kept.append((keep, m))
            off, bit, k = keep, 2 * bit, k + 1
        self.off = off
        self.over_y = links.remote(zb.at[0, off], ry, at["Y"])

    def core_send(self, j):
        self.core[j].start()

    def core_done(self):
        self.core[0].wait_recv()
        self.core[1].wait_recv()
        rows = self.zb.shape[2]
        for j, f in enumerate(("t2", "t")):
            part = self.part(self.at[f])
            for i in range(self.dp):
                where = pl.ds(i * rows, rows)
                total = part[where, :].astype(F32) + self.rc[1 - j, where, :].astype(F32)
                self.zb[j, reversed_bits(i, self.dp)] = total.astype(BF16)
        self.over_z[0].start()

    def z_done(self, k):
        self.over_z[k].wait_recv()
        keep, m = self.kept[k]
        for j in range(2):
            live = self.zb.at[j, pl.ds(keep, m)]
            live[...] = (live[...].astype(F32) + self.zr[k][j].astype(F32)).astype(BF16)
        (self.over_z[k + 1] if k + 1 < len(self.over_z) else self.over_y).start()

    def y_done(self, out):
        self.over_y.wait_recv()
        out[...] = self.zb[1, self.off].astype(F32) + self.ry[...].astype(F32)

    def finish(self):
        for c in self.core + [self.over_y] + self.over_z:
            c.wait_send()


def layers(names, *refs):
    ref = dict(zip(names, refs))
    R = lambda name: ref[name]
    p, d, t = lax.axis_index("pipe"), lax.axis_index("dp"), lax.axis_index("tensor")
    is_enc, is_dec = p == 0, p == 1
    dp = lax.axis_size("dp")
    t1, t2, t3 = flip(t, 1), flip(t, 2), 3 - t
    zbits = []
    while 2 ** len(zbits) < dp:
        zbits.append((p, flip(d, 2 ** len(zbits)), t))
    at = dict(t=t, t1=t1, t2=t2, t3=t3, d=d, b=bit_of(d, 1), C=(p, d, t1), Y=(p, d, t2), T=(p, d, t3), X=(1 - p, d, t), Z=zbits)
    rows, own, width = R("x").shape
    win, cwin = own + 2 * HALO, 2 * own + 2 * HALO
    slots = 4 * own
    tokens = rows * own
    hw = R("wa").shape[2] // 3
    fw = R("w1").shape[2]
    inner = t % 3 != 0
    scale = jnp.asarray(DH**-0.5, BF16)
    gain_ref, x_ref = R("gains"), R("x")
    side = 3 * own // 4
    copies_out = []

    def rowsl(r, n=own):
        return pl.ds(pl.multiple_of(r * n, n), n)

    def lanes(s, n=hw):
        return pl.ds(pl.multiple_of(s * n, n), n)

    def far_lanes(s):
        return pl.ds(pl.multiple_of(s * 2 * hw + hw, hw), hw)

    def in_row(r, span):
        return pl.ds(pl.multiple_of(r * slots + span.start, HALO), span.size)

    def near_first(i):
        return 2 * lax.rem(lax.div(t, 2) + lax.div(i, 2), 2) + lax.rem(lax.rem(t, 2) + lax.rem(i, 2), 2)

    def far_first(i):
        return 2 * lax.rem(lax.div(t, 2) + lax.rem(lax.div(i + 1, 2), 2), 2) + lax.rem(lax.rem(t, 2) + 1 - lax.div(i, 2), 2)

    def seg_row(side_, r, start):
        row = jnp.broadcast_to(R("segs")[side_, pl.ds(r, 1), :].astype(F32), (8, slots))
        return pltpu.roll(row, lax.rem(2 * slots - start, slots), 1)

    def seg_column(side_, r):
        row = seg_row(side_, r, t * own)[:1, :own]
        return jnp.broadcast_to(row, (128, own)).T

    def spread(column, n):
        return jnp.concatenate([column] * (n // 128), axis=1)

    links = Links(R("send"), R("recv"), R("local"))

    def by_shard(name, n=None):
        def slot(s, span, i=None):
            full = R(name).at[s] if span is None else R(name).at[s, span]
            return full if i is None else full.at[:, pl.ds(i * n, n)]

        return slot

    def by_columns(name, n):
        def slot(s, span):
            return R(name).at[:, lanes(s, n)] if span is None else R(name).at[span, lanes(s, n)]

        return slot

    g_wa = Gather(links, R("wa_h"), by_shard("wa", hw), at, 3)
    g_wo = Gather(links, R("wo_h"), by_shard("wo"), at)
    g_w1 = Gather(links, R("w1_h"), by_shard("w1"), at)
    g_w2 = Gather(links, R("w2_h"), by_shard("w2"), at)
    g_cq = Gather(links, R("cx_h").at[:, pl.ds(0, hw)], by_columns("cqw", hw), at)
    g_co = Gather(links, R("cx_h").at[:, pl.ds(hw, hw)], by_columns("cow", hw), at)
    c0_x = links.remote(R("cx_h"), R("c0").at[:, lanes(t, 2 * hw)], at["X"])
    g_c0 = Gather(links, None, by_columns("c0", 2 * hw), at)
    x_right = links.remote(x_ref.at[:, pl.ds(own - HALO, HALO)], R("xh").at[0], (p, d, lax.rem(t + 1, 4)))
    x_left = links.remote(x_ref.at[:, pl.ds(0, HALO)], R("xh").at[1], (p, d, lax.rem(t + 3, 4)))
    base_mem, base_memc, base_memt = links.take(rows), links.take(rows), links.take(rows)
    base_dmc, base_dmt, base_dmx = links.take(rows), links.take(rows), links.take(rows)
    block = pl.ds(pl.multiple_of(t * own, own), own)
    block1 = pl.ds(pl.multiple_of(t1 * own, own), own)
    edge_out = pl.ds(pl.multiple_of(lax.rem(own // 2 + side * t, slots), HALO), side)
    edge_in = pl.ds(pl.multiple_of(lax.rem(own // 2 + side * t3, slots), HALO), side)

    def mem_x(r):
        return links.remote(R("secs").at[rowsl(r)], R("memf").at[in_row(r, block)], at["X"], base_mem + r)

    def mem_c(r):
        return links.remote(R("memf").at[in_row(r, block)], R("memf").at[in_row(r, block)], at["C"], base_memc + r)

    def mem_t(r):
        return links.remote(R("memf").at[in_row(r, edge_out)], R("memf").at[in_row(r, edge_out)], at["T"], base_memt + r)

    def dm_rows(r, span):
        return R("dmf").at[in_row(r, span)]

    def dm_c(r):
        return links.remote(dm_rows(r, block1), R("rcc").at[r], at["C"], base_dmc + r)

    def dm_t(r):
        return links.remote(dm_rows(r, edge_in), R("rct").at[r], at["T"], base_dmt + r)

    def dm_x(r):
        return links.remote(R("dm").at[r], R("dm").at[r], at["X"], base_dmx + r)

    def by_rows(name, m):
        return lambda s: R(name).at[pl.ds(pl.multiple_of(s * width, width), width), pl.ds(0, m)]

    def by_lanes(name, m, row=0):
        return lambda s: R(name).at[pl.ds(row, width), lanes(s, m)]

    def reduce_of(name, part, kind=Reduce):
        zr = [R(f"zr{k}_{name}") for k in range(len(zbits))]
        return kind(links, part, R("rc_" + name), R("ry_" + name), R("zb_" + name), zr, at)

    r_w2 = reduce_of("w2", by_rows("memf", fw))
    r_w1 = reduce_of("w1", by_rows("dmf", fw), ReduceZ)
    r_wo = reduce_of("wo", by_lanes("dwo", hw))
    r_wa = reduce_of("wa", by_rows("cp", 3 * hw))
    r_c0 = reduce_of("c0", by_lanes("kv", 2 * hw))
    r_c1 = reduce_of("c1", by_lanes("kv", 2 * hw, width))
    c0_back = links.remote(R("dc0"), R("dc0r"), at["X"])
    dn_right = links.remote(R("dhs").at[1], R("dhr").at[0], (p, d, lax.rem(t + 1, 4)))
    dn_left = links.remote(R("dhs").at[0], R("dhr").at[1], (p, d, lax.rem(t + 3, 4)))
    gain_links = [links.remote(R("dgs").at[k], R("dgr").at[k], dev) for k, dev in enumerate([at["C"], at["Y"]] + zbits)]

    @pl.when(is_dec)
    def _():
        for at_t, start in ((0, 2 * own), (1, 2 * own + side), (3, 2 * own - 2 * HALO)):
            @pl.when(t == at_t)
            def _():
                for r in range(rows):
                    R("memf")[pl.ds(r * slots + start, 2 * HALO), :] = jnp.zeros((2 * HALO, width), BF16)

    barrier = pltpu.get_barrier_semaphore()
    partners = [at["C"], at["Y"], at["T"], at["X"]] + zbits
    for dev in partners:
        pl.semaphore_signal(barrier, inc=1, device_id=dev, device_id_type=MESH)
    pl.semaphore_wait(barrier, len(partners))

    pl.when(t < 3)(x_right.start)
    pl.when(t > 0)(x_left.start)
    g_wa.start()
    g_wo.start()

    @pl.when(is_enc)
    def _():
        g_w1.start()
        g_w2.start()
        c0_x.start()

    @pl.when(is_dec)
    def _():
        g_cq.start()
        g_co.start()
        g_w2.start()
        g_w1.start()

    nw_ref, bias_ref = R("nw"), R("bias")
    gain0, gain1, gain2 = gain_ref[0], gain_ref[1], gain_ref[2]
    for r in range(rows):
        nw_ref[pl.ds(r * win + HALO, own), :] = norm(x_ref[r].astype(F32), gain0).astype(BF16)
        keys = seg_row(p, r, lax.rem(t * own + slots - HALO, slots))[:1, :win]
        same = spread(seg_column(p, r), win) == keys
        qpos = lax.broadcasted_iota(jnp.int32, (own, win), 0)
        kpos = lax.broadcasted_iota(jnp.int32, (own, win), 1) - HALO
        before = kpos - qpos <= jnp.where(is_enc, 4 * win, 0)
        bias_ref[r] = jnp.where(same & before, 0.0, MASKED)

    @pl.when(t == 0)
    def _():
        R("xh")[0] = jnp.zeros((rows, HALO, width), BF16)

    @pl.when(t == 3)
    def _():
        R("xh")[1] = jnp.zeros((rows, HALO, width), BF16)

    pl.when(t > 0)(x_right.wait_recv)
    pl.when(t < 3)(x_left.wait_recv)
    for r in range(rows):
        nw_ref[pl.ds(r * win, HALO), :] = norm(R("xh")[0, r].astype(F32), gain0).astype(BF16)
        nw_ref[pl.ds(r * win + HALO + own, HALO), :] = norm(R("xh")[1, r].astype(F32), gain0).astype(BF16)

    def after_pair(i):
        @pl.when(i == 1)
        def _():
            g_wa.step1()
            g_wo.step1()

            @pl.when(is_dec)
            def _():
                c0_x.wait_recv()
                g_c0.start()

            g_wa.step2()

        @pl.when(i == 2)
        def _():
            pl.when(is_enc)(g_w1.step1)

            @pl.when(is_dec)
            def _():
                g_cq.step1()
                g_co.step1()

            g_wo.step2()

        @pl.when(i == 3)
        def _():
            pl.when(is_enc)(g_w2.step1)
            pl.when(is_dec)(g_w2.step1)

    def wait_ready(i, *weights):
        for k in range(4):
            @pl.when(i == k)
            def _():
                for w in weights:
                    w.ready(k)

    q_ref, k_ref, v_ref, p_ref, o_ref, inv_ref = R("q"), R("k"), R("v"), R("p"), R("o"), R("inv")

    def self_pair(i, _):
        s = near_first(i)
        wait_ready(i, g_wa)
        packed = mm(nw_ref[...], R("wa")[s])
        for r in range(rows):
            q_ref[s, r] = packed[r * win + HALO : r * win + HALO + own, :hw].astype(BF16) * scale
            k_ref[s, r] = packed[r * win : (r + 1) * win, hw : 2 * hw].astype(BF16)
            v_ref[s, r] = packed[r * win : (r + 1) * win, 2 * hw :].astype(BF16)
        for r in range(rows):
            def keep(h, e):
                p_ref[s, r, h] = e

            o2, inv = attend(q_ref[s, r], k_ref[s, r], v_ref[s, r], lambda scores: scores + bias_ref[r], keep)
            o_ref[pl.ds(r * own, own), lanes(s)] = o2.astype(BF16)
            inv_ref[pl.ds(r * own, own), lanes(s)] = inv.astype(BF16)
        after_pair(i)
        return 0

    lax.fori_loop(0, 4, self_pair, 0)
    for k in range(4):
        g_wo.ready(k)
    r1_ref, r2_ref, n2_ref, n3_ref = R("r1"), R("r2"), R("n2"), R("n3")
    u_ref, gp_ref, sec_ref = R("u"), R("gp"), R("secs")
    acc_ref, g_ref, gb_ref, do_ref = R("acc"), R("g"), R("gb"), R("do")
    first = mm(o_ref[...], R("wo")[...].reshape(4 * hw, width))
    for r in range(rows):
        r1_ref[pl.ds(r * own, own), :] = x_ref[r].astype(F32) + first[r * own : (r + 1) * own]
    n2_ref[...] = norm(r1_ref[...], gain1).astype(BF16)

    @pl.when(is_enc)
    def _():
        r2_ref[...] = r1_ref[...]

        def feed(i, rs):
            s = near_first(i)
            u, gp = gelu_parts(mm(n2_ref[rs, :], R("w1")[s]))
            u = u.astype(BF16)
            u_ref[s, rs, :] = u
            gp_ref[s, rs, :] = gp.astype(BF16)
            r2_ref[rs, :] += mm(u, R("w2")[s])

        def near(i, _):
            wait_ready(i, g_w1, g_w2)
            feed(i, pl.ds(0, tokens))
            pl.when(i == 0)(g_w1.step2)
            pl.when(i == 1)(g_w2.step2)
            return 0

        lax.fori_loop(0, 2, near, 0)

        def row(r, _):
            rs = rowsl(r)

            def far(i, _):
                pl.when(r == 0)(lambda: wait_ready(i, g_w1, g_w2))
                feed(i, rs)
                return 0

            lax.fori_loop(2, 4, far, 0)
            sec_ref[rs, :] = norm(r2_ref[rs, :], gain2).astype(BF16)
            mem_x(r).start()
            return 0

        lax.fori_loop(0, rows, row, 0)

    cstart = pl.multiple_of(jnp.minimum(t * (own - HALO), slots - cwin), HALO)
    cwindow = pl.ds(cstart, cwin)
    kv_ref, cq_ref, cp_ref, dkv_ref, cinv_ref = R("kv"), R("cq"), R("cp"), R("dkv"), R("cinv")
    c0_ref, cqw_ref, cow_ref, oc_ref, cot_ref = R("c0"), R("cqw"), R("cow"), R("oc"), R("cot")
    cols, keys_ref = R("cols"), R("keys")
    half = 4 * hw

    @pl.when(is_dec)
    def _():
        g_cq.step2()
        g_co.step2()
        g_c0.step1()
        g_w1.step1()
        kv_ref[...] = jnp.zeros_like(kv_ref)
        R("dmf")[...] = jnp.zeros_like(R("dmf"))
        for r in range(rows):
            cols[r] = seg_column(1, r)
            keys_ref[r] = seg_row(0, r, cstart)[:, :cwin]
        g_w2.step2()
        for k in range(4):
            g_cq.ready(k)
        cq_ref[...] = mm(n2_ref[...], cqw_ref[...]).astype(BF16) * scale
        g_c0.step2()
        g_w1.step2()
        for k in range(4):
            g_w2.ready(k)

        def early(s, _):
            gp_ref[s] = mm_nt(cot_ref[...], R("w2")[s]).astype(BF16)
            return 0

        lax.fori_loop(0, 4, early, 0)
        for k in range(4):
            g_w1.ready(k)
            g_co.ready(k)
            g_c0.ready(k)

        def row(r, _):
            rs = rowsl(r)

            def project(span):
                for j in range(2):
                    kv = mm(R("memf")[in_row(r, span), :], c0_ref[:, j * half : (j + 1) * half])
                    kv_ref[span, j * half : (j + 1) * half] = kv.astype(BF16)

            mem_x(r).wait_recv()
            mem_c(r).start()
            pl.when(inner)(mem_t(r).start)
            project(block)
            mem_c(r).wait_recv()
            project(block1)

            @pl.when(inner)
            def _():
                mem_t(r).wait_recv()
                project(edge_in)

            def cross(i, _):
                for s in (2 * i, 2 * i + 1):
                    def keep(h, e):
                        cp_ref[rowsl(2 * s + h), :] = e

                    def mask(scores):
                        same = spread(cols[r], cwin) == keys_ref[r, pl.ds(0, 1), :]
                        return jnp.where(same, scores, MASKED)

                    o2, inv = attend(cq_ref[rs, lanes(s)], kv_ref[cwindow, lanes(2 * s)], kv_ref[cwindow, lanes(2 * s + 1)], mask, keep)
                    oc_ref[rs, lanes(s)] = o2.astype(BF16)
                    cinv_ref[:, lanes(s)] = inv.astype(BF16)
                return 0

            lax.fori_loop(0, 2, cross, 0)
            r2_ref[rs, :] = r1_ref[rs, :] + mm_nt(oc_ref[rs, :], cow_ref[...])
            n3_ref[rs, :] = norm(r2_ref[rs, :], gain2).astype(BF16)
            dn = pl.ds(0, own)
            acc_ref[dn, :] = jnp.zeros((own, width), F32)
            g_ref[rs, :] = r2_ref[rs, :]

            def feed(s, _):
                u, gp = gelu_parts(mm(n3_ref[rs, :], R("w1")[s]))
                u = u.astype(BF16)
                u_ref[s, rs, :] = u
                g_ref[rs, :] += mm(u, R("w2")[s])
                dh = (gp_ref[s, rs, :].astype(F32) * gp).astype(BF16)
                gp_ref[s, rs, :] = dh
                acc_ref[dn, :] += mm_nt(dh, R("w1")[s])
                return 0

            lax.fori_loop(0, 4, feed, 0)
            sec_ref[rs, :] = g_ref[rs, :].astype(BF16)
            dx, dg = norm_back(r2_ref[rs, :], gain2, acc_ref[dn, :])
            R("dg")[r, pl.ds(2, 1), :] = dg
            g2 = cot_ref[rs, :].astype(F32) + dx
            g_ref[rs, :] = g2
            gb_ref[rs, :] = g2.astype(BF16)
            do_ref[rs, :] = mm(gb_ref[rs, :], cow_ref[...]).astype(BF16)
            ws = pl.ds(pl.multiple_of(r * cwin, HALO), cwin)

            def back(i, _):
                for s in (2 * i, 2 * i + 1):
                    dq, dk, dv = attend_back(
                        cq_ref[rs, lanes(s)], kv_ref[cwindow, lanes(2 * s)], kv_ref[cwindow, lanes(2 * s + 1)],
                        do_ref[rs, lanes(s)], oc_ref[rs, lanes(s)], cinv_ref[:, lanes(s)], lambda h: cp_ref[rowsl(2 * s + h), :],
                    )
                    cq_ref[rs, lanes(s)] = dq
                    dkv_ref[ws, lanes(2 * s)] = dk
                    dkv_ref[ws, lanes(2 * s + 1)] = dv
                return 0

            lax.fori_loop(0, 2, back, 0)
            R("dmf")[in_row(r, cwindow), :] = mm_nt(dkv_ref[ws, :], c0_ref[...]).astype(BF16)
            dm_c(r).start()
            pl.when(inner)(dm_t(r).start)
            dx, dg = norm_back(r1_ref[rs, :], gain1, mm_nt(cq_ref[rs, :], cqw_ref[...]))
            R("dg")[r, pl.ds(1, 1), :] = dg
            g_ref[rs, :] += dx
            dm_c(r).wait_recv()
            acc_ref[dn, :] = R("dmf")[in_row(r, block), :].astype(F32) + R("rcc")[r].astype(F32)

            @pl.when(inner)
            def _():
                dm_t(r).wait_recv()
                place = pl.ds(pl.multiple_of((2 - t) * (own - side), HALO), side)
                acc_ref[place, :] += R("rct")[r].astype(F32)

            R("dm")[r] = acc_ref[dn, :].astype(BF16)
            dm_x(r).start()
            return 0

        lax.fori_loop(0, rows, row, 0)
        for r in range(rows):
            dm_c(r).wait_send()
            pl.when(inner)(dm_t(r).wait_send)

        def sends(reduction, i):
            pl.when(i == 0)(lambda: reduction.core_send(0))
            pl.when(i == 1)(lambda: reduction.core_send(1))

        def c0_grad(i, _):
            s = far_first(i)
            total = mm_tn(R("memf")[in_row(0, cwindow), :], dkv_ref[pl.ds(0, cwin), lanes(s, 2 * hw)])
            for r in range(1, rows):
                total += mm_tn(R("memf")[in_row(r, cwindow), :], dkv_ref[pl.ds(r * cwin, cwin), lanes(s, 2 * hw)])
            r_c0.part(s)[...] = total.astype(BF16)
            sends(r_c0, i)
            return 0

        lax.fori_loop(0, 4, c0_grad, 0)
        dcq = mm_tn(n2_ref[...], cq_ref[...]).astype(BF16)
        dco = mm_tn(gb_ref[...], oc_ref[...]).astype(BF16)
        for s in range(4):
            r_c1.part(s)[:, :hw] = dcq[:, s * hw : (s + 1) * hw]
            r_c1.part(s)[:, hw:] = dco[:, s * hw : (s + 1) * hw]
        r_c1.core_send(0)
        r_c1.core_send(1)
        r_c0.core_done()

        for r in range(rows):
            mem_c(r).wait_send()
            pl.when(inner)(mem_t(r).wait_send)

        def w2_grad(i, _):
            s = far_first(i)
            r_w2.part(s)[...] = mm_tn(cot_ref[...], u_ref[s]).astype(BF16)
            sends(r_w2, i)
            return 0

        lax.fori_loop(0, 4, w2_grad, 0)
        r_c1.core_done()

        def w1_grad(i, _):
            s = far_first(i)
            r_w1.part(s)[...] = mm_tn(n3_ref[...], gp_ref[s]).astype(BF16)
            sends(r_w1, i)
            pl.when(i == 0)(r_w2.core_done)
            return 0

        lax.fori_loop(0, 4, w1_grad, 0)

    @pl.when(is_enc)
    def _():
        def row(r, _):
            rs = rowsl(r)
            dm_x(r).wait_recv()
            dx, dg = norm_back(r2_ref[rs, :], gain2, R("dm")[r].astype(F32))
            R("dg")[r, pl.ds(2, 1), :] = dg
            g_ref[rs, :] = dx
            gb_ref[rs, :] = dx.astype(BF16)
            return 0

        lax.fori_loop(0, rows, row, 0)

        def sends(reduction, i):
            pl.when(i == 0)(lambda: reduction.core_send(0))
            pl.when(i == 1)(lambda: reduction.core_send(1))

        def w2_grad(i, _):
            s = far_first(i)
            r_w2.part(s)[...] = mm_tn(gb_ref[...], u_ref[s]).astype(BF16)
            sends(r_w2, i)
            return 0

        lax.fori_loop(0, 4, w2_grad, 0)
        dn = pl.ds(0, tokens)
        acc_ref[dn, :] = jnp.zeros((tokens, width), F32)

        def w1_grad(i, _):
            s = far_first(i)
            dh = (mm_nt(gb_ref[...], R("w2")[s]) * gp_ref[s].astype(F32)).astype(BF16)
            r_w1.part(s)[...] = mm_tn(n2_ref[...], dh).astype(BF16)
            sends(r_w1, i)
            acc_ref[dn, :] += mm_nt(dh, R("w1")[s])
            pl.when(i == 0)(r_w2.core_done)
            return 0

        lax.fori_loop(0, 4, w1_grad, 0)
        dx, dg = norm_back(r1_ref[...], gain1, acc_ref[dn, :])
        R("dg")[0, pl.ds(1, 1), :] = dg
        for r in range(1, rows):
            R("dg")[r, pl.ds(1, 1), :] = jnp.zeros_like(dg)
        g_ref[...] += dx

    sec_out = links.here(sec_ref, R("sec"))
    sec_out.start()
    r_w1.core_done()
    gb_ref[...] = g_ref[...].astype(BF16)
    R("dwo")[...] = mm_tn(gb_ref[...], o_ref[...]).astype(BF16)
    r_wo.core_send(0)
    r_wo.core_send(1)
    do_ref[...] = mm_nt(gb_ref[...], R("wo")[...].reshape(4 * hw, width)).astype(BF16)
    acc_ref[...] = jnp.zeros_like(acc_ref)
    dqkv_ref = R("dqkv")
    for r in range(rows):
        dqkv_ref[pl.ds(r * win, HALO), :hw] = jnp.zeros((HALO, hw), BF16)
        dqkv_ref[pl.ds(r * win + HALO + own, HALO), :hw] = jnp.zeros((HALO, hw), BF16)

    def self_back(i, _):
        s = far_first(i)
        for r in range(rows):
            rs = pl.ds(r * own, own)
            dq, dk, dv = attend_back(
                q_ref[s, r], k_ref[s, r], v_ref[s, r], do_ref[rs, lanes(s)], o_ref[rs, lanes(s)], inv_ref[rs, lanes(s)],
                lambda h: p_ref[s, r, h],
            )
            dqkv_ref[pl.ds(r * win + HALO, own), :hw] = dq
            dqkv_ref[pl.ds(r * win, win), hw : 2 * hw] = dk
            dqkv_ref[pl.ds(r * win, win), 2 * hw :] = dv
        r_wa.part(s)[...] = mm_tn(nw_ref[...], dqkv_ref[...]).astype(BF16)
        acc_ref[...] += mm_nt(dqkv_ref[...], R("wa")[s])

        @pl.when(i == 0)
        def _():
            r_wa.core_send(0)
            r_wo.core_done()

        @pl.when(i == 1)
        def _():
            r_wa.core_send(1)
            pl.when(is_dec)(r_c0.y_done)

        @pl.when(i == 2)
        def _():
            pl.when(is_enc)(r_w2.y_done)

        @pl.when(i == 3)
        def _():
            @pl.when(is_dec)
            def _():
                r_c1.y_done()
                r_c0.z_done(0, R("dc0"))

        return 0

    lax.fori_loop(0, 4, self_back, 0)
    for r in range(rows):
        R("dhs")[0, r] = acc_ref[pl.ds(r * win, HALO), :].astype(BF16)
        R("dhs")[1, r] = acc_ref[pl.ds(r * win + HALO + own, HALO), :].astype(BF16)
    pl.when(t < 3)(dn_right.start)
    pl.when(t > 0)(dn_left.start)
    r_wa.core_done()
    r_w1.z_done(0)

    @pl.when(t == 0)
    def _():
        R("dhr")[0] = jnp.zeros((rows, HALO, width), BF16)

    @pl.when(t == 3)
    def _():
        R("dhr")[1] = jnp.zeros((rows, HALO, width), BF16)

    pl.when(t > 0)(dn_right.wait_recv)
    pl.when(t < 3)(dn_left.wait_recv)
    for r in range(rows):
        lo, hi = pl.ds(r * win + HALO, HALO), pl.ds(r * win + own, HALO)
        acc_ref[lo, :] += R("dhr")[0, r].astype(F32)
        acc_ref[hi, :] += R("dhr")[1, r].astype(F32)
    total = jnp.zeros((1, width), F32)
    for r in range(rows):
        rs = pl.ds(r * own, own)
        dx, dg = norm_back(x_ref[r].astype(F32), gain0, acc_ref[pl.ds(r * win + HALO, own), :])
        gb_ref[rs, :] = (g_ref[rs, :] + dx).astype(BF16)
        total += dg
    gx_out = links.here(gb_ref, R("gx"))
    gx_out.start()
    R("dgs")[0] = jnp.zeros((8, width), F32)
    R("dgs")[0, pl.ds(0, 1), :] = total
    R("dgs")[0, pl.ds(1, 2), :] = sum(R("dg")[r, pl.ds(1, 2), :] for r in range(rows))
    gain_links[0].start()

    def gain_step(k):
        gain_links[k].wait_recv()
        if k + 1 < len(gain_links):
            R("dgs")[k + 1] = R("dgs")[k] + R("dgr")[k]
            gain_links[k + 1].start()
        else:
            R("dgain")[...] = pltpu.roll(R("dgs")[k] + R("dgr")[k], lax.rem(width - d * (width // dp), width), 1)

    pl.when(is_dec)(r_w2.y_done)
    r_wo.y_done()
    r_w2.z_done(0, R("dw2_o"))
    gain_step(0)

    @pl.when(is_dec)
    def _():
        r_c0.rest_z(1, R("dc0"))
        c0_back.start()
        r_c1.z_done(0, R("dc"))

    for k in range(1, len(zbits)):
        r_w1.z_done(k)
    r_wo.z_done(0, R("dwo_o"))
    gain_step(1)
    r_w2.rest_z(1, R("dw2_o"))
    r_wa.y_done()
    gain_step(2)
    pl.when(is_dec)(lambda: r_c1.rest_z(1, R("dc")))
    r_wo.rest_z(1, R("dwo_o"))
    r_w1.y_done(R("dw1_o"))
    r_wa.z_done(0, R("da_o"))
    for k in range(3, len(gain_links)):
        gain_step(k)
    r_wa.rest_z(1, R("da_o"))

    sec_out.wait()
    gx_out.wait()
    for g in (g_wa, g_wo, g_w1, g_w2):
        g.finish()
    for g in (r_w2, r_w1, r_wo, r_wa):
        g.finish()
    for c in gain_links:
        c.wait_send()
    pl.when(t < 3)(x_right.wait_send)
    pl.when(t > 0)(x_left.wait_send)
    pl.when(t < 3)(dn_right.wait_send)
    pl.when(t > 0)(dn_left.wait_send)

    @pl.when(is_enc)
    def _():
        c0_x.wait_send()
        for r in range(rows):
            mem_x(r).wait_send()
        c0_back.wait_recv()
        R("dc")[...] = R("dc0r")[...]

    @pl.when(is_dec)
    def _():
        for g in (g_cq, g_co, g_c0, r_c0, r_c1):
            g.finish()
        for r in range(rows):
            dm_x(r).wait_send()
        c0_back.wait_send()


def arrange(aligned, sec, gx, dgain, da, dwo, dc, dw1, dw2, sec_o, gx_o, dgain_o, da_o, dwo_o, dc_o, dw1_o, dw2_o):
    share, hw = dwo.shape
    sec_o[...] = sec[...]
    gx_o[...] = gx[...]
    for i in range(3):
        dgain_o[i] = dgain[pl.ds(i, 1), pl.ds(0, share)]
        da_o[i] = da[:, pl.ds(i * hw, hw)]
    for i in range(2):
        dc_o[:, i, :] = dc[:, pl.ds(i * hw, hw)]
    dw1_o[...] = dw1[...]
    dwo_o[...] = dwo[...].T if aligned else dwo[...]
    dw2_o[...] = dw2[...].T if aligned else dw2[...]


def body(embeds, segments, cotangent, norm_gains, attn_in, attn_out, cross_proj, ffn_in, ffn_out):
    dp = lax.axis_size("dp")
    rows, own, width = embeds.shape[1:]
    slots = segments.shape[2]
    hw = attn_in.shape[3]
    fw = ffn_in.shape[2]
    win = own + 2 * HALO
    cwin = 2 * own + 2 * HALO
    tokens = rows * own
    side = 3 * own // 4
    share = width // dp
    zsteps = (dp - 1).bit_length()

    ins = dict(
        x=embeds[0], segs=segments, gains=norm_gains.transpose(1, 0, 2), cot=cotangent.reshape(tokens, width),
        wa_h=attn_in[0].transpose(1, 0, 2), wo_h=attn_out[0], w1_h=ffn_in[0], w2_h=ffn_out[0],
        cx_h=cross_proj[0].reshape(width, 2 * hw),
    )
    outs = dict(
        sec=((tokens, width), BF16), gx=((tokens, width), BF16), dgain=((8, width), F32),
        da_o=((share, 3 * hw), F32), dwo_o=((share, hw), F32), dc=((share, 2 * hw), F32),
        dw1_o=((share, fw), F32), dw2_o=((share, fw), F32),
    )
    vm = dict(
        wa=((4, width, 3 * hw), BF16), wo=((4, hw, width), BF16), w1=((4, width, fw), BF16), w2=((4, fw, width), BF16),
        c0=((width, 8 * hw), BF16), cqw=((width, 4 * hw), BF16), cow=((width, 4 * hw), BF16),
        xh=((2, rows, HALO, width), BF16), nw=((rows * win, width), BF16),
        q=((4, rows, own, hw), BF16), k=((4, rows, win, hw), BF16), v=((4, rows, win, hw), BF16),
        p=((4, rows, 2, own, win), BF16), o=((tokens, width), BF16), inv=((tokens, width), BF16), bias=((rows, own, win), F32),
        r1=((tokens, width), F32), r2=((tokens, width), F32), n2=((tokens, width), BF16), n3=((tokens, width), BF16),
        u=((4, tokens, fw), BF16), gp=((4, tokens, fw), BF16), secs=((tokens, width), BF16),
        acc=((rows * win, width), F32), g=((tokens, width), F32), gb=((tokens, width), BF16), do=((tokens, width), BF16),
        memf=((max(rows * slots, 4 * width), max(width, fw)), BF16), kv=((slots, 8 * hw), BF16), cq=((tokens, width), BF16),
        cp=((max(8 * own, 4 * width), cwin), BF16), cinv=((own, width), BF16), oc=((tokens, width), BF16),
        cols=((rows, own, 128), F32), keys=((rows, 8, cwin), F32),
        dkv=((rows * cwin, 8 * hw), BF16), dmf=((max(rows * slots, 4 * width), max(width, fw)), BF16),
        rcc=((rows, own, width), BF16), rct=((rows, side, width), BF16), dm=((rows, own, width), BF16),
        dg=((rows, 8, width), F32),
        dqkv=((rows * win, 3 * hw), BF16), dhs=((2, rows, HALO, width), BF16), dhr=((2, rows, HALO, width), BF16),
        dgs=((2 + zsteps, 8, width), F32), dgr=((2 + zsteps, 8, width), F32),
        dwo=((width, 4 * hw), BF16),
        dc0=((share, 2 * hw), F32), dc0r=((share, 2 * hw), F32),
    )
    for name, m in dict(w2=fw, w1=fw, wo=hw, wa=3 * hw, c0=2 * hw, c1=2 * hw).items():
        both = (2,) if name == "w1" else ()
        vm["rc_" + name] = ((2, width, m), BF16)
        vm["ry_" + name] = ((share if both else width, m), BF16)
        vm["zb_" + name] = (both + (dp, share, m), BF16)
        for k in range(zsteps):
            vm[f"zr{k}_{name}"] = (both + (dp >> (k + 1), share, m), BF16)
    copies = 140 + 8 * zsteps
    sems = dict(send=pltpu.SemaphoreType.DMA((copies,)), recv=pltpu.SemaphoreType.DMA((copies,)), local=pltpu.SemaphoreType.DMA((12,)))
    in_hbm = {"wa_h", "wo_h", "w1_h", "w2_h", "cx_h"}
    out_hbm = {"sec", "gx"}
    results = pl.pallas_call(
        functools.partial(layers, list(ins) + list(outs) + list(vm) + list(sems)),
        name="layers",
        out_shape=[jax.ShapeDtypeStruct(*o) for o in outs.values()],
        in_specs=[pl.BlockSpec(memory_space=pl.ANY if n in in_hbm else pltpu.VMEM) for n in ins],
        out_specs=[pl.BlockSpec(memory_space=pl.ANY if n in out_hbm else pltpu.VMEM) for n in outs],
        scratch_shapes=[pltpu.VMEM(*s) for s in vm.values()] + list(sems.values()),
        compiler_params=pltpu.CompilerParams(vmem_limit_bytes=VMEM_LIMIT, collective_id=0, has_side_effects=True),
    )(*ins.values())
    aligned = share % 128 == 0
    flat, turned = (share, hw), (hw, share)
    sec, gx, dgain, da, dwo, dc, dw1, dw2 = pl.pallas_call(
        functools.partial(arrange, aligned),
        name="arrange",
        out_shape=[
            jax.ShapeDtypeStruct((tokens, width), BF16),
            jax.ShapeDtypeStruct((tokens, width), BF16),
            jax.ShapeDtypeStruct((3, 1, share), F32),
            jax.ShapeDtypeStruct((3, share, hw), F32),
            jax.ShapeDtypeStruct((hw, share) if aligned else (share, hw), F32),
            jax.ShapeDtypeStruct((share, 2, hw), F32),
            jax.ShapeDtypeStruct((share, fw), F32),
            jax.ShapeDtypeStruct((fw, share) if aligned else (share, fw), F32),
        ],
        in_specs=[pl.BlockSpec(memory_space=pltpu.VMEM)] * 8,
        out_specs=[pl.BlockSpec(memory_space=pltpu.VMEM)] * 8,
    )(*results)
    if not aligned:
        dwo, dw2 = dwo.T, dw2.T
    return (
        sec.reshape(1, rows, own, width), gx.reshape(1, rows, own, width), dgain.transpose(1, 0, 2),
        da.transpose(1, 0, 2)[None], dwo[None], dc[None], dw1[None], dw2[None],
    )


def solution(mesh):
    return jax.shard_map(
        body,
        mesh=mesh,
        in_specs=(
            P("pipe", "dp", "tensor", None),
            P(None, "dp", None),
            P("dp", "tensor", None),
            P("pipe", None, None),
            P("pipe", None, None, "tensor"),
            P("pipe", "tensor", None),
            P("pipe", None, None, "tensor"),
            P("pipe", None, "tensor"),
            P("pipe", "tensor", None),
        ),
        out_specs=(
            P("pipe", "dp", "tensor", None),
            P("pipe", "dp", "tensor", None),
            P("pipe", None, "dp"),
            P("pipe", "dp", None, "tensor"),
            P("pipe", "tensor", "dp"),
            P("pipe", "dp", None, "tensor"),
            P("pipe", "dp", "tensor"),
            P("pipe", "tensor", "dp"),
        ),
        check_vma=False,
    )
```

time: 196 us -> 157 us (0.80)
  the two profiles are of different devices: /device:TPU:19 before, /device:TPU:0 now
where the time goes in v3:
time: 157 us; the launch traced here: 155 us
  Pallas kernels  153 us (97%)
  local copies, waits for them, and re-layouts  1.69 us (1%)
    pallas_call x1, Pallas kernels, body(): pl.pallas_call(functools.partial(layers, list(ins) + list(outs) + list(vm...  150 us

profile of v3, /device:TPU:0, one launch (start us, length us, event | category | flops | bytes accessed | tf_op | source)
XLA Modules:
  0.0 155.0 jit_solution(5446112605302975277)
XLA Ops:
  0.6 1.7 %copy.19 = bf16[64,8,2,128]{3,1,2,0:T(8,128)(2,1)} copy(bf16[64,8,2,128]{3,2,1,0:T(2,128)(2,1)} %bitcast.30) | data formatting | bytes 524288
  2.3 149.8 %layers.1 = (bf16[512,512]{1,0:T(8,128)(2,1)}, bf16[512,512]{1,0:T(8,128)(2,1)}, f32[8,512]{1,0:T(8,128)}, f32[128,384]{1,0:T(8,128)}, f32[128,128]{1,0:T(8,128)...) custom-call(bf16[2,256,512]{2,1,0:T(8,128)(2,1)} %bitcast.25, s32[2,2,1024]{2,1,0:T(2,128)} %refs_1_.1, ...), custom_call_target="tpu_custom_call" | custom-call | tf_op jit(solution)/shard_map/layers/pallas_call | solution.py:1035
  152.1 2.9 %arrange.1 = (bf16[512,512]{1,0:T(8,128)(2,1)}, bf16[512,512]{1,0:T(8,128)(2,1)}, f32[3,1,128]{2,1,0:T(1,128)}, f32[3,128,128]{2,1,0:T(8,128)}, f32[128,128]{1,0...) custom-call(bf16[512,512]{1,0:T(8,128)(2,1)} %get-tuple-element.24.sec, ...), custom_call_target="tpu_custom_call" | custom-call | tf_op jit(solution)/shard_map/arrange/pallas_call | solution.py:1046

commit v4 on v3

--- a/solution.py
+++ b/solution.py
@@ -143,13 +143,11 @@
 
 
 class Gather:
-    def __init__(self, links, src, slot, at, planes=None):
+    def __init__(self, links, src, slot, depth, at, pieces=1, planes=None):
         t, t2 = at["t"], at["t2"]
-        depth = slot(t, None).shape[0]
         half = depth // 2
+        n = half // pieces
         whole = pl.ds(0, depth)
-        mine = pl.ds(pl.multiple_of(at["b"] * half, half), half)
-        other = pl.ds(pl.multiple_of((1 - at["b"]) * half, half), half)
         if src is None:
             self.own = []
         elif planes is None:
@@ -159,10 +157,14 @@
         self.inner = src is None or planes is not None
         src = slot(t, whole) if self.inner else src
         self.core = links.remote(src, slot(t, whole), at["C"])
-        self.over_y = links.remote(src.at[mine], slot(t, mine), at["Y"])
-        self.over_z = links.remote(slot(t2, mine), slot(t2, mine), at["Z"][0])
-        self.core_a = links.remote(slot(t2, mine), slot(t2, mine), at["C"])
-        self.core_b = links.remote(slot(t2, other), slot(t2, other), at["C"])
+        self.over_y, self.over_z, self.core_a, self.core_b = [], [], [], []
+        for i in range(pieces):
+            mine = pl.ds(pl.multiple_of(at["b"] * half + i * n, n), n)
+            other = pl.ds(pl.multiple_of((1 - at["b"]) * half + i * n, n), n)
+            self.over_y.append(links.remote(src.at[mine], slot(t, mine), at["Y"]))
+            self.over_z.append(links.remote(slot(t2, mine), slot(t2, mine), at["Z"][0]))
+            self.core_a.append(links.remote(slot(t2, mine), slot(t2, mine), at["C"]))
+            self.core_b.append(links.remote(slot(t2, other), slot(t2, other), at["C"]))
 
     def start(self):
         for c in self.own:
@@ -170,17 +172,18 @@
         if self.inner:
             for c in self.own:
                 c.wait()
-        self.over_y.start()
+        for c in self.over_y:
+            c.start()
         self.core.start()
 
-    def step1(self):
-        self.over_y.wait_recv()
-        self.over_z.start()
-        self.core_a.start()
-
-    def step2(self):
-        self.over_z.wait_recv()
-        self.core_b.start()
+    def step1(self, i=0):
+        self.over_y[i].wait_recv()
+        self.over_z[i].start()
+        self.core_a[i].start()
+
+    def step2(self, i=0):
+        self.over_z[i].wait_recv()
+        self.core_b[i].start()
 
     def ready(self, i):
         if i == 0 and not self.inner:
@@ -189,77 +192,20 @@
         if i == 1:
             self.core.wait_recv()
         if i == 3:
-            self.core_a.wait_recv()
-            self.core_b.wait_recv()
+            for c in self.core_a + self.core_b:
+                c.wait_recv()
 
     def finish(self):
-        for c in (self.core, self.over_y, self.over_z, self.core_a, self.core_b):
+        for c in [self.core] + self.over_y + self.over_z + self.core_a + self.core_b:
             c.wait_send()
 
 
 class Reduce:
-    def __init__(self, links, part, rc, ry, zb, zr, at):
-        self.part, self.at = part, at
+    def __init__(self, links, part, rc, ry, zb, zr, at, y_first):
+        self.part, self.at, self.y_first = part, at, y_first
         self.rc, self.ry, self.zb, self.zr = rc, ry, zb, zr
-        self.dp = zb.shape[0]
-        self.core = [links.remote(part(at[f]), rc.at[j], at["C"]) for j, f in enumerate(("t1", "t3"))]
-        self.over_y = links.remote(part(at["t2"]), ry, at["Y"])
-        self.over_z = []
-        off, m, bit, k = 0, self.dp, 1, 0
-        self.kept = []
-        while m > 1:
-            m //= 2
-            b = bit_of(at["d"], bit)
-            keep, give = off + b * m, off + (1 - b) * m
-            self.over_z.append(links.remote(zb.at[pl.ds(give, m)], zr[k], at["Z"][k]))
-            self.kept.append((keep, m))
-            off, bit, k = keep, 2 * bit, k + 1
-
-    def core_send(self, j):
-        self.core[j].start()
-
-    def core_done(self):
-        self.core[0].wait_recv()
-        self.core[1].wait_recv()
-        far, near = self.part(self.at["t2"]), self.part(self.at["t"])
-        far[...] = (far[...].astype(F32) + self.rc[1].astype(F32)).astype(BF16)
-        self.over_y.start()
-        near[...] = (near[...].astype(F32) + self.rc[0].astype(F32)).astype(BF16)
-
-    def y_done(self):
-        self.over_y.wait_recv()
-        near = self.part(self.at["t"])
-        rows = self.zb.shape[1]
-        for i in range(self.dp):
-            where = pl.ds(i * rows, rows)
-            total = near[where].astype(F32) + self.ry[where].astype(F32)
-            self.zb[reversed_bits(i, self.dp)] = total.astype(BF16)
-        self.over_z[0].start()
-
-    def z_done(self, k, out=None):
-        self.over_z[k].wait_recv()
-        keep, m = self.kept[k]
-        if k == len(self.over_z) - 1:
-            out[...] = self.zb[keep].astype(F32) + self.zr[k][0].astype(F32)
-        else:
-            live = self.zb.at[pl.ds(keep, m)]
-            live[...] = (live[...].astype(F32) + self.zr[k][...].astype(F32)).astype(BF16)
-            self.over_z[k + 1].start()
-
-    def rest_z(self, k, out):
-        for j in range(k, len(self.over_z)):
-            self.z_done(j, out)
-
-    def finish(self):
-        for c in self.core + [self.over_y] + self.over_z:
-            c.wait_send()
-
-
-class ReduceZ:
-    def __init__(self, links, part, rc, ry, zb, zr, at):
-        self.part, self.at = part, at
-        self.rc, self.ry, self.zb, self.zr = rc, ry, zb, zr
-        self.dp = zb.shape[1]
+        self.n = zb.shape[0]
+        self.dp, self.rows = zb.shape[1:3]
         self.core = [links.remote(part(at[f]), rc.at[j], at["C"]) for j, f in enumerate(("t1", "t3"))]
         self.over_z, self.kept = [], []
         off, m, bit, k = 0, self.dp, 1, 0
@@ -271,34 +217,52 @@
             self.kept.append((keep, m))
             off, bit, k = keep, 2 * bit, k + 1
         self.off = off
-        self.over_y = links.remote(zb.at[0, off], ry, at["Y"])
+        self.over_y = links.remote(part(at["t2"]) if y_first else zb.at[1, off], ry, at["Y"])
 
     def core_send(self, j):
         self.core[j].start()
+
+    def into_zb(self, j, mine, theirs):
+        for i in range(self.dp):
+            where = pl.ds(i * self.rows, self.rows)
+            self.zb[j, reversed_bits(i, self.dp)] = (mine[where, :].astype(F32) + theirs[where, :].astype(F32)).astype(BF16)
 
     def core_done(self):
         self.core[0].wait_recv()
         self.core[1].wait_recv()
-        rows = self.zb.shape[2]
-        for j, f in enumerate(("t2", "t")):
-            part = self.part(self.at[f])
-            for i in range(self.dp):
-                where = pl.ds(i * rows, rows)
-                total = part[where, :].astype(F32) + self.rc[1 - j, where, :].astype(F32)
-                self.zb[j, reversed_bits(i, self.dp)] = total.astype(BF16)
-        self.over_z[0].start()
-
-    def z_done(self, k):
+        far, near = self.part(self.at["t2"]), self.part(self.at["t"])
+        if self.y_first:
+            far[...] = (far[...].astype(F32) + self.rc[1].astype(F32)).astype(BF16)
+            self.over_y.start()
+            near[...] = (near[...].astype(F32) + self.rc[0].astype(F32)).astype(BF16)
+        else:
+            self.into_zb(0, near, self.rc.at[0])
+            self.into_zb(1, far, self.rc.at[1])
+            self.over_z[0].start()
+
+    def y_done(self, out=None):
+        self.over_y.wait_recv()
+        if self.y_first:
+            self.into_zb(0, self.part(self.at["t"]), self.ry)
+            self.over_z[0].start()
+        else:
+            out[...] = self.zb[0, self.off].astype(F32) + self.ry[...].astype(F32)
+
+    def z_done(self, k, out=None):
         self.over_z[k].wait_recv()
         keep, m = self.kept[k]
-        for j in range(2):
-            live = self.zb.at[j, pl.ds(keep, m)]
-            live[...] = (live[...].astype(F32) + self.zr[k][j].astype(F32)).astype(BF16)
-        (self.over_z[k + 1] if k + 1 < len(self.over_z) else self.over_y).start()
-
-    def y_done(self, out):
-        self.over_y.wait_recv()
-        out[...] = self.zb[1, self.off].astype(F32) + self.ry[...].astype(F32)
+        last = k == len(self.over_z) - 1
+        if last and self.y_first:
+            out[...] = self.zb[0, keep].astype(F32) + self.zr[k][0, 0].astype(F32)
+        else:
+            for j in range(self.n):
+                live = self.zb.at[j, pl.ds(keep, m)]
+                live[...] = (live[...].astype(F32) + self.zr[k][j].astype(F32)).astype(BF16)
+            (self.over_y if last else self.over_z[k + 1]).start()
+
+    def z_rest(self, out=None):
+        for k in range(1, len(self.over_z)):
+            self.z_done(k, out)
 
     def finish(self):
         for c in self.core + [self.over_y] + self.over_z:
@@ -326,7 +290,6 @@
     scale = jnp.asarray(DH**-0.5, BF16)
     gain_ref, x_ref = R("gains"), R("x")
     side = 3 * own // 4
-    copies_out = []
 
     def rowsl(r, n=own):
         return pl.ds(pl.multiple_of(r * n, n), n)
@@ -361,27 +324,27 @@
 
     def by_shard(name, n=None):
         def slot(s, span, i=None):
-            full = R(name).at[s] if span is None else R(name).at[s, span]
+            full = R(name).at[s, span]
             return full if i is None else full.at[:, pl.ds(i * n, n)]
 
         return slot
 
-    def by_columns(name, n):
+    def by_columns(name, n, row):
         def slot(s, span):
-            return R(name).at[:, lanes(s, n)] if span is None else R(name).at[span, lanes(s, n)]
+            return R(name).at[pl.ds(pl.multiple_of(span.start + row, HALO), span.size), lanes(s, n)]
 
         return slot
 
-    g_wa = Gather(links, R("wa_h"), by_shard("wa", hw), at, 3)
-    g_wo = Gather(links, R("wo_h"), by_shard("wo"), at)
-    g_w1 = Gather(links, R("w1_h"), by_shard("w1"), at)
-    g_w2 = Gather(links, R("w2_h"), by_shard("w2"), at)
-    g_cq = Gather(links, R("cx_h").at[:, pl.ds(0, hw)], by_columns("cqw", hw), at)
-    g_co = Gather(links, R("cx_h").at[:, pl.ds(hw, hw)], by_columns("cow", hw), at)
-    c0_x = links.remote(R("cx_h"), R("c0").at[:, lanes(t, 2 * hw)], at["X"])
-    g_c0 = Gather(links, None, by_columns("c0", 2 * hw), at)
-    x_right = links.remote(x_ref.at[:, pl.ds(own - HALO, HALO)], R("xh").at[0], (p, d, lax.rem(t + 1, 4)))
-    x_left = links.remote(x_ref.at[:, pl.ds(0, HALO)], R("xh").at[1], (p, d, lax.rem(t + 3, 4)))
+    g_wa = Gather(links, R("wa_h"), by_shard("wa", hw), width, at, 2, 3)
+    g_wo = Gather(links, R("wo_h"), by_shard("wo"), hw, at)
+    g_w1 = Gather(links, R("w1_h"), by_shard("w1"), width, at, 2)
+    g_w2 = Gather(links, R("w2_h"), by_shard("w2"), fw, at, 2)
+    g_c1 = Gather(links, R("cx_h"), by_columns("dmf", hw, 0), 2 * width, at)
+    c0_x = links.remote(R("cx_h"), R("dmf").at[pl.ds(2 * width, 2 * width), lanes(t)], at["X"])
+    g_c0 = Gather(links, None, by_columns("dmf", hw, 2 * width), 2 * width, at)
+    loads = [links.here(R(n + "_h"), R(n)) for n in ("x", "cot", "segs")]
+    x_right = links.remote(R("x_h").at[:, pl.ds(own - HALO, HALO)], R("xh").at[0], (p, d, lax.rem(t + 1, 4)))
+    x_left = links.remote(R("x_h").at[:, pl.ds(0, HALO)], R("xh").at[1], (p, d, lax.rem(t + 3, 4)))
     base_mem, base_memc, base_memt = links.take(rows), links.take(rows), links.take(rows)
     base_dmc, base_dmt, base_dmx = links.take(rows), links.take(rows), links.take(rows)
     block = pl.ds(pl.multiple_of(t * own, own), own)
@@ -410,26 +373,30 @@
     def dm_x(r):
         return links.remote(R("dm").at[r], R("dm").at[r], at["X"], base_dmx + r)
 
-    def by_rows(name, m):
-        return lambda s: R(name).at[pl.ds(pl.multiple_of(s * width, width), width), pl.ds(0, m)]
+    def by_rows(name, m, col=0):
+        return lambda s: R(name).at[pl.ds(pl.multiple_of(s * width, width), width), pl.ds(col, m)]
 
     def by_lanes(name, m, row=0):
         return lambda s: R(name).at[pl.ds(row, width), lanes(s, m)]
 
-    def reduce_of(name, part, kind=Reduce):
+    def reduce_of(name, part, y_first=True):
         zr = [R(f"zr{k}_{name}") for k in range(len(zbits))]
-        return kind(links, part, R("rc_" + name), R("ry_" + name), R("zb_" + name), zr, at)
-
-    r_w2 = reduce_of("w2", by_rows("memf", fw))
-    r_w1 = reduce_of("w1", by_rows("dmf", fw), ReduceZ)
+        return Reduce(links, part, R("rc_" + name), R("ry_" + name), R("zb_" + name), zr, at, y_first)
+
+    fh = fw // 2
+    r_w2 = [reduce_of(f"w2{j}", by_rows("dw2", fh, j * fh), j > 0) for j in range(2)]
+    r_w1 = [reduce_of(f"w1{j}", by_rows("dmf", fh, j * fh)) for j in range(2)]
     r_wo = reduce_of("wo", by_lanes("dwo", hw))
-    r_wa = reduce_of("wa", by_rows("cp", 3 * hw))
+    r_wa = [reduce_of(f"wa{j}", by_rows("cp", hw, j * hw)) for j in range(3)]
     r_c0 = reduce_of("c0", by_lanes("kv", 2 * hw))
     r_c1 = reduce_of("c1", by_lanes("kv", 2 * hw, width))
+    w2_out = [R("dw2_o").at[:, pl.ds(j * fh, fh)] for j in range(2)]
+    w1_out = [R("dw1_o").at[:, pl.ds(j * fh, fh)] for j in range(2)]
+    wa_out = [R("da_o").at[:, pl.ds(j * hw, hw)] for j in range(3)]
     c0_back = links.remote(R("dc0"), R("dc0r"), at["X"])
-    dn_right = links.remote(R("dhs").at[1], R("dhr").at[0], (p, d, lax.rem(t + 1, 4)))
-    dn_left = links.remote(R("dhs").at[0], R("dhr").at[1], (p, d, lax.rem(t + 3, 4)))
-    gain_links = [links.remote(R("dgs").at[k], R("dgr").at[k], dev) for k, dev in enumerate([at["C"], at["Y"]] + zbits)]
+    dn_right = links.remote(R("xh").at[1], R("dhr").at[0], (p, d, lax.rem(t + 1, 4)))
+    dn_left = links.remote(R("xh").at[0], R("dhr").at[1], (p, d, lax.rem(t + 3, 4)))
+    gain_links = [links.remote(R("dgs").at[k], R("dgr").at[k], dev) for k, dev in enumerate([at["C"]] + zbits + [at["Y"]])]
 
     @pl.when(is_dec)
     def _():
@@ -439,6 +406,8 @@
                 for r in range(rows):
                     R("memf")[pl.ds(r * slots + start, 2 * HALO), :] = jnp.zeros((2 * HALO, width), BF16)
 
+    for c in loads:
+        c.start()
     barrier = pltpu.get_barrier_semaphore()
     partners = [at["C"], at["Y"], at["T"], at["X"]] + zbits
     for dev in partners:
@@ -452,16 +421,16 @@
 
     @pl.when(is_enc)
     def _():
+        c0_x.start()
         g_w1.start()
         g_w2.start()
-        c0_x.start()
 
     @pl.when(is_dec)
     def _():
-        g_cq.start()
-        g_co.start()
-        g_w2.start()
-        g_w1.start()
+        g_c1.start()
+
+    for c in loads:
+        c.wait()
 
     nw_ref, bias_ref = R("nw"), R("bias")
     gain0, gain1, gain2 = gain_ref[0], gain_ref[1], gain_ref[2]
@@ -489,33 +458,42 @@
         nw_ref[pl.ds(r * win + HALO + own, HALO), :] = norm(R("xh")[1, r].astype(F32), gain0).astype(BF16)
 
     def after_pair(i):
+        @pl.when(i == 0)
+        def _():
+            g_wa.step1(0)
+
         @pl.when(i == 1)
         def _():
-            g_wa.step1()
+            g_wa.step1(1)
+            g_wa.step2(0)
             g_wo.step1()
 
             @pl.when(is_dec)
             def _():
                 c0_x.wait_recv()
                 g_c0.start()
-
-            g_wa.step2()
+                g_w2.start()
+                g_w1.start()
+
+            g_wa.step2(1)
 
         @pl.when(i == 2)
         def _():
-            pl.when(is_enc)(g_w1.step1)
+            pl.when(is_enc)(lambda: g_w1.step1(0))
+            pl.when(is_dec)(g_c1.step1)
+            g_wo.step2()
+
+        @pl.when(i == 3)
+        def _():
+            @pl.when(is_enc)
+            def _():
+                g_w1.step1(1)
+                g_w1.step2(0)
 
             @pl.when(is_dec)
             def _():
-                g_cq.step1()
-                g_co.step1()
-
-            g_wo.step2()
-
-        @pl.when(i == 3)
-        def _():
-            pl.when(is_enc)(g_w2.step1)
-            pl.when(is_dec)(g_w2.step1)
+                g_c0.step1()
+                g_c1.step2()
 
     def wait_ready(i, *weights):
         for k in range(4):
@@ -559,37 +537,52 @@
     def _():
         r2_ref[...] = r1_ref[...]
 
-        def feed(i, rs):
+        def up(i):
             s = near_first(i)
-            u, gp = gelu_parts(mm(n2_ref[rs, :], R("w1")[s]))
-            u = u.astype(BF16)
-            u_ref[s, rs, :] = u
-            gp_ref[s, rs, :] = gp.astype(BF16)
-            r2_ref[rs, :] += mm(u, R("w2")[s])
+            u, gp = gelu_parts(mm(n2_ref[...], R("w1")[s]))
+            u_ref[s] = u.astype(BF16)
+            gp_ref[s] = gp.astype(BF16)
+            return s
+
+        g_w2.step1(0)
 
         def near(i, _):
             wait_ready(i, g_w1, g_w2)
-            feed(i, pl.ds(0, tokens))
-            pl.when(i == 0)(g_w1.step2)
-            pl.when(i == 1)(g_w2.step2)
+            s = up(i)
+            r2_ref[...] += mm(u_ref[s], R("w2")[s])
+            pl.when(i == 0)(lambda: g_w1.step2(1))
+            pl.when(i == 1)(lambda: g_w2.step1(1))
             return 0
 
         lax.fori_loop(0, 2, near, 0)
+
+        def far(i, _):
+            wait_ready(i, g_w1)
+            up(i)
+            pl.when(i == 2)(lambda: g_w2.step2(0))
+            pl.when(i == 3)(lambda: g_w2.step2(1))
+            return 0
+
+        lax.fori_loop(2, 4, far, 0)
+        g_w2.ready(3)
+        far1, far2 = near_first(2), near_first(3)
 
         def row(r, _):
             rs = rowsl(r)
-
-            def far(i, _):
-                pl.when(r == 0)(lambda: wait_ready(i, g_w1, g_w2))
-                feed(i, rs)
-                return 0
-
-            lax.fori_loop(2, 4, far, 0)
-            sec_ref[rs, :] = norm(r2_ref[rs, :], gain2).astype(BF16)
+            total = r2_ref[rs, :] + mm(u_ref[far1, rs, :], R("w2")[far1]) + mm(u_ref[far2, rs, :], R("w2")[far2])
+            r2_ref[rs, :] = total
+            sec_ref[rs, :] = norm(total, gain2).astype(BF16)
             mem_x(r).start()
             return 0
 
         lax.fori_loop(0, rows, row, 0)
+
+    def sends(reductions, i):
+        for j in range(2):
+            @pl.when(i == j)
+            def _():
+                for reduction in reductions:
+                    reduction.core_send(j)
 
     cstart = pl.multiple_of(jnp.minimum(t * (own - HALO), slots - cwin), HALO)
     cwindow = pl.ds(cstart, cwin)
@@ -600,21 +593,43 @@
 
     @pl.when(is_dec)
     def _():
-        g_cq.step2()
-        g_co.step2()
-        g_c0.step1()
-        g_w1.step1()
+        g_c0.step2()
+        g_w2.step1(0)
+        for k in range(4):
+            g_c1.ready(k)
+        pick_shape = (width // 4, width // 2)
+        twice = 2 * lax.broadcasted_iota(jnp.int32, pick_shape, 0)
+        at_col = lax.broadcasted_iota(jnp.int32, pick_shape, 1)
+        picks = [jnp.where(at_col == twice + j, 1.0, 0.0).astype(BF16) for j in range(2)]
+
+        def unweave(base, m):
+            return [mm(pick, R("dmf")[pl.ds(base + m * (width // 2), width // 2), :]).astype(BF16) for pick in picks]
+
+        for m in range(4):
+            span = pl.ds(m * (width // 4), width // 4)
+            cqw_ref[span, :], cow_ref[span, :] = unweave(0, m)
+        cq_ref[...] = mm(n2_ref[...], cqw_ref[...]).astype(BF16) * scale
+        g_w2.step1(1)
+        g_w2.step2(0)
+        g_w1.step1(0)
         kv_ref[...] = jnp.zeros_like(kv_ref)
-        R("dmf")[...] = jnp.zeros_like(R("dmf"))
         for r in range(rows):
             cols[r] = seg_column(1, r)
             keys_ref[r] = seg_row(0, r, cstart)[:, :cwin]
-        g_w2.step2()
         for k in range(4):
-            g_cq.ready(k)
-        cq_ref[...] = mm(n2_ref[...], cqw_ref[...]).astype(BF16) * scale
-        g_c0.step2()
-        g_w1.step2()
+            g_c0.ready(k)
+        for m in range(4):
+            span = pl.ds(m * (width // 4), width // 4)
+            ck, cv = unweave(2 * width, m)
+            for s in range(4):
+                c0_ref[span, 2 * s * hw : (2 * s + 1) * hw] = ck[:, s * hw : (s + 1) * hw]
+                c0_ref[span, (2 * s + 1) * hw : (2 * s + 2) * hw] = cv[:, s * hw : (s + 1) * hw]
+        g_w2.step2(1)
+        g_w1.step1(1)
+        g_w1.step2(0)
+        for g in (g_c1, g_c0):
+            g.finish()
+        R("dmf")[...] = jnp.zeros_like(R("dmf"))
         for k in range(4):
             g_w2.ready(k)
 
@@ -623,10 +638,23 @@
             return 0
 
         lax.fori_loop(0, 4, early, 0)
+        g_w1.step2(1)
         for k in range(4):
             g_w1.ready(k)
-            g_co.ready(k)
-            g_c0.ready(k)
+
+        def settle(r):
+            span = pl.ds(0, own)
+            dm_c(r).wait_recv()
+            acc_ref[span, :] = R("dmf")[in_row(r, block), :].astype(F32) + R("rcc")[r].astype(F32)
+
+            @pl.when(inner)
+            def _():
+                dm_t(r).wait_recv()
+                place = pl.ds(pl.multiple_of((2 - t) * (own - side), HALO), side)
+                acc_ref[place, :] += R("rct")[r].astype(F32)
+
+            R("dm")[r] = acc_ref[span, :].astype(BF16)
+            dm_x(r).start()
 
         def row(r, _):
             rs = rowsl(r)
@@ -663,6 +691,7 @@
                 return 0
 
             lax.fori_loop(0, 2, cross, 0)
+            pl.when(r > 0)(lambda: settle(r - 1))
             r2_ref[rs, :] = r1_ref[rs, :] + mm_nt(oc_ref[rs, :], cow_ref[...])
             n3_ref[rs, :] = norm(r2_ref[rs, :], gain2).astype(BF16)
             dn = pl.ds(0, own)
@@ -687,6 +716,17 @@
             g_ref[rs, :] = g2
             gb_ref[rs, :] = g2.astype(BF16)
             do_ref[rs, :] = mm(gb_ref[rs, :], cow_ref[...]).astype(BF16)
+
+            @pl.when(r == rows - 1)
+            def _():
+                def w2_grad(i, _):
+                    s = far_first(i)
+                    R("dw2")[rowsl(s, width), :] = mm_tn(cot_ref[...], u_ref[s]).astype(BF16)
+                    sends(r_w2, i)
+                    return 0
+
+                lax.fori_loop(0, 4, w2_grad, 0)
+
             ws = pl.ds(pl.multiple_of(r * cwin, HALO), cwin)
 
             def back(i, _):
@@ -707,17 +747,13 @@
             dx, dg = norm_back(r1_ref[rs, :], gain1, mm_nt(cq_ref[rs, :], cqw_ref[...]))
             R("dg")[r, pl.ds(1, 1), :] = dg
             g_ref[rs, :] += dx
-            dm_c(r).wait_recv()
-            acc_ref[dn, :] = R("dmf")[in_row(r, block), :].astype(F32) + R("rcc")[r].astype(F32)
-
-            @pl.when(inner)
+
+            @pl.when(r == rows - 1)
             def _():
-                dm_t(r).wait_recv()
-                place = pl.ds(pl.multiple_of((2 - t) * (own - side), HALO), side)
-                acc_ref[place, :] += R("rct")[r].astype(F32)
-
-            R("dm")[r] = acc_ref[dn, :].astype(BF16)
-            dm_x(r).start()
+                r_w2[0].core_done()
+                r_w2[1].core_done()
+                settle(r)
+
             return 0
 
         lax.fori_loop(0, rows, row, 0)
@@ -725,9 +761,13 @@
             dm_c(r).wait_send()
             pl.when(inner)(dm_t(r).wait_send)
 
-        def sends(reduction, i):
-            pl.when(i == 0)(lambda: reduction.core_send(0))
-            pl.when(i == 1)(lambda: reduction.core_send(1))
+        def w1_grad(i, _):
+            s = far_first(i)
+            R("dmf")[rowsl(s, width), :] = mm_tn(n3_ref[...], gp_ref[s]).astype(BF16)
+            sends(r_w1, i)
+            return 0
+
+        lax.fori_loop(0, 4, w1_grad, 0)
 
         def c0_grad(i, _):
             s = far_first(i)
@@ -735,40 +775,24 @@
             for r in range(1, rows):
                 total += mm_tn(R("memf")[in_row(r, cwindow), :], dkv_ref[pl.ds(r * cwin, cwin), lanes(s, 2 * hw)])
             r_c0.part(s)[...] = total.astype(BF16)
-            sends(r_c0, i)
+            sends([r_c0], i)
+
+            @pl.when(i == 1)
+            def _():
+                r_w1[0].core_done()
+                r_w1[1].core_done()
+
             return 0
 
         lax.fori_loop(0, 4, c0_grad, 0)
         dcq = mm_tn(n2_ref[...], cq_ref[...]).astype(BF16)
         dco = mm_tn(gb_ref[...], oc_ref[...]).astype(BF16)
+        r_c0.core_done()
         for s in range(4):
             r_c1.part(s)[:, :hw] = dcq[:, s * hw : (s + 1) * hw]
             r_c1.part(s)[:, hw:] = dco[:, s * hw : (s + 1) * hw]
-        r_c1.core_send(0)
-        r_c1.core_send(1)
-        r_c0.core_done()
-
-        for r in range(rows):
-            mem_c(r).wait_send()
-            pl.when(inner)(mem_t(r).wait_send)
-
-        def w2_grad(i, _):
-            s = far_first(i)
-            r_w2.part(s)[...] = mm_tn(cot_ref[...], u_ref[s]).astype(BF16)
-            sends(r_w2, i)
-            return 0
-
-        lax.fori_loop(0, 4, w2_grad, 0)
-        r_c1.core_done()
-
-        def w1_grad(i, _):
-            s = far_first(i)
-            r_w1.part(s)[...] = mm_tn(n3_ref[...], gp_ref[s]).astype(BF16)
-            sends(r_w1, i)
-            pl.when(i == 0)(r_w2.core_done)
-            return 0
-
-        lax.fori_loop(0, 4, w1_grad, 0)
+        sends([r_c1], 0)
+        sends([r_c1], 1)
 
     @pl.when(is_enc)
     def _():
@@ -783,13 +807,9 @@
 
         lax.fori_loop(0, rows, row, 0)
 
-        def sends(reduction, i):
-            pl.when(i == 0)(lambda: reduction.core_send(0))
-            pl.when(i == 1)(lambda: reduction.core_send(1))
-
         def w2_grad(i, _):
             s = far_first(i)
-            r_w2.part(s)[...] = mm_tn(gb_ref[...], u_ref[s]).astype(BF16)
+            R("dw2")[rowsl(s, width), :] = mm_tn(gb_ref[...], u_ref[s]).astype(BF16)
             sends(r_w2, i)
             return 0
 
@@ -800,13 +820,20 @@
         def w1_grad(i, _):
             s = far_first(i)
             dh = (mm_nt(gb_ref[...], R("w2")[s]) * gp_ref[s].astype(F32)).astype(BF16)
-            r_w1.part(s)[...] = mm_tn(n2_ref[...], dh).astype(BF16)
+            R("dmf")[rowsl(s, width), :] = mm_tn(n2_ref[...], dh).astype(BF16)
             sends(r_w1, i)
             acc_ref[dn, :] += mm_nt(dh, R("w1")[s])
-            pl.when(i == 0)(r_w2.core_done)
+
+            @pl.when(i == 0)
+            def _():
+                r_w2[0].core_done()
+                r_w2[1].core_done()
+
             return 0
 
         lax.fori_loop(0, 4, w1_grad, 0)
+        r_w1[0].core_done()
+        r_w1[1].core_done()
         dx, dg = norm_back(r1_ref[...], gain1, acc_ref[dn, :])
         R("dg")[0, pl.ds(1, 1), :] = dg
         for r in range(1, rows):
@@ -815,7 +842,6 @@
 
     sec_out = links.here(sec_ref, R("sec"))
     sec_out.start()
-    r_w1.core_done()
     gb_ref[...] = g_ref[...].astype(BF16)
     R("dwo")[...] = mm_tn(gb_ref[...], o_ref[...]).astype(BF16)
     r_wo.core_send(0)
@@ -838,40 +864,54 @@
             dqkv_ref[pl.ds(r * win + HALO, own), :hw] = dq
             dqkv_ref[pl.ds(r * win, win), hw : 2 * hw] = dk
             dqkv_ref[pl.ds(r * win, win), 2 * hw :] = dv
-        r_wa.part(s)[...] = mm_tn(nw_ref[...], dqkv_ref[...]).astype(BF16)
+        R("cp")[rowsl(s, width), pl.ds(0, 3 * hw)] = mm_tn(nw_ref[...], dqkv_ref[...]).astype(BF16)
+        sends(r_wa, i)
         acc_ref[...] += mm_nt(dqkv_ref[...], R("wa")[s])
 
         @pl.when(i == 0)
         def _():
-            r_wa.core_send(0)
             r_wo.core_done()
-
-        @pl.when(i == 1)
+            r_w2[0].z_done(0)
+            r_w2[1].y_done()
+
+        @pl.when((i == 1) & is_dec)
         def _():
-            r_wa.core_send(1)
-            pl.when(is_dec)(r_c0.y_done)
-
-        @pl.when(i == 2)
+            r_w1[0].y_done()
+            for k in range(1, len(zbits)):
+                r_w2[0].z_done(k)
+
+        @pl.when((i == 2) & is_enc)
         def _():
-            pl.when(is_enc)(r_w2.y_done)
-
-        @pl.when(i == 3)
+            r_w1[0].y_done()
+            r_w2[1].z_done(0, w2_out[1])
+
+        @pl.when((i == 2) & is_dec)
         def _():
-            @pl.when(is_dec)
-            def _():
-                r_c1.y_done()
-                r_c0.z_done(0, R("dc0"))
+            r_w2[1].z_done(0, w2_out[1])
+            r_w1[0].z_done(0, w1_out[0])
+
+        @pl.when((i == 3) & is_enc)
+        def _():
+            for k in range(1, len(zbits)):
+                r_w2[0].z_done(k)
+            r_w2[1].z_rest(w2_out[1])
+
+        @pl.when((i == 3) & is_dec)
+        def _():
+            r_w1[1].y_done()
+            r_w2[1].z_rest(w2_out[1])
 
         return 0
 
     lax.fori_loop(0, 4, self_back, 0)
     for r in range(rows):
-        R("dhs")[0, r] = acc_ref[pl.ds(r * win, HALO), :].astype(BF16)
-        R("dhs")[1, r] = acc_ref[pl.ds(r * win + HALO + own, HALO), :].astype(BF16)
+        R("xh")[0, r] = acc_ref[pl.ds(r * win, HALO), :].astype(BF16)
+        R("xh")[1, r] = acc_ref[pl.ds(r * win + HALO + own, HALO), :].astype(BF16)
     pl.when(t < 3)(dn_right.start)
     pl.when(t > 0)(dn_left.start)
-    r_wa.core_done()
-    r_w1.z_done(0)
+    pl.when(is_dec)(r_c1.core_done)
+    for j in range(3):
+        r_wa[j].core_done()
 
     @pl.when(t == 0)
     def _():
@@ -880,6 +920,17 @@
     @pl.when(t == 3)
     def _():
         R("dhr")[1] = jnp.zeros((rows, HALO, width), BF16)
+
+    @pl.when(is_enc)
+    def _():
+        r_w1[1].y_done()
+        r_w1[0].z_done(0, w1_out[0])
+
+    @pl.when(is_dec)
+    def _():
+        r_w1[0].z_rest(w1_out[0])
+        r_w1[1].z_done(0, w1_out[1])
+        r_c0.y_done()
 
     pl.when(t > 0)(dn_right.wait_recv)
     pl.when(t < 3)(dn_left.wait_recv)
@@ -908,37 +959,63 @@
         else:
             R("dgain")[...] = pltpu.roll(R("dgs")[k] + R("dgr")[k], lax.rem(width - d * (width // dp), width), 1)
 
-    pl.when(is_dec)(r_w2.y_done)
-    r_wo.y_done()
-    r_w2.z_done(0, R("dw2_o"))
-    gain_step(0)
+    last_gain = len(gain_links) - 1
+
+    @pl.when(is_enc)
+    def _():
+        r_w1[0].z_rest(w1_out[0])
+        gain_step(0)
+        r_w1[1].z_done(0, w1_out[1])
+        r_wo.y_done()
+        r_wa[0].y_done()
+        r_w1[1].z_rest(w1_out[1])
+        r_wo.z_done(0, R("dwo_o"))
+        for k in range(1, last_gain):
+            gain_step(k)
+        r_wa[1].y_done()
+        r_wa[0].z_done(0, wa_out[0])
+        r_wo.z_rest(R("dwo_o"))
+        r_wa[2].y_done()
+        r_wa[1].z_done(0, wa_out[1])
+        r_wa[0].z_rest(wa_out[0])
+        r_w2[0].y_done(w2_out[0])
+        r_wa[2].z_done(0, wa_out[2])
+        r_wa[1].z_rest(wa_out[1])
+        gain_step(last_gain)
+        r_wa[2].z_rest(wa_out[2])
 
     @pl.when(is_dec)
     def _():
-        r_c0.rest_z(1, R("dc0"))
+        r_w1[1].z_rest(w1_out[1])
+        r_c0.z_done(0, R("dc0"))
+        gain_step(0)
+        r_wo.y_done()
+        r_c0.z_rest(R("dc0"))
         c0_back.start()
+        r_c1.y_done()
+        r_wo.z_done(0, R("dwo_o"))
+        for k in range(1, last_gain):
+            gain_step(k)
+        r_wa[0].y_done()
         r_c1.z_done(0, R("dc"))
-
-    for k in range(1, len(zbits)):
-        r_w1.z_done(k)
-    r_wo.z_done(0, R("dwo_o"))
-    gain_step(1)
-    r_w2.rest_z(1, R("dw2_o"))
-    r_wa.y_done()
-    gain_step(2)
-    pl.when(is_dec)(lambda: r_c1.rest_z(1, R("dc")))
-    r_wo.rest_z(1, R("dwo_o"))
-    r_w1.y_done(R("dw1_o"))
-    r_wa.z_done(0, R("da_o"))
-    for k in range(3, len(gain_links)):
-        gain_step(k)
-    r_wa.rest_z(1, R("da_o"))
+        r_wo.z_rest(R("dwo_o"))
+        r_wa[1].y_done()
+        r_wa[0].z_done(0, wa_out[0])
+        r_c1.z_rest(R("dc"))
+        r_wa[2].y_done()
+        r_wa[1].z_done(0, wa_out[1])
+        r_wa[0].z_rest(wa_out[0])
+        r_w2[0].y_done(w2_out[0])
+        r_wa[2].z_done(0, wa_out[2])
+        r_wa[1].z_rest(wa_out[1])
+        gain_step(last_gain)
+        r_wa[2].z_rest(wa_out[2])
 
     sec_out.wait()
     gx_out.wait()
     for g in (g_wa, g_wo, g_w1, g_w2):
         g.finish()
-    for g in (r_w2, r_w1, r_wo, r_wa):
+    for g in r_w2 + r_w1 + [r_wo] + r_wa:
         g.finish()
     for c in gain_links:
         c.wait_send()
@@ -957,9 +1034,11 @@
 
     @pl.when(is_dec)
     def _():
-        for g in (g_cq, g_co, g_c0, r_c0, r_c1):
+        for g in (r_c0, r_c1):
             g.finish()
         for r in range(rows):
+            mem_c(r).wait_send()
+            pl.when(inner)(mem_t(r).wait_send)
             dm_x(r).wait_send()
         c0_back.wait_send()
 
@@ -992,9 +1071,9 @@
     zsteps = (dp - 1).bit_length()
 
     ins = dict(
-        x=embeds[0], segs=segments, gains=norm_gains.transpose(1, 0, 2), cot=cotangent.reshape(tokens, width),
+        x_h=embeds[0], segs_h=segments, gains=norm_gains.transpose(1, 0, 2), cot_h=cotangent.reshape(tokens, width),
         wa_h=attn_in[0].transpose(1, 0, 2), wo_h=attn_out[0], w1_h=ffn_in[0], w2_h=ffn_out[0],
-        cx_h=cross_proj[0].reshape(width, 2 * hw),
+        cx_h=cross_proj[0].reshape(2 * width, hw),
     )
     outs = dict(
         sec=((tokens, width), BF16), gx=((tokens, width), BF16), dgain=((8, width), F32),
@@ -1002,6 +1081,7 @@
         dw1_o=((share, fw), F32), dw2_o=((share, fw), F32),
     )
     vm = dict(
+        x=((rows, own, width), BF16), cot=((tokens, width), BF16), segs=(segments.shape, jnp.int32),
         wa=((4, width, 3 * hw), BF16), wo=((4, hw, width), BF16), w1=((4, width, fw), BF16), w2=((4, fw, width), BF16),
         c0=((width, 8 * hw), BF16), cqw=((width, 4 * hw), BF16), cow=((width, 4 * hw), BF16),
         xh=((2, rows, HALO, width), BF16), nw=((rows * win, width), BF16),
@@ -1016,21 +1096,22 @@
         dkv=((rows * cwin, 8 * hw), BF16), dmf=((max(rows * slots, 4 * width), max(width, fw)), BF16),
         rcc=((rows, own, width), BF16), rct=((rows, side, width), BF16), dm=((rows, own, width), BF16),
         dg=((rows, 8, width), F32),
-        dqkv=((rows * win, 3 * hw), BF16), dhs=((2, rows, HALO, width), BF16), dhr=((2, rows, HALO, width), BF16),
+        dqkv=((rows * win, 3 * hw), BF16), dhr=((2, rows, HALO, width), BF16),
         dgs=((2 + zsteps, 8, width), F32), dgr=((2 + zsteps, 8, width), F32),
-        dwo=((width, 4 * hw), BF16),
+        dw2=((4 * width, fw), BF16), dwo=((width, 4 * hw), BF16),
         dc0=((share, 2 * hw), F32), dc0r=((share, 2 * hw), F32),
     )
-    for name, m in dict(w2=fw, w1=fw, wo=hw, wa=3 * hw, c0=2 * hw, c1=2 * hw).items():
-        both = (2,) if name == "w1" else ()
+    sums = dict(w20=fw // 2, w21=fw // 2, w10=fw // 2, w11=fw // 2, wo=hw, wa0=hw, wa1=hw, wa2=hw, c0=2 * hw, c1=2 * hw)
+    for name, m in sums.items():
+        shards = 2 if name == "w20" else 1
         vm["rc_" + name] = ((2, width, m), BF16)
-        vm["ry_" + name] = ((share if both else width, m), BF16)
-        vm["zb_" + name] = (both + (dp, share, m), BF16)
+        vm["ry_" + name] = ((share if shards == 2 else width, m), BF16)
+        vm["zb_" + name] = ((shards, dp, share, m), BF16)
         for k in range(zsteps):
-            vm[f"zr{k}_{name}"] = (both + (dp >> (k + 1), share, m), BF16)
-    copies = 140 + 8 * zsteps
-    sems = dict(send=pltpu.SemaphoreType.DMA((copies,)), recv=pltpu.SemaphoreType.DMA((copies,)), local=pltpu.SemaphoreType.DMA((12,)))
-    in_hbm = {"wa_h", "wo_h", "w1_h", "w2_h", "cx_h"}
+            vm[f"zr{k}_{name}"] = ((shards, dp >> (k + 1), share, m), BF16)
+    copies = 150 + 12 * zsteps
+    sems = dict(send=pltpu.SemaphoreType.DMA((copies,)), recv=pltpu.SemaphoreType.DMA((copies,)), local=pltpu.SemaphoreType.DMA((16,)))
+    in_hbm = {n for n in ins if n.endswith("_h")}
     out_hbm = {"sec", "gx"}
     results = pl.pallas_call(
         functools.partial(layers, list(ins) + list(outs) + list(vm) + list(sems)),

time: 157 us -> 149 us (0.949); the launches traced: 155 us -> 149 us
  Pallas kernels: 153 us -> 149 us
  local copies, waits for them, and re-layouts: 1.69 us -> 0 us
    pallas_call x1, Pallas kernels: 150 us -> 146 us  [body(): pl.pallas_call(functools.partial(layers, list(ins) + list(outs) + list(vm...]
    unnamed x1 -> x0, local copies, waits for them, and re-layouts: 1.69 us -> none
where the time goes in v4:
time: 149 us
  Pallas kernels  149 us (100%)
    pallas_call x1, Pallas kernels, body(): pl.pallas_call(functools.partial(layers, list(ins) + list(outs) + list(vm...  146 us

profile of v4, /device:TPU:0, one launch (start us, length us, event | category | flops | bytes accessed | tf_op | source)
XLA Modules:
  0.0 149.3 jit_solution(8877265939827950108)
XLA Ops:
  0.6 145.7 %layers.1 = (bf16[512,512]{1,0:T(8,128)(2,1)}, bf16[512,512]{1,0:T(8,128)(2,1)}, f32[8,512]{1,0:T(8,128)}, f32[128,384]{1,0:T(8,128)}, f32[128,128]{1,0:T(8,128)...) custom-call(bf16[2,256,512]{2,1,0:T(8,128)(2,1)} %bitcast.20, s32[2,2,1024]{2,1,0:T(2,128)} %refs_1_.1, ...), custom_call_target="tpu_custom_call" | custom-call | tf_op jit(solution)/shard_map/layers/pallas_call | solution.py:1116
  146.4 2.9 %arrange.1 = (bf16[512,512]{1,0:T(8,128)(2,1)}, bf16[512,512]{1,0:T(8,128)(2,1)}, f32[3,1,128]{2,1,0:T(1,128)}, f32[3,128,128]{2,1,0:T(8,128)}, f32[128,128]{1,0...) custom-call(bf16[512,512]{1,0:T(8,128)(2,1)} %get-tuple-element.24.sec, ...), custom_call_target="tpu_custom_call" | custom-call | tf_op jit(solution)/shard_map/arrange/pallas_call | solution.py:1127

commit v5 on v4

--- a/solution.py
+++ b/solution.py
@@ -338,7 +338,7 @@
     g_wa = Gather(links, R("wa_h"), by_shard("wa", hw), width, at, 2, 3)
     g_wo = Gather(links, R("wo_h"), by_shard("wo"), hw, at)
     g_w1 = Gather(links, R("w1_h"), by_shard("w1"), width, at, 2)
-    g_w2 = Gather(links, R("w2_h"), by_shard("w2"), fw, at, 2)
+    g_w2 = Gather(links, R("w2_h"), by_shard("w2"), fw, at, 4)
     g_c1 = Gather(links, R("cx_h"), by_columns("dmf", hw, 0), 2 * width, at)
     c0_x = links.remote(R("cx_h"), R("dmf").at[pl.ds(2 * width, 2 * width), lanes(t)], at["X"])
     g_c0 = Gather(links, None, by_columns("dmf", hw, 2 * width), 2 * width, at)
@@ -371,7 +371,7 @@
         return links.remote(dm_rows(r, edge_in), R("rct").at[r], at["T"], base_dmt + r)
 
     def dm_x(r):
-        return links.remote(R("dm").at[r], R("dm").at[r], at["X"], base_dmx + r)
+        return links.remote(R("rcc").at[r], R("rcc").at[r], at["X"], base_dmx + r)
 
     def by_rows(name, m, col=0):
         return lambda s: R(name).at[pl.ds(pl.multiple_of(s * width, width), width), pl.ds(col, m)]
@@ -384,8 +384,8 @@
         return Reduce(links, part, R("rc_" + name), R("ry_" + name), R("zb_" + name), zr, at, y_first)
 
     fh = fw // 2
-    r_w2 = [reduce_of(f"w2{j}", by_rows("dw2", fh, j * fh), j > 0) for j in range(2)]
-    r_w1 = [reduce_of(f"w1{j}", by_rows("dmf", fh, j * fh)) for j in range(2)]
+    r_w2 = [reduce_of(f"w2{j}", by_rows("dw2", fh, j * fh), j == 1) for j in range(2)]
+    r_w1 = [reduce_of(f"w1{j}", by_rows("dmf", fh, j * fh), j == 0) for j in range(2)]
     r_wo = reduce_of("wo", by_lanes("dwo", hw))
     r_wa = [reduce_of(f"wa{j}", by_rows("cp", hw, j * hw)) for j in range(3)]
     r_c0 = reduce_of("c0", by_lanes("kv", 2 * hw))
@@ -396,7 +396,11 @@
     c0_back = links.remote(R("dc0"), R("dc0r"), at["X"])
     dn_right = links.remote(R("xh").at[1], R("dhr").at[0], (p, d, lax.rem(t + 1, 4)))
     dn_left = links.remote(R("xh").at[0], R("dhr").at[1], (p, d, lax.rem(t + 3, 4)))
-    gain_links = [links.remote(R("dgs").at[k], R("dgr").at[k], dev) for k, dev in enumerate([at["C"]] + zbits + [at["Y"]])]
+    gain_over_t = [links.remote(R("dgt").at[t], R("dgt").at[t], at[f]) for f in ("C", "Y", "T")]
+    gain_over_d = []
+    for k in range(1, dp):
+        to = lax.rem(d + k, dp)
+        gain_over_d.append(links.remote(R("dgd").at[d], R("dgd").at[d], (p, to, t)))
 
     @pl.when(is_dec)
     def _():
@@ -409,7 +413,7 @@
     for c in loads:
         c.start()
     barrier = pltpu.get_barrier_semaphore()
-    partners = [at["C"], at["Y"], at["T"], at["X"]] + zbits
+    partners = [at["C"], at["Y"], at["T"], at["X"]] + [(p, lax.rem(d + k, dp), t) for k in range(1, dp)]
     for dev in partners:
         pl.semaphore_signal(barrier, inc=1, device_id=dev, device_id_type=MESH)
     pl.semaphore_wait(barrier, len(partners))
@@ -465,8 +469,8 @@
         @pl.when(i == 1)
         def _():
             g_wa.step1(1)
+            g_wo.step1()
             g_wa.step2(0)
-            g_wo.step1()
 
             @pl.when(is_dec)
             def _():
@@ -474,26 +478,19 @@
                 g_c0.start()
                 g_w2.start()
                 g_w1.start()
-
+                g_c1.step1()
+
+            pl.when(is_enc)(lambda: g_w1.step1(0))
             g_wa.step2(1)
 
         @pl.when(i == 2)
         def _():
-            pl.when(is_enc)(lambda: g_w1.step1(0))
-            pl.when(is_dec)(g_c1.step1)
             g_wo.step2()
+            pl.when(is_enc)(lambda: g_w1.step1(1))
 
         @pl.when(i == 3)
         def _():
-            @pl.when(is_enc)
-            def _():
-                g_w1.step1(1)
-                g_w1.step2(0)
-
-            @pl.when(is_dec)
-            def _():
-                g_c0.step1()
-                g_c1.step2()
+            pl.when(is_dec)(g_c0.step1)
 
     def wait_ready(i, *weights):
         for k in range(4):
@@ -545,13 +542,24 @@
             return s
 
         g_w2.step1(0)
+        g_w1.step2(0)
 
         def near(i, _):
             wait_ready(i, g_w1, g_w2)
             s = up(i)
             r2_ref[...] += mm(u_ref[s], R("w2")[s])
-            pl.when(i == 0)(lambda: g_w1.step2(1))
-            pl.when(i == 1)(lambda: g_w2.step1(1))
+
+            @pl.when(i == 0)
+            def _():
+                g_w2.step1(1)
+                g_w1.step2(1)
+
+            @pl.when(i == 1)
+            def _():
+                g_w2.step1(2)
+                g_w2.step2(0)
+                g_w2.step1(3)
+
             return 0
 
         lax.fori_loop(0, 2, near, 0)
@@ -559,8 +567,13 @@
         def far(i, _):
             wait_ready(i, g_w1)
             up(i)
-            pl.when(i == 2)(lambda: g_w2.step2(0))
-            pl.when(i == 3)(lambda: g_w2.step2(1))
+            pl.when(i == 2)(lambda: g_w2.step2(1))
+
+            @pl.when(i == 3)
+            def _():
+                g_w2.step2(2)
+                g_w2.step2(3)
+
             return 0
 
         lax.fori_loop(2, 4, far, 0)
@@ -593,8 +606,8 @@
 
     @pl.when(is_dec)
     def _():
-        g_c0.step2()
         g_w2.step1(0)
+        g_c1.step2()
         for k in range(4):
             g_c1.ready(k)
         pick_shape = (width // 4, width // 2)
@@ -610,8 +623,9 @@
             cqw_ref[span, :], cow_ref[span, :] = unweave(0, m)
         cq_ref[...] = mm(n2_ref[...], cqw_ref[...]).astype(BF16) * scale
         g_w2.step1(1)
-        g_w2.step2(0)
-        g_w1.step1(0)
+        g_c0.step2()
+        g_w2.step1(2)
+        g_w2.step1(3)
         kv_ref[...] = jnp.zeros_like(kv_ref)
         for r in range(rows):
             cols[r] = seg_column(1, r)
@@ -624,12 +638,15 @@
             for s in range(4):
                 c0_ref[span, 2 * s * hw : (2 * s + 1) * hw] = ck[:, s * hw : (s + 1) * hw]
                 c0_ref[span, (2 * s + 1) * hw : (2 * s + 2) * hw] = cv[:, s * hw : (s + 1) * hw]
+        g_w1.step1(0)
+        g_w2.step2(0)
         g_w2.step2(1)
-        g_w1.step1(1)
-        g_w1.step2(0)
         for g in (g_c1, g_c0):
             g.finish()
         R("dmf")[...] = jnp.zeros_like(R("dmf"))
+        g_w1.step1(1)
+        g_w2.step2(2)
+        g_w2.step2(3)
         for k in range(4):
             g_w2.ready(k)
 
@@ -638,6 +655,7 @@
             return 0
 
         lax.fori_loop(0, 4, early, 0)
+        g_w1.step2(0)
         g_w1.step2(1)
         for k in range(4):
             g_w1.ready(k)
@@ -653,7 +671,7 @@
                 place = pl.ds(pl.multiple_of((2 - t) * (own - side), HALO), side)
                 acc_ref[place, :] += R("rct")[r].astype(F32)
 
-            R("dm")[r] = acc_ref[span, :].astype(BF16)
+            R("rcc")[r] = acc_ref[span, :].astype(BF16)
             dm_x(r).start()
 
         def row(r, _):
@@ -716,17 +734,6 @@
             g_ref[rs, :] = g2
             gb_ref[rs, :] = g2.astype(BF16)
             do_ref[rs, :] = mm(gb_ref[rs, :], cow_ref[...]).astype(BF16)
-
-            @pl.when(r == rows - 1)
-            def _():
-                def w2_grad(i, _):
-                    s = far_first(i)
-                    R("dw2")[rowsl(s, width), :] = mm_tn(cot_ref[...], u_ref[s]).astype(BF16)
-                    sends(r_w2, i)
-                    return 0
-
-                lax.fori_loop(0, 4, w2_grad, 0)
-
             ws = pl.ds(pl.multiple_of(r * cwin, HALO), cwin)
 
             def back(i, _):
@@ -744,16 +751,21 @@
             R("dmf")[in_row(r, cwindow), :] = mm_nt(dkv_ref[ws, :], c0_ref[...]).astype(BF16)
             dm_c(r).start()
             pl.when(inner)(dm_t(r).start)
+
+            @pl.when(r == rows - 1)
+            def _():
+                def w2_grad(i, _):
+                    s = far_first(i)
+                    R("dw2")[rowsl(s, width), :] = mm_tn(cot_ref[...], u_ref[s]).astype(BF16)
+                    sends(r_w2, i)
+                    return 0
+
+                lax.fori_loop(0, 4, w2_grad, 0)
+                settle(r)
+
             dx, dg = norm_back(r1_ref[rs, :], gain1, mm_nt(cq_ref[rs, :], cqw_ref[...]))
             R("dg")[r, pl.ds(1, 1), :] = dg
             g_ref[rs, :] += dx
-
-            @pl.when(r == rows - 1)
-            def _():
-                r_w2[0].core_done()
-                r_w2[1].core_done()
-                settle(r)
-
             return 0
 
         lax.fori_loop(0, rows, row, 0)
@@ -765,6 +777,12 @@
             s = far_first(i)
             R("dmf")[rowsl(s, width), :] = mm_tn(n3_ref[...], gp_ref[s]).astype(BF16)
             sends(r_w1, i)
+
+            @pl.when(i == 0)
+            def _():
+                r_w2[0].core_done()
+                r_w2[1].core_done()
+
             return 0
 
         lax.fori_loop(0, 4, w1_grad, 0)
@@ -799,7 +817,7 @@
         def row(r, _):
             rs = rowsl(r)
             dm_x(r).wait_recv()
-            dx, dg = norm_back(r2_ref[rs, :], gain2, R("dm")[r].astype(F32))
+            dx, dg = norm_back(r2_ref[rs, :], gain2, R("rcc")[r].astype(F32))
             R("dg")[r, pl.ds(2, 1), :] = dg
             g_ref[rs, :] = dx
             gb_ref[rs, :] = dx.astype(BF16)
@@ -870,36 +888,22 @@
 
         @pl.when(i == 0)
         def _():
+            r_w2[0].z_done(0)
+            pl.when(is_dec)(r_c1.core_done)
             r_wo.core_done()
-            r_w2[0].z_done(0)
             r_w2[1].y_done()
 
-        @pl.when((i == 1) & is_dec)
+        @pl.when(i == 2)
         def _():
+            r_w1[1].z_done(0)
             r_w1[0].y_done()
-            for k in range(1, len(zbits)):
-                r_w2[0].z_done(k)
-
-        @pl.when((i == 2) & is_enc)
+
+        @pl.when(i == 3)
         def _():
-            r_w1[0].y_done()
+            pl.when(is_enc)(r_wo.y_done)
             r_w2[1].z_done(0, w2_out[1])
-
-        @pl.when((i == 2) & is_dec)
-        def _():
-            r_w2[1].z_done(0, w2_out[1])
-            r_w1[0].z_done(0, w1_out[0])
-
-        @pl.when((i == 3) & is_enc)
-        def _():
-            for k in range(1, len(zbits)):
-                r_w2[0].z_done(k)
-            r_w2[1].z_rest(w2_out[1])
-
-        @pl.when((i == 3) & is_dec)
-        def _():
-            r_w1[1].y_done()
-            r_w2[1].z_rest(w2_out[1])
+            r_w2[0].z_rest()
+            pl.when(is_dec)(r_c0.y_done)
 
         return 0
 
@@ -909,7 +913,6 @@
         R("xh")[1, r] = acc_ref[pl.ds(r * win + HALO + own, HALO), :].astype(BF16)
     pl.when(t < 3)(dn_right.start)
     pl.when(t > 0)(dn_left.start)
-    pl.when(is_dec)(r_c1.core_done)
     for j in range(3):
         r_wa[j].core_done()
 
@@ -921,16 +924,14 @@
     def _():
         R("dhr")[1] = jnp.zeros((rows, HALO, width), BF16)
 
-    @pl.when(is_enc)
-    def _():
-        r_w1[1].y_done()
+    @pl.when(is_dec)
+    def _():
         r_w1[0].z_done(0, w1_out[0])
-
-    @pl.when(is_dec)
-    def _():
-        r_w1[0].z_rest(w1_out[0])
-        r_w1[1].z_done(0, w1_out[1])
-        r_c0.y_done()
+        r_w1[1].z_rest()
+        r_c1.y_done()
+        r_w2[1].z_rest(w2_out[1])
+        r_wo.y_done()
+        r_c0.z_done(0, R("dc0"))
 
     pl.when(t > 0)(dn_right.wait_recv)
     pl.when(t < 3)(dn_left.wait_recv)
@@ -944,72 +945,70 @@
         dx, dg = norm_back(x_ref[r].astype(F32), gain0, acc_ref[pl.ds(r * win + HALO, own), :])
         gb_ref[rs, :] = (g_ref[rs, :] + dx).astype(BF16)
         total += dg
+    dgt, dgd = R("dgt"), R("dgd")
+    dgt[t] = jnp.zeros((8, width), F32)
+    dgt[t, pl.ds(0, 1), :] = total
+    dgt[t, pl.ds(1, 2), :] = sum(R("dg")[r, pl.ds(1, 2), :] for r in range(rows))
+    for c in gain_over_t:
+        c.start()
     gx_out = links.here(gb_ref, R("gx"))
     gx_out.start()
-    R("dgs")[0] = jnp.zeros((8, width), F32)
-    R("dgs")[0, pl.ds(0, 1), :] = total
-    R("dgs")[0, pl.ds(1, 2), :] = sum(R("dg")[r, pl.ds(1, 2), :] for r in range(rows))
-    gain_links[0].start()
-
-    def gain_step(k):
-        gain_links[k].wait_recv()
-        if k + 1 < len(gain_links):
-            R("dgs")[k + 1] = R("dgs")[k] + R("dgr")[k]
-            gain_links[k + 1].start()
-        else:
-            R("dgain")[...] = pltpu.roll(R("dgs")[k] + R("dgr")[k], lax.rem(width - d * (width // dp), width), 1)
-
-    last_gain = len(gain_links) - 1
+
+    def gains_over_t():
+        for c in gain_over_t:
+            c.wait_recv()
+        dgd[d] = dgt[0] + dgt[1] + dgt[2] + dgt[3]
+        for c in gain_over_d:
+            c.start()
+
+    def gains_over_d():
+        total = jnp.zeros((8, width), F32)
+        for c in gain_over_d:
+            c.wait_recv()
+        for k in range(dp):
+            total += dgd[k]
+        R("dgain")[...] = pltpu.roll(total, lax.rem(width - d * (width // dp), width), 1)
 
     @pl.when(is_enc)
     def _():
+        r_w2[0].y_done(w2_out[0])
+        r_w1[0].z_done(0, w1_out[0])
+        r_w1[1].z_rest()
+        r_wa[0].y_done()
+        r_wo.z_done(0, R("dwo_o"))
+        r_wa[1].y_done()
+        gains_over_t()
+        r_w2[1].z_rest(w2_out[1])
+        r_wa[0].z_done(0, wa_out[0])
+        r_wa[2].y_done()
         r_w1[0].z_rest(w1_out[0])
-        gain_step(0)
-        r_w1[1].z_done(0, w1_out[1])
-        r_wo.y_done()
+        r_wa[1].z_done(0, wa_out[1])
+        r_w1[1].y_done(w1_out[1])
+        gains_over_d()
+        r_wo.z_rest(R("dwo_o"))
+
+    @pl.when(is_dec)
+    def _():
+        r_w2[0].y_done(w2_out[0])
+        r_w1[0].z_rest(w1_out[0])
+        r_c1.z_done(0, R("dc"))
         r_wa[0].y_done()
-        r_w1[1].z_rest(w1_out[1])
         r_wo.z_done(0, R("dwo_o"))
-        for k in range(1, last_gain):
-            gain_step(k)
         r_wa[1].y_done()
-        r_wa[0].z_done(0, wa_out[0])
-        r_wo.z_rest(R("dwo_o"))
-        r_wa[2].y_done()
-        r_wa[1].z_done(0, wa_out[1])
-        r_wa[0].z_rest(wa_out[0])
-        r_w2[0].y_done(w2_out[0])
-        r_wa[2].z_done(0, wa_out[2])
-        r_wa[1].z_rest(wa_out[1])
-        gain_step(last_gain)
-        r_wa[2].z_rest(wa_out[2])
-
-    @pl.when(is_dec)
-    def _():
-        r_w1[1].z_rest(w1_out[1])
-        r_c0.z_done(0, R("dc0"))
-        gain_step(0)
-        r_wo.y_done()
         r_c0.z_rest(R("dc0"))
         c0_back.start()
-        r_c1.y_done()
-        r_wo.z_done(0, R("dwo_o"))
-        for k in range(1, last_gain):
-            gain_step(k)
-        r_wa[0].y_done()
-        r_c1.z_done(0, R("dc"))
+        r_wa[0].z_done(0, wa_out[0])
+        r_wa[2].y_done()
+        r_c1.z_rest(R("dc"))
+        r_wa[1].z_done(0, wa_out[1])
+        r_w1[1].y_done(w1_out[1])
+        gains_over_t()
         r_wo.z_rest(R("dwo_o"))
-        r_wa[1].y_done()
-        r_wa[0].z_done(0, wa_out[0])
-        r_c1.z_rest(R("dc"))
-        r_wa[2].y_done()
-        r_wa[1].z_done(0, wa_out[1])
-        r_wa[0].z_rest(wa_out[0])
-        r_w2[0].y_done(w2_out[0])
-        r_wa[2].z_done(0, wa_out[2])
-        r_wa[1].z_rest(wa_out[1])
-        gain_step(last_gain)
-        r_wa[2].z_rest(wa_out[2])
+        gains_over_d()
+
+    r_wa[2].z_done(0, wa_out[2])
+    for j in range(3):
+        r_wa[j].z_rest(wa_out[j])
 
     sec_out.wait()
     gx_out.wait()
@@ -1017,7 +1016,7 @@
         g.finish()
     for g in r_w2 + r_w1 + [r_wo] + r_wa:
         g.finish()
-    for c in gain_links:
+    for c in gain_over_t + gain_over_d:
         c.wait_send()
     pl.when(t < 3)(x_right.wait_send)
     pl.when(t > 0)(x_left.wait_send)
@@ -1094,22 +1093,22 @@
         cp=((max(8 * own, 4 * width), cwin), BF16), cinv=((own, width), BF16), oc=((tokens, width), BF16),
         cols=((rows, own, 128), F32), keys=((rows, 8, cwin), F32),
         dkv=((rows * cwin, 8 * hw), BF16), dmf=((max(rows * slots, 4 * width), max(width, fw)), BF16),
-        rcc=((rows, own, width), BF16), rct=((rows, side, width), BF16), dm=((rows, own, width), BF16),
+        rcc=((rows, own, width), BF16), rct=((rows, side, width), BF16),
         dg=((rows, 8, width), F32),
         dqkv=((rows * win, 3 * hw), BF16), dhr=((2, rows, HALO, width), BF16),
-        dgs=((2 + zsteps, 8, width), F32), dgr=((2 + zsteps, 8, width), F32),
+        dgt=((4, 8, width), F32), dgd=((dp, 8, width), F32),
         dw2=((4 * width, fw), BF16), dwo=((width, 4 * hw), BF16),
         dc0=((share, 2 * hw), F32), dc0r=((share, 2 * hw), F32),
     )
     sums = dict(w20=fw // 2, w21=fw // 2, w10=fw // 2, w11=fw // 2, wo=hw, wa0=hw, wa1=hw, wa2=hw, c0=2 * hw, c1=2 * hw)
     for name, m in sums.items():
-        shards = 2 if name == "w20" else 1
+        shards = 2 if name in ("w20", "w11") else 1
         vm["rc_" + name] = ((2, width, m), BF16)
         vm["ry_" + name] = ((share if shards == 2 else width, m), BF16)
         vm["zb_" + name] = ((shards, dp, share, m), BF16)
         for k in range(zsteps):
             vm[f"zr{k}_{name}"] = ((shards, dp >> (k + 1), share, m), BF16)
-    copies = 150 + 12 * zsteps
+    copies = 140 + 12 * zsteps + dp
     sems = dict(send=pltpu.SemaphoreType.DMA((copies,)), recv=pltpu.SemaphoreType.DMA((copies,)), local=pltpu.SemaphoreType.DMA((16,)))
     in_hbm = {n for n in ins if n.endswith("_h")}
     out_hbm = {"sec", "gx"}
@@ -1123,7 +1122,6 @@
         compiler_params=pltpu.CompilerParams(vmem_limit_bytes=VMEM_LIMIT, collective_id=0, has_side_effects=True),
     )(*ins.values())
     aligned = share % 128 == 0
-    flat, turned = (share, hw), (hw, share)
     sec, gx, dgain, da, dwo, dc, dw1, dw2 = pl.pallas_call(
         functools.partial(arrange, aligned),
         name="arrange",

time: 149 us -> 142 us (0.953)
  Pallas kernels: 149 us -> 142 us
    pallas_call x1, Pallas kernels: 146 us -> 139 us  [body(): pl.pallas_call(functools.partial(layers, list(ins) + list(outs) + list(vm...]
where the time goes in v5:
time: 142 us
  Pallas kernels  142 us (100%)
    pallas_call x1, Pallas kernels, body(): pl.pallas_call(functools.partial(layers, list(ins) + list(outs) + list(vm...  139 us
    pallas_call x1, Pallas kernels, body(): pl.pallas_call(functools.partial(arrange, aligned), name='arrange', out_s...  2.9 us

profile of v5, /device:TPU:0, one launch (start us, length us, event | category | flops | bytes accessed | tf_op | source)
XLA Modules:
  0.0 142.2 jit_solution(15381684028616722984)
XLA Ops:
  0.6 138.7 %layers.1 = (bf16[512,512]{1,0:T(8,128)(2,1)}, bf16[512,512]{1,0:T(8,128)(2,1)}, f32[8,512]{1,0:T(8,128)}, f32[128,384]{1,0:T(8,128)}, f32[128,128]{1,0:T(8,128)...) custom-call(bf16[2,256,512]{2,1,0:T(8,128)(2,1)} %bitcast.20, s32[2,2,1024]{2,1,0:T(2,128)} %refs_1_.1, ...), custom_call_target="tpu_custom_call" | custom-call | tf_op jit(solution)/shard_map/layers/pallas_call | solution.py:1115
  139.3 2.9 %arrange.1 = (bf16[512,512]{1,0:T(8,128)(2,1)}, bf16[512,512]{1,0:T(8,128)(2,1)}, f32[3,1,128]{2,1,0:T(1,128)}, f32[3,128,128]{2,1,0:T(8,128)}, f32[128,128]{1,0...) custom-call(bf16[512,512]{1,0:T(8,128)(2,1)} %get-tuple-element.24.sec, ...), custom_call_target="tpu_custom_call" | custom-call | tf_op jit(solution)/shard_map/arrange/pallas_call | solution.py:1125

commit v6 on v5

--- a/solution.py
+++ b/solution.py
@@ -602,7 +602,6 @@
     kv_ref, cq_ref, cp_ref, dkv_ref, cinv_ref = R("kv"), R("cq"), R("cp"), R("dkv"), R("cinv")
     c0_ref, cqw_ref, cow_ref, oc_ref, cot_ref = R("c0"), R("cqw"), R("cow"), R("oc"), R("cot")
     cols, keys_ref = R("cols"), R("keys")
-    half = 4 * hw
 
     @pl.when(is_dec)
     def _():
@@ -641,12 +640,13 @@
         g_w1.step1(0)
         g_w2.step2(0)
         g_w2.step2(1)
+        g_w1.step1(1)
         for g in (g_c1, g_c0):
             g.finish()
         R("dmf")[...] = jnp.zeros_like(R("dmf"))
-        g_w1.step1(1)
         g_w2.step2(2)
         g_w2.step2(3)
+        g_w1.step2(0)
         for k in range(4):
             g_w2.ready(k)
 
@@ -655,10 +655,11 @@
             return 0
 
         lax.fori_loop(0, 4, early, 0)
-        g_w1.step2(0)
-        g_w1.step2(1)
-        for k in range(4):
-            g_w1.ready(k)
+
+        def pass_memory_on(r):
+            mem_x(r).wait_recv()
+            mem_c(r).start()
+            pl.when(inner)(mem_t(r).start)
 
         def settle(r):
             span = pl.ds(0, own)
@@ -678,14 +679,15 @@
             rs = rowsl(r)
 
             def project(span):
-                for j in range(2):
-                    kv = mm(R("memf")[in_row(r, span), :], c0_ref[:, j * half : (j + 1) * half])
-                    kv_ref[span, j * half : (j + 1) * half] = kv.astype(BF16)
-
-            mem_x(r).wait_recv()
-            mem_c(r).start()
-            pl.when(inner)(mem_t(r).start)
+                kv_ref[span, :] = mm(R("memf")[in_row(r, span), :], c0_ref[...]).astype(BF16)
+
+            @pl.when(r == 0)
+            def _():
+                g_w1.step2(1)
+                pass_memory_on(0)
+
             project(block)
+            pl.when(r > 0)(lambda: settle(r - 1))
             mem_c(r).wait_recv()
             project(block1)
 
@@ -709,25 +711,31 @@
                 return 0
 
             lax.fori_loop(0, 2, cross, 0)
-            pl.when(r > 0)(lambda: settle(r - 1))
+            pl.when(r < rows - 1)(lambda: pass_memory_on(r + 1))
             r2_ref[rs, :] = r1_ref[rs, :] + mm_nt(oc_ref[rs, :], cow_ref[...])
             n3_ref[rs, :] = norm(r2_ref[rs, :], gain2).astype(BF16)
+
+            @pl.when(r == 0)
+            def _():
+                for k in range(4):
+                    g_w1.ready(k)
+
             dn = pl.ds(0, own)
             acc_ref[dn, :] = jnp.zeros((own, width), F32)
-            g_ref[rs, :] = r2_ref[rs, :]
-
-            def feed(s, _):
-                u, gp = gelu_parts(mm(n3_ref[rs, :], R("w1")[s]))
-                u = u.astype(BF16)
-                u_ref[s, rs, :] = u
-                g_ref[rs, :] += mm(u, R("w2")[s])
-                dh = (gp_ref[s, rs, :].astype(F32) * gp).astype(BF16)
-                gp_ref[s, rs, :] = dh
-                acc_ref[dn, :] += mm_nt(dh, R("w1")[s])
+
+            def feed(i, _):
+                back = acc_ref[dn, :]
+                for s in (2 * i, 2 * i + 1):
+                    u, gp = gelu_parts(mm(n3_ref[rs, :], R("w1")[s]))
+                    u = u.astype(BF16)
+                    u_ref[s, rs, :] = u
+                    dh = (gp_ref[s, rs, :].astype(F32) * gp).astype(BF16)
+                    gp_ref[s, rs, :] = dh
+                    back += mm_nt(dh, R("w1")[s])
+                acc_ref[dn, :] = back
                 return 0
 
-            lax.fori_loop(0, 4, feed, 0)
-            sec_ref[rs, :] = g_ref[rs, :].astype(BF16)
+            lax.fori_loop(0, 2, feed, 0)
             dx, dg = norm_back(r2_ref[rs, :], gain2, acc_ref[dn, :])
             R("dg")[r, pl.ds(2, 1), :] = dg
             g2 = cot_ref[rs, :].astype(F32) + dx
@@ -763,9 +771,6 @@
                 lax.fori_loop(0, 4, w2_grad, 0)
                 settle(r)
 
-            dx, dg = norm_back(r1_ref[rs, :], gain1, mm_nt(cq_ref[rs, :], cqw_ref[...]))
-            R("dg")[r, pl.ds(1, 1), :] = dg
-            g_ref[rs, :] += dx
             return 0
 
         lax.fori_loop(0, rows, row, 0)
@@ -803,6 +808,14 @@
             return 0
 
         lax.fori_loop(0, 4, c0_grad, 0)
+        def query_norm(r, _):
+            rs = rowsl(r)
+            dx, dg = norm_back(r1_ref[rs, :], gain1, mm_nt(cq_ref[rs, :], cqw_ref[...]))
+            R("dg")[r, pl.ds(1, 1), :] = dg
+            g_ref[rs, :] += dx
+            return 0
+
+        lax.fori_loop(0, rows, query_norm, 0)
         dcq = mm_tn(n2_ref[...], cq_ref[...]).astype(BF16)
         dco = mm_tn(gb_ref[...], oc_ref[...]).astype(BF16)
         r_c0.core_done()
@@ -838,15 +851,15 @@
         def w1_grad(i, _):
             s = far_first(i)
             dh = (mm_nt(gb_ref[...], R("w2")[s]) * gp_ref[s].astype(F32)).astype(BF16)
+
+            @pl.when(i == 1)
+            def _():
+                r_w2[0].core_done()
+                r_w2[1].core_done()
+
             R("dmf")[rowsl(s, width), :] = mm_tn(n2_ref[...], dh).astype(BF16)
             sends(r_w1, i)
             acc_ref[dn, :] += mm_nt(dh, R("w1")[s])
-
-            @pl.when(i == 0)
-            def _():
-                r_w2[0].core_done()
-                r_w2[1].core_done()
-
             return 0
 
         lax.fori_loop(0, 4, w1_grad, 0)
@@ -859,7 +872,7 @@
         g_ref[...] += dx
 
     sec_out = links.here(sec_ref, R("sec"))
-    sec_out.start()
+    pl.when(is_enc)(sec_out.start)
     gb_ref[...] = g_ref[...].astype(BF16)
     R("dwo")[...] = mm_tn(gb_ref[...], o_ref[...]).astype(BF16)
     r_wo.core_send(0)
@@ -915,6 +928,19 @@
     pl.when(t > 0)(dn_left.start)
     for j in range(3):
         r_wa[j].core_done()
+
+    @pl.when(is_dec)
+    def _():
+        def decoded(r, _):
+            rs = rowsl(r)
+            total = r2_ref[rs, :]
+            for s in range(4):
+                total += mm(u_ref[s, rs, :], R("w2")[s])
+            sec_ref[rs, :] = total.astype(BF16)
+            return 0
+
+        lax.fori_loop(0, rows, decoded, 0)
+        sec_out.start()
 
     @pl.when(t == 0)
     def _():

time: 142 us -> 139 us (0.979)
  Pallas kernels: 142 us -> 138 us
    pallas_call x1, Pallas kernels: 139 us -> 135 us  [body(): pl.pallas_call(functools.partial(layers, list(ins) + list(outs) + list(vm...]
where the time goes in v6:
time: 139 us
  Pallas kernels  138 us (99%)
    pallas_call x1, Pallas kernels, body(): pl.pallas_call(functools.partial(layers, list(ins) + list(outs) + list(vm...  135 us
    pallas_call x1, Pallas kernels, body(): pl.pallas_call(functools.partial(arrange, aligned), name='arrange', out_s...  2.9 us

profile of v6, /device:TPU:0, one launch (start us, length us, event | category | flops | bytes accessed | tf_op | source)
XLA Modules:
  0.0 139.0 jit_solution(13497253922859422461)
XLA Ops:
  0.6 135.4 %layers.1 = (bf16[512,512]{1,0:T(8,128)(2,1)}, bf16[512,512]{1,0:T(8,128)(2,1)}, f32[8,512]{1,0:T(8,128)}, f32[128,384]{1,0:T(8,128)}, f32[128,128]{1,0:T(8,128)...) custom-call(bf16[2,256,512]{2,1,0:T(8,128)(2,1)} %bitcast.20, s32[2,2,1024]{2,1,0:T(2,128)} %refs_1_.1, ...), custom_call_target="tpu_custom_call" | custom-call | tf_op jit(solution)/shard_map/layers/pallas_call | solution.py:1141
  136.1 2.9 %arrange.1 = (bf16[512,512]{1,0:T(8,128)(2,1)}, bf16[512,512]{1,0:T(8,128)(2,1)}, f32[3,1,128]{2,1,0:T(1,128)}, f32[3,128,128]{2,1,0:T(8,128)}, f32[128,128]{1,0...) custom-call(bf16[512,512]{1,0:T(8,128)(2,1)} %get-tuple-element.24.sec, ...), custom_call_target="tpu_custom_call" | custom-call | tf_op jit(solution)/shard_map/arrange/pallas_call | solution.py:1151

commit v7 on v6

--- a/solution.py
+++ b/solution.py
@@ -143,7 +143,7 @@
 
 
 class Gather:
-    def __init__(self, links, src, slot, depth, at, pieces=1, planes=None):
+    def __init__(self, links, src, slot, depth, at, pieces=1, planes=None, last_straight=False):
         t, t2 = at["t"], at["t2"]
         half = depth // 2
         n = half // pieces
@@ -155,6 +155,7 @@
         else:
             self.own = [links.here(src.at[i], slot(t, whole, i)) for i in range(planes)]
         self.inner = src is None or planes is not None
+        self.straight = pieces - 1 if last_straight else None
         src = slot(t, whole) if self.inner else src
         self.core = links.remote(src, slot(t, whole), at["C"])
         self.over_y, self.over_z, self.core_a, self.core_b = [], [], [], []
@@ -162,7 +163,10 @@
             mine = pl.ds(pl.multiple_of(at["b"] * half + i * n, n), n)
             other = pl.ds(pl.multiple_of((1 - at["b"]) * half + i * n, n), n)
             self.over_y.append(links.remote(src.at[mine], slot(t, mine), at["Y"]))
-            self.over_z.append(links.remote(slot(t2, mine), slot(t2, mine), at["Z"][0]))
+            if last_straight and i == pieces - 1:
+                self.over_z.append(links.remote(src.at[other], slot(t, other), at["Y"]))
+            else:
+                self.over_z.append(links.remote(slot(t2, mine), slot(t2, mine), at["Z"][0]))
             self.core_a.append(links.remote(slot(t2, mine), slot(t2, mine), at["C"]))
             self.core_b.append(links.remote(slot(t2, other), slot(t2, other), at["C"]))
 
@@ -174,11 +178,14 @@
                 c.wait()
         for c in self.over_y:
             c.start()
+        if self.straight is not None:
+            self.over_z[self.straight].start()
         self.core.start()
 
     def step1(self, i=0):
         self.over_y[i].wait_recv()
-        self.over_z[i].start()
+        if i != self.straight:
+            self.over_z[i].start()
         self.core_a[i].start()
 
     def step2(self, i=0):
@@ -338,7 +345,7 @@
     g_wa = Gather(links, R("wa_h"), by_shard("wa", hw), width, at, 2, 3)
     g_wo = Gather(links, R("wo_h"), by_shard("wo"), hw, at)
     g_w1 = Gather(links, R("w1_h"), by_shard("w1"), width, at, 2)
-    g_w2 = Gather(links, R("w2_h"), by_shard("w2"), fw, at, 4)
+    g_w2 = Gather(links, R("w2_h"), by_shard("w2"), fw, at, 4, None, True)
     g_c1 = Gather(links, R("cx_h"), by_columns("dmf", hw, 0), 2 * width, at)
     c0_x = links.remote(R("cx_h"), R("dmf").at[pl.ds(2 * width, 2 * width), lanes(t)], at["X"])
     g_c0 = Gather(links, None, by_columns("dmf", hw, 2 * width), 2 * width, at)
@@ -697,7 +704,7 @@
                 project(edge_in)
 
             def cross(i, _):
-                for s in (2 * i, 2 * i + 1):
+                for s in range(4):
                     def keep(h, e):
                         cp_ref[rowsl(2 * s + h), :] = e
 
@@ -710,7 +717,7 @@
                     cinv_ref[:, lanes(s)] = inv.astype(BF16)
                 return 0
 
-            lax.fori_loop(0, 2, cross, 0)
+            cross(0, 0)
             pl.when(r < rows - 1)(lambda: pass_memory_on(r + 1))
             r2_ref[rs, :] = r1_ref[rs, :] + mm_nt(oc_ref[rs, :], cow_ref[...])
             n3_ref[rs, :] = norm(r2_ref[rs, :], gain2).astype(BF16)
@@ -725,7 +732,7 @@
 
             def feed(i, _):
                 back = acc_ref[dn, :]
-                for s in (2 * i, 2 * i + 1):
+                for s in range(4):
                     u, gp = gelu_parts(mm(n3_ref[rs, :], R("w1")[s]))
                     u = u.astype(BF16)
                     u_ref[s, rs, :] = u
@@ -735,7 +742,7 @@
                 acc_ref[dn, :] = back
                 return 0
 
-            lax.fori_loop(0, 2, feed, 0)
+            feed(0, 0)
             dx, dg = norm_back(r2_ref[rs, :], gain2, acc_ref[dn, :])
             R("dg")[r, pl.ds(2, 1), :] = dg
             g2 = cot_ref[rs, :].astype(F32) + dx
@@ -745,7 +752,7 @@
             ws = pl.ds(pl.multiple_of(r * cwin, HALO), cwin)
 
             def back(i, _):
-                for s in (2 * i, 2 * i + 1):
+                for s in range(4):
                     dq, dk, dv = attend_back(
                         cq_ref[rs, lanes(s)], kv_ref[cwindow, lanes(2 * s)], kv_ref[cwindow, lanes(2 * s + 1)],
                         do_ref[rs, lanes(s)], oc_ref[rs, lanes(s)], cinv_ref[:, lanes(s)], lambda h: cp_ref[rowsl(2 * s + h), :],
@@ -755,7 +762,7 @@
                     dkv_ref[ws, lanes(2 * s + 1)] = dv
                 return 0
 
-            lax.fori_loop(0, 2, back, 0)
+            back(0, 0)
             R("dmf")[in_row(r, cwindow), :] = mm_nt(dkv_ref[ws, :], c0_ref[...]).astype(BF16)
             dm_c(r).start()
             pl.when(inner)(dm_t(r).start)
@@ -827,45 +834,58 @@
 
     @pl.when(is_enc)
     def _():
-        def row(r, _):
+        def receive(r):
             rs = rowsl(r)
             dm_x(r).wait_recv()
             dx, dg = norm_back(r2_ref[rs, :], gain2, R("rcc")[r].astype(F32))
             R("dg")[r, pl.ds(2, 1), :] = dg
             g_ref[rs, :] = dx
             gb_ref[rs, :] = dx.astype(BF16)
+
+        def hidden_back(s, rs):
+            dh = (mm_nt(gb_ref[rs, :], R("w2")[s]) * gp_ref[s, rs, :].astype(F32)).astype(BF16)
+            gp_ref[s, rs, :] = dh
+            acc_ref[rs, :] += mm_nt(dh, R("w1")[s])
+
+        head, last = pl.ds(0, (rows - 1) * own), pl.ds((rows - 1) * own, own)
+        acc_ref[pl.ds(0, tokens), :] = jnp.zeros((tokens, width), F32)
+        for r in range(rows - 1):
+            receive(r)
+
+        def head_grads(s, _):
+            R("dw2")[rowsl(s, width), :] = mm_tn(gb_ref[head, :], u_ref[s, head, :]).astype(BF16)
+            hidden_back(s, head)
             return 0
 
-        lax.fori_loop(0, rows, row, 0)
+        lax.fori_loop(0, 4, head_grads, 0)
+        receive(rows - 1)
 
         def w2_grad(i, _):
             s = far_first(i)
-            R("dw2")[rowsl(s, width), :] = mm_tn(gb_ref[...], u_ref[s]).astype(BF16)
+            part = R("dw2").at[rowsl(s, width)]
+            part[...] = (part[...].astype(F32) + mm_tn(gb_ref[last, :], u_ref[s, last, :])).astype(BF16)
             sends(r_w2, i)
             return 0
 
         lax.fori_loop(0, 4, w2_grad, 0)
-        dn = pl.ds(0, tokens)
-        acc_ref[dn, :] = jnp.zeros((tokens, width), F32)
 
         def w1_grad(i, _):
             s = far_first(i)
-            dh = (mm_nt(gb_ref[...], R("w2")[s]) * gp_ref[s].astype(F32)).astype(BF16)
+            hidden_back(s, last)
 
             @pl.when(i == 1)
             def _():
                 r_w2[0].core_done()
                 r_w2[1].core_done()
 
-            R("dmf")[rowsl(s, width), :] = mm_tn(n2_ref[...], dh).astype(BF16)
+            R("dmf")[rowsl(s, width), :] = mm_tn(n2_ref[...], gp_ref[s]).astype(BF16)
             sends(r_w1, i)
-            acc_ref[dn, :] += mm_nt(dh, R("w1")[s])
             return 0
 
         lax.fori_loop(0, 4, w1_grad, 0)
         r_w1[0].core_done()
         r_w1[1].core_done()
-        dx, dg = norm_back(r1_ref[...], gain1, acc_ref[dn, :])
+        dx, dg = norm_back(r1_ref[...], gain1, acc_ref[pl.ds(0, tokens), :])
         R("dg")[0, pl.ds(1, 1), :] = dg
         for r in range(1, rows):
             R("dg")[r, pl.ds(1, 1), :] = jnp.zeros_like(dg)

time: 139 us -> 134 us (0.964)
  Pallas kernels: 138 us -> 133 us
    pallas_call x1, Pallas kernels: 135 us -> 130 us  [body(): pl.pallas_call(functools.partial(layers, list(ins) + list(outs) + list(vm...]
where the time goes in v7:
time: 134 us
  Pallas kernels  133 us (99%)
    pallas_call x1, Pallas kernels, body(): pl.pallas_call(functools.partial(layers, list(ins) + list(outs) + list(vm...  130 us
    pallas_call x1, Pallas kernels, body(): pl.pallas_call(functools.partial(arrange, aligned), name='arrange', out_s...  2.9 us

profile of v7, /device:TPU:0, one launch (start us, length us, event | category | flops | bytes accessed | tf_op | source)
XLA Modules:
  0.0 133.9 jit_solution(12676995946045720664)
XLA Ops:
  0.6 130.4 %layers.1 = (bf16[512,512]{1,0:T(8,128)(2,1)}, bf16[512,512]{1,0:T(8,128)(2,1)}, f32[8,512]{1,0:T(8,128)}, f32[128,384]{1,0:T(8,128)}, f32[128,128]{1,0:T(8,128)...) custom-call(bf16[2,256,512]{2,1,0:T(8,128)(2,1)} %bitcast.20, s32[2,2,1024]{2,1,0:T(2,128)} %refs_1_.1, ...), custom_call_target="tpu_custom_call" | custom-call | tf_op jit(solution)/shard_map/layers/pallas_call | solution.py:1161
  131.0 2.9 %arrange.1 = (bf16[512,512]{1,0:T(8,128)(2,1)}, bf16[512,512]{1,0:T(8,128)(2,1)}, f32[3,1,128]{2,1,0:T(1,128)}, f32[3,128,128]{2,1,0:T(8,128)}, f32[128,128]{1,0...) custom-call(bf16[512,512]{1,0:T(8,128)(2,1)} %get-tuple-element.24.sec, ...), custom_call_target="tpu_custom_call" | custom-call | tf_op jit(solution)/shard_map/arrange/pallas_call | solution.py:1171

commit v8 on v7

--- a/solution.py
+++ b/solution.py
@@ -63,17 +63,15 @@
 
 
 def attend(q2, k2, v2, mask, keep):
-    low, lowq = lane_low(v2.shape), lane_low(q2.shape)
-    one, zero = jnp.ones_like(v2), jnp.zeros_like(q2)
-    outs = []
-    for h in range(2):
-        qh = jnp.where(lowq, q2, zero) if h == 0 else jnp.where(lowq, zero, q2)
-        s = mask(mm_nt(qh, k2))
-        e = jnp.exp(s - jnp.max(s, axis=-1, keepdims=True)).astype(BF16)
-        keep(h, e)
-        outs.append(mm(e, jnp.where(low, v2, one) if h == 0 else jnp.where(low, one, v2)))
-    inv = 1.0 / swap_halves(pair_join(outs[1], outs[0]))
-    return pair_join(*outs) * inv, inv
+    n, width = q2.shape
+    lowq, zero = lane_low(q2.shape), jnp.zeros_like(q2)
+    s = mm_nt(jnp.concatenate([jnp.where(lowq, q2, zero), jnp.where(lowq, zero, q2)], axis=0), k2)
+    s = jnp.concatenate([mask(s[:n]), mask(s[n:])], axis=0)
+    e = jnp.exp(s - jnp.max(s, axis=-1, keepdims=True)).astype(BF16)
+    keep(e)
+    out = mm(e, jnp.concatenate([v2, jnp.ones_like(v2)], axis=1))
+    inv = 1.0 / pair_join(out[:n, width:], out[n:, width:])
+    return pair_join(out[:n, :width], out[n:, :width]) * inv, inv
 
 
 def attend_back(q2, k2, v2, do2, o2, inv, kept):
@@ -517,8 +515,8 @@
             k_ref[s, r] = packed[r * win : (r + 1) * win, hw : 2 * hw].astype(BF16)
             v_ref[s, r] = packed[r * win : (r + 1) * win, 2 * hw :].astype(BF16)
         for r in range(rows):
-            def keep(h, e):
-                p_ref[s, r, h] = e
+            def keep(e):
+                p_ref[s, r] = e
 
             o2, inv = attend(q_ref[s, r], k_ref[s, r], v_ref[s, r], lambda scores: scores + bias_ref[r], keep)
             o_ref[pl.ds(r * own, own), lanes(s)] = o2.astype(BF16)
@@ -705,8 +703,8 @@
 
             def cross(i, _):
                 for s in range(4):
-                    def keep(h, e):
-                        cp_ref[rowsl(2 * s + h), :] = e
+                    def keep(e):
+                        cp_ref[rowsl(s, 2 * own), :] = e
 
                     def mask(scores):
                         same = spread(cols[r], cwin) == keys_ref[r, pl.ds(0, 1), :]
@@ -860,29 +858,23 @@
         lax.fori_loop(0, 4, head_grads, 0)
         receive(rows - 1)
 
-        def w2_grad(i, _):
+        for i in range(4):
             s = far_first(i)
             part = R("dw2").at[rowsl(s, width)]
             part[...] = (part[...].astype(F32) + mm_tn(gb_ref[last, :], u_ref[s, last, :])).astype(BF16)
-            sends(r_w2, i)
-            return 0
-
-        lax.fori_loop(0, 4, w2_grad, 0)
-
-        def w1_grad(i, _):
+            if i < 2:
+                for reduction in r_w2:
+                    reduction.core_send(i)
+        for i in range(4):
             s = far_first(i)
             hidden_back(s, last)
-
-            @pl.when(i == 1)
-            def _():
+            if i == 1:
                 r_w2[0].core_done()
                 r_w2[1].core_done()
-
             R("dmf")[rowsl(s, width), :] = mm_tn(n2_ref[...], gp_ref[s]).astype(BF16)
-            sends(r_w1, i)
-            return 0
-
-        lax.fori_loop(0, 4, w1_grad, 0)
+            if i < 2:
+                for reduction in r_w1:
+                    reduction.core_send(i)
         r_w1[0].core_done()
         r_w1[1].core_done()
         dx, dg = norm_back(r1_ref[...], gain1, acc_ref[pl.ds(0, tokens), :])
@@ -910,7 +902,7 @@
             rs = pl.ds(r * own, own)
             dq, dk, dv = attend_back(
                 q_ref[s, r], k_ref[s, r], v_ref[s, r], do_ref[rs, lanes(s)], o_ref[rs, lanes(s)], inv_ref[rs, lanes(s)],
-                lambda h: p_ref[s, r, h],
+                lambda h: p_ref[s, r, pl.ds(h * own, own), :],
             )
             dqkv_ref[pl.ds(r * win + HALO, own), :hw] = dq
             dqkv_ref[pl.ds(r * win, win), hw : 2 * hw] = dk
@@ -944,8 +936,9 @@
     for r in range(rows):
         R("xh")[0, r] = acc_ref[pl.ds(r * win, HALO), :].astype(BF16)
         R("xh")[1, r] = acc_ref[pl.ds(r * win + HALO + own, HALO), :].astype(BF16)
+    pl.when(t == 1)(dn_left.start)
     pl.when(t < 3)(dn_right.start)
-    pl.when(t > 0)(dn_left.start)
+    pl.when(t > 1)(dn_left.start)
     for j in range(3):
         r_wa[j].core_done()
 
@@ -1023,14 +1016,13 @@
         r_wa[0].y_done()
         r_wo.z_done(0, R("dwo_o"))
         r_wa[1].y_done()
-        gains_over_t()
         r_w2[1].z_rest(w2_out[1])
         r_wa[0].z_done(0, wa_out[0])
         r_wa[2].y_done()
+        gains_over_t()
         r_w1[0].z_rest(w1_out[0])
         r_wa[1].z_done(0, wa_out[1])
         r_w1[1].y_done(w1_out[1])
-        gains_over_d()
         r_wo.z_rest(R("dwo_o"))
 
     @pl.when(is_dec)
@@ -1050,11 +1042,11 @@
         r_w1[1].y_done(w1_out[1])
         gains_over_t()
         r_wo.z_rest(R("dwo_o"))
-        gains_over_d()
 
     r_wa[2].z_done(0, wa_out[2])
     for j in range(3):
         r_wa[j].z_rest(wa_out[j])
+    gains_over_d()
 
     sec_out.wait()
     gx_out.wait()
@@ -1131,7 +1123,7 @@
         c0=((width, 8 * hw), BF16), cqw=((width, 4 * hw), BF16), cow=((width, 4 * hw), BF16),
         xh=((2, rows, HALO, width), BF16), nw=((rows * win, width), BF16),
         q=((4, rows, own, hw), BF16), k=((4, rows, win, hw), BF16), v=((4, rows, win, hw), BF16),
-        p=((4, rows, 2, own, win), BF16), o=((tokens, width), BF16), inv=((tokens, width), BF16), bias=((rows, own, win), F32),
+        p=((4, rows, 2 * own, win), BF16), o=((tokens, width), BF16), inv=((tokens, width), BF16), bias=((rows, own, win), F32),
         r1=((tokens, width), F32), r2=((tokens, width), F32), n2=((tokens, width), BF16), n3=((tokens, width), BF16),
         u=((4, tokens, fw), BF16), gp=((4, tokens, fw), BF16), secs=((tokens, width), BF16),
         acc=((rows * win, width), F32), g=((tokens, width), F32), gb=((tokens, width), BF16), do=((tokens, width), BF16),

time: 134 us -> 132 us (0.985)
  Pallas kernels: 133 us -> 131 us
    pallas_call x1, Pallas kernels: 130 us -> 128 us  [body(): pl.pallas_call(functools.partial(layers, list(ins) + list(outs) + list(vm...]
where the time goes in v8:
time: 132 us
  Pallas kernels  131 us (99%)
    pallas_call x1, Pallas kernels, body(): pl.pallas_call(functools.partial(layers, list(ins) + list(outs) + list(vm...  128 us
    pallas_call x1, Pallas kernels, body(): pl.pallas_call(functools.partial(arrange, aligned), name='arrange', out_s...  2.9 us

profile of v8, /device:TPU:0, one launch (start us, length us, event | category | flops | bytes accessed | tf_op | source)
XLA Modules:
  0.0 132.0 jit_solution(5922818518168061841)
XLA Ops:
  0.6 128.5 %layers.1 = (bf16[512,512]{1,0:T(8,128)(2,1)}, bf16[512,512]{1,0:T(8,128)(2,1)}, f32[8,512]{1,0:T(8,128)}, f32[128,384]{1,0:T(8,128)}, f32[128,128]{1,0:T(8,128)...) custom-call(bf16[2,256,512]{2,1,0:T(8,128)(2,1)} %bitcast.20, s32[2,2,1024]{2,1,0:T(2,128)} %refs_1_.1, ...), custom_call_target="tpu_custom_call" | custom-call | tf_op jit(solution)/shard_map/layers/pallas_call | solution.py:1153
  129.1 2.9 %arrange.1 = (bf16[512,512]{1,0:T(8,128)(2,1)}, bf16[512,512]{1,0:T(8,128)(2,1)}, f32[3,1,128]{2,1,0:T(1,128)}, f32[3,128,128]{2,1,0:T(8,128)}, f32[128,128]{1,0...) custom-call(bf16[512,512]{1,0:T(8,128)(2,1)} %get-tuple-element.24.sec, ...), custom_call_target="tpu_custom_call" | custom-call | tf_op jit(solution)/shard_map/arrange/pallas_call | solution.py:1163

commit v9 on v8

--- a/solution.py
+++ b/solution.py
@@ -350,18 +350,23 @@
     loads = [links.here(R(n + "_h"), R(n)) for n in ("x", "cot", "segs")]
     x_right = links.remote(R("x_h").at[:, pl.ds(own - HALO, HALO)], R("xh").at[0], (p, d, lax.rem(t + 1, 4)))
     x_left = links.remote(R("x_h").at[:, pl.ds(0, HALO)], R("xh").at[1], (p, d, lax.rem(t + 3, 4)))
-    base_mem, base_memc, base_memt = links.take(rows), links.take(rows), links.take(rows)
+    base_mem, base_memc, base_memt = links.take(2 * rows), links.take(2 * rows), links.take(rows)
     base_dmc, base_dmt, base_dmx = links.take(rows), links.take(rows), links.take(rows)
     block = pl.ds(pl.multiple_of(t * own, own), own)
     block1 = pl.ds(pl.multiple_of(t1 * own, own), own)
     edge_out = pl.ds(pl.multiple_of(lax.rem(own // 2 + side * t, slots), HALO), side)
     edge_in = pl.ds(pl.multiple_of(lax.rem(own // 2 + side * t3, slots), HALO), side)
 
-    def mem_x(r):
-        return links.remote(R("secs").at[rowsl(r)], R("memf").at[in_row(r, block)], at["X"], base_mem + r)
-
-    def mem_c(r):
-        return links.remote(R("memf").at[in_row(r, block)], R("memf").at[in_row(r, block)], at["C"], base_memc + r)
+    def half_block(h):
+        return pl.ds(pl.multiple_of(t * own + h * (own // 2), own // 2), own // 2)
+
+    def mem_x(r, h):
+        half = pl.ds(pl.multiple_of(r * own + h * (own // 2), own // 2), own // 2)
+        return links.remote(R("secs").at[half], R("memf").at[in_row(r, half_block(h))], at["X"], base_mem + 2 * r + h)
+
+    def mem_c(r, h):
+        rows_ = R("memf").at[in_row(r, half_block(h))]
+        return links.remote(rows_, rows_, at["C"], base_memc + 2 * r + h)
 
     def mem_t(r):
         return links.remote(R("memf").at[in_row(r, edge_out)], R("memf").at[in_row(r, edge_out)], at["T"], base_memt + r)
@@ -415,8 +420,6 @@
                 for r in range(rows):
                     R("memf")[pl.ds(r * slots + start, 2 * HALO), :] = jnp.zeros((2 * HALO, width), BF16)
 
-    for c in loads:
-        c.start()
     barrier = pltpu.get_barrier_semaphore()
     partners = [at["C"], at["Y"], at["T"], at["X"]] + [(p, lax.rem(d + k, dp), t) for k in range(1, dp)]
     for dev in partners:
@@ -425,8 +428,11 @@
 
     pl.when(t < 3)(x_right.start)
     pl.when(t > 0)(x_left.start)
+    loads[0].start()
     g_wa.start()
     g_wo.start()
+    for c in loads[1:]:
+        c.start()
 
     @pl.when(is_enc)
     def _():
@@ -450,7 +456,7 @@
         qpos = lax.broadcasted_iota(jnp.int32, (own, win), 0)
         kpos = lax.broadcasted_iota(jnp.int32, (own, win), 1) - HALO
         before = kpos - qpos <= jnp.where(is_enc, 4 * win, 0)
-        bias_ref[r] = jnp.where(same & before, 0.0, MASKED)
+        bias_ref[:, pl.ds(r * win, win)] = jnp.where(same & before, 0.0, MASKED)
 
     @pl.when(t == 0)
     def _():
@@ -518,7 +524,7 @@
             def keep(e):
                 p_ref[s, r] = e
 
-            o2, inv = attend(q_ref[s, r], k_ref[s, r], v_ref[s, r], lambda scores: scores + bias_ref[r], keep)
+            o2, inv = attend(q_ref[s, r], k_ref[s, r], v_ref[s, r], lambda scores: scores + bias_ref[:, pl.ds(r * win, win)], keep)
             o_ref[pl.ds(r * own, own), lanes(s)] = o2.astype(BF16)
             inv_ref[pl.ds(r * own, own), lanes(s)] = inv.astype(BF16)
         after_pair(i)
@@ -590,7 +596,8 @@
             total = r2_ref[rs, :] + mm(u_ref[far1, rs, :], R("w2")[far1]) + mm(u_ref[far2, rs, :], R("w2")[far2])
             r2_ref[rs, :] = total
             sec_ref[rs, :] = norm(total, gain2).astype(BF16)
-            mem_x(r).start()
+            for h in range(2):
+                mem_x(r, h).start()
             return 0
 
         lax.fori_loop(0, rows, row, 0)
@@ -662,8 +669,9 @@
         lax.fori_loop(0, 4, early, 0)
 
         def pass_memory_on(r):
-            mem_x(r).wait_recv()
-            mem_c(r).start()
+            for h in range(2):
+                mem_x(r, h).wait_recv()
+                mem_c(r, h).start()
             pl.when(inner)(mem_t(r).start)
 
         def settle(r):
@@ -691,9 +699,11 @@
                 g_w1.step2(1)
                 pass_memory_on(0)
 
+            bias_ref[:, pl.ds(0, cwin)] = jnp.where(spread(cols[r], cwin) == keys_ref[r, pl.ds(0, 1), :], 0.0, MASKED)
             project(block)
             pl.when(r > 0)(lambda: settle(r - 1))
-            mem_c(r).wait_recv()
+            for h in range(2):
+                mem_c(r, h).wait_recv()
             project(block1)
 
             @pl.when(inner)
@@ -706,11 +716,7 @@
                     def keep(e):
                         cp_ref[rowsl(s, 2 * own), :] = e
 
-                    def mask(scores):
-                        same = spread(cols[r], cwin) == keys_ref[r, pl.ds(0, 1), :]
-                        return jnp.where(same, scores, MASKED)
-
-                    o2, inv = attend(cq_ref[rs, lanes(s)], kv_ref[cwindow, lanes(2 * s)], kv_ref[cwindow, lanes(2 * s + 1)], mask, keep)
+                    o2, inv = attend(cq_ref[rs, lanes(s)], kv_ref[cwindow, lanes(2 * s)], kv_ref[cwindow, lanes(2 * s + 1)], lambda scores: scores + bias_ref[:, pl.ds(0, cwin)], keep)
                     oc_ref[rs, lanes(s)] = o2.astype(BF16)
                     cinv_ref[:, lanes(s)] = inv.astype(BF16)
                 return 0
@@ -1065,7 +1071,8 @@
     def _():
         c0_x.wait_send()
         for r in range(rows):
-            mem_x(r).wait_send()
+            for h in range(2):
+                mem_x(r, h).wait_send()
         c0_back.wait_recv()
         R("dc")[...] = R("dc0r")[...]
 
@@ -1074,7 +1081,8 @@
         for g in (r_c0, r_c1):
             g.finish()
         for r in range(rows):
-            mem_c(r).wait_send()
+            for h in range(2):
+                mem_c(r, h).wait_send()
             pl.when(inner)(mem_t(r).wait_send)
             dm_x(r).wait_send()
         c0_back.wait_send()
@@ -1123,7 +1131,7 @@
         c0=((width, 8 * hw), BF16), cqw=((width, 4 * hw), BF16), cow=((width, 4 * hw), BF16),
         xh=((2, rows, HALO, width), BF16), nw=((rows * win, width), BF16),
         q=((4, rows, own, hw), BF16), k=((4, rows, win, hw), BF16), v=((4, rows, win, hw), BF16),
-        p=((4, rows, 2 * own, win), BF16), o=((tokens, width), BF16), inv=((tokens, width), BF16), bias=((rows, own, win), F32),
+        p=((4, rows, 2 * own, win), BF16), o=((tokens, width), BF16), inv=((tokens, width), BF16), bias=((own, max(rows * win, cwin)), F32),
         r1=((tokens, width), F32), r2=((tokens, width), F32), n2=((tokens, width), BF16), n3=((tokens, width), BF16),
         u=((4, tokens, fw), BF16), gp=((4, tokens, fw), BF16), secs=((tokens, width), BF16),
         acc=((rows * win, width), F32), g=((tokens, width), F32), gb=((tokens, width), BF16), do=((tokens, width), BF16),

time: 132 us -> 132 us (level)
  no operation moved by 1% of the time
where the time goes in v9:
time: 132 us
  Pallas kernels  131 us (99%)
    pallas_call x1, Pallas kernels, body(): pl.pallas_call(functools.partial(layers, list(ins) + list(outs) + list(vm...  128 us
    pallas_call x1, Pallas kernels, body(): pl.pallas_call(functools.partial(arrange, aligned), name='arrange', out_s...  2.9 us

profile of v9, /device:TPU:0, one launch (start us, length us, event | category | flops | bytes accessed | tf_op | source)
XLA Modules:
  0.0 131.7 jit_solution(2939821916014309201)
XLA Ops:
  0.6 128.1 %layers.1 = (bf16[512,512]{1,0:T(8,128)(2,1)}, bf16[512,512]{1,0:T(8,128)(2,1)}, f32[8,512]{1,0:T(8,128)}, f32[128,384]{1,0:T(8,128)}, f32[128,128]{1,0:T(8,128)...) custom-call(bf16[2,256,512]{2,1,0:T(8,128)(2,1)} %bitcast.20, s32[2,2,1024]{2,1,0:T(2,128)} %refs_1_.1, ...), custom_call_target="tpu_custom_call" | custom-call | tf_op jit(solution)/shard_map/layers/pallas_call | solution.py:1161
  128.8 2.9 %arrange.1 = (bf16[512,512]{1,0:T(8,128)(2,1)}, bf16[512,512]{1,0:T(8,128)(2,1)}, f32[3,1,128]{2,1,0:T(1,128)}, f32[3,128,128]{2,1,0:T(8,128)}, f32[128,128]{1,0...) custom-call(bf16[512,512]{1,0:T(8,128)(2,1)} %get-tuple-element.24.sec, ...), custom_call_target="tpu_custom_call" | custom-call | tf_op jit(solution)/shard_map/arrange/pallas_call | solution.py:1171

commit v10 on v9

--- a/solution.py
+++ b/solution.py
@@ -428,8 +428,8 @@
 
     pl.when(t < 3)(x_right.start)
     pl.when(t > 0)(x_left.start)
+    g_wa.start()
     loads[0].start()
-    g_wa.start()
     g_wo.start()
     for c in loads[1:]:
         c.start()

time: 132 us -> 132 us (level)
  no operation moved by 1% of the time
where the time goes in v10:
time: 132 us
  Pallas kernels  131 us (99%)
    pallas_call x1, Pallas kernels, body(): pl.pallas_call(functools.partial(layers, list(ins) + list(outs) + list(vm...  128 us
    pallas_call x1, Pallas kernels, body(): pl.pallas_call(functools.partial(arrange, aligned), name='arrange', out_s...  2.9 us

profile of v10, /device:TPU:0, one launch (start us, length us, event | category | flops | bytes accessed | tf_op | source)
XLA Modules:
  0.0 131.6 jit_solution(17416949997494062149)
XLA Ops:
  0.6 128.1 %layers.1 = (bf16[512,512]{1,0:T(8,128)(2,1)}, bf16[512,512]{1,0:T(8,128)(2,1)}, f32[8,512]{1,0:T(8,128)}, f32[128,384]{1,0:T(8,128)}, f32[128,128]{1,0:T(8,128)...) custom-call(bf16[2,256,512]{2,1,0:T(8,128)(2,1)} %bitcast.20, s32[2,2,1024]{2,1,0:T(2,128)} %refs_1_.1, ...), custom_call_target="tpu_custom_call" | custom-call | tf_op jit(solution)/shard_map/layers/pallas_call | solution.py:1161
  128.7 2.9 %arrange.1 = (bf16[512,512]{1,0:T(8,128)(2,1)}, bf16[512,512]{1,0:T(8,128)(2,1)}, f32[3,1,128]{2,1,0:T(1,128)}, f32[3,128,128]{2,1,0:T(8,128)}, f32[128,128]{1,0...) custom-call(bf16[512,512]{1,0:T(8,128)(2,1)} %get-tuple-element.24.sec, ...), custom_call_target="tpu_custom_call" | custom-call | tf_op jit(solution)/shard_map/arrange/pallas_call | solution.py:1171
